TPU v7x, 256 devices: a whole 4x4x8 slice. The times are simulated.
256 devices in a mesh: user: 4 (over x), heads: 2 (over y_lo), ctx: 32 (over y_hi, z, core).
Axes of the slice: x: 4, y: 4 (y_hi: 2, y_lo: 2; y = y_hi * 2 + y_lo), z: 8, core: 2. Of those that a mesh axis runs over, the one named last changes fastest.
Arguments:
- keys: bfloat16 [65536, 512], P(('user', 'ctx'), 'heads'), parts along dimension 0, may hold values from -6 to 6
- values: bfloat16 [65536, 512], P(('user', 'ctx'), 'heads'), parts along dimension 0, may hold values from -6 to 6
- queries: bfloat16 [4, 98304, 128], P('heads', ('user', 'ctx')), parts along dimension 1, may hold values from -240 to 240
- positions: int32 [98304], P(('user', 'ctx')), parts along dimension 0, may hold values from 0 to 16383
Outputs:
- attended: bfloat16 [4, 98304, 128], P('heads', ('user', 'ctx')), parts along dimension 1
There are 4 independent parts, one for each index of `user`. A program takes and returns all parts, laid end to end along the dimension named above; each array names one. Nothing has to cross between parts.
All inputs are finite; a program needn't handle non-finite values.
Results may differ from a plain program's by a relative error of at most 0.008.
The roundings to bfloat16 on the way count: a program that leaves them out, or rounds other values in their place, can miss the bound.
Values may be sent and summed in bfloat16 or wider, within the bound.
No kernel may reach another device: no remote copies, remote signals or barrier semaphores. Data moves between devices by JAX's collectives and lax.ppermute only.
A program may use at most 128 MiB of HBM per device.

v0:
```python
import functools
import math

import jax
import jax.numpy as jnp
import ml_dtypes
import numpy as np
from jax import lax
from jax.experimental import pallas as pl
from jax.experimental.pallas import tpu as pltpu
from jax.sharding import Mesh
from jax.sharding import PartitionSpec as P

WINDOW = 16384
KEPT = WINDOW // 2
HEAD = 128
HALF = HEAD // 2
COLUMNS = 16
BASE = 128
ROWS = 136
THETA = 500000.0
BF16 = jnp.bfloat16
F32 = jnp.float32
SWAP = [(0, 1), (1, 0)]


def split(matrix):
    high = matrix.astype(ml_dtypes.bfloat16)
    low = (matrix - high.astype(np.float64)).astype(ml_dtypes.bfloat16)
    return high, low


@functools.cache
def transform_tables(sources):
    per_source = BASE // sources
    order = np.arange(BASE)
    a = per_source * (order % sources) + order // sources
    b = np.arange(BASE)
    k0 = np.arange(ROWS)
    live = (k0 <= BASE).astype(np.float64)[:, None]
    t0 = np.arange(64)
    t1 = np.arange(128)
    k1 = np.arange(-32, 32)
    angle = 2 * np.pi * (np.outer(k0, a) % 256) / 256
    first = np.concatenate([np.cos(angle) * live, -np.sin(angle) * live])
    first = np.concatenate(split(first), axis=1)
    angle = np.pi * np.outer(k0, 2 * b + 1) / (2 * WINDOW)
    twist = np.stack([np.cos(angle), np.sin(angle)]).astype(np.float32)
    angle_b = np.pi * (np.outer(2 * b + 1, k1) % 256) / 128
    angle_t = np.pi * (np.outer(k1, 2 * t0 + 1) % 128) / 64
    real = np.concatenate([np.cos(angle_b) @ np.cos(angle_t), np.sin(angle_b) @ np.cos(angle_t)])
    imag = np.concatenate([np.cos(angle_b) @ np.sin(angle_t), np.sin(angle_b) @ np.sin(angle_t)])
    zero = np.zeros_like(real)
    middle = np.concatenate(
        [
            np.concatenate([real, zero, imag, zero], axis=1),
            np.concatenate([zero, real, zero, imag], axis=1),
        ]
    )
    middle = np.stack(split(middle))
    weight = np.where((k0 == 0) | (k0 == BASE), 1.0 / WINDOW, 2.0 / WINDOW)[:, None] * live
    angle = np.pi * np.outer(k0, 2 * np.tile(t0, 2) + 1) / WINDOW
    untwist = np.stack([weight * np.cos(angle), weight * np.sin(angle)]).astype(np.float32)
    angle = 2 * np.pi * (np.outer(t1, k0) % 256) / 256
    last = np.concatenate([np.cos(angle) * live.T, -np.sin(angle) * live.T], axis=1)
    last = np.stack(split(last))
    return first, twist, middle, untwist, last


def inverse_freq():
    return jnp.exp(jnp.arange(HALF).astype(F32) * (-2.0 * math.log(THETA) / HEAD))


def pack_kernel(core_ref, keys_ref, values_ref, other_ref, out_ref):
    core = core_ref[0]
    tokens = keys_ref.shape[0]
    heads, parts = 2, out_ref.shape[0] // 2
    mine = jnp.where(core == 0, keys_ref[...].astype(F32), values_ref[...].astype(F32))
    for block, place in ((mine, core), (other_ref[...].astype(F32), 1 - core)):
        turned = block.T
        at = pl.multiple_of(place * tokens, 128)
        for head in range(heads):
            for part in range(parts):
                low = head * HEAD + part * 8
                rows = jnp.concatenate(
                    [turned[low : low + 8], turned[low + HALF : low + HALF + 8]], axis=0
                )
                out_ref[head * parts + part, :, pl.ds(at, tokens)] = rows.astype(BF16)


def halves(block):
    high = block.astype(BF16)
    return high, (block - high.astype(F32)).astype(BF16)


def dot(left, right):
    return jnp.dot(left, right, preferred_element_type=F32)


def transform_kernel(
    x_ref, first_ref, twist_ref, middle_ref, untwist_ref, last_ref, cos_ref, sin_ref, out_ref,
    wide_ref, rows_ref,
):
    sources, columns, run = x_ref.shape
    for source in range(sources):
        block = x_ref[source].astype(F32)
        for i in range(run // BASE):
            at = (i * sources + source) * columns
            wide_ref[pl.ds(at, columns), :] = block[:, i * BASE : i * BASE + BASE]
    pieces = [wide_ref[pl.ds(column, BASE, stride=columns), :] for column in range(columns)]
    x = jnp.concatenate(pieces, axis=1).astype(BF16)
    cosine, sine = twist_ref[0], twist_ref[1]
    z_real, z_imag = [], []
    for pair in range(columns // 2):
        xp = x[:, pair * 256 : pair * 256 + 256]
        one = dot(first_ref[...], jnp.concatenate([xp, xp], axis=0))
        parts = []
        for which in range(2):
            real = one[:ROWS, which * BASE : which * BASE + BASE]
            imag = one[ROWS:, which * BASE : which * BASE + BASE]
            parts.append(real * cosine + imag * sine)
            parts.append(imag * cosine - real * sine)
        high, low = halves(jnp.concatenate(parts, axis=1))
        two = (
            dot(high, middle_ref[0]) + dot(low, middle_ref[0]) + dot(high, middle_ref[1])
        )
        real, imag = two[:, :BASE], two[:, BASE:]
        z_real.append(real * untwist_ref[0] - imag * untwist_ref[1])
        z_imag.append(real * untwist_ref[1] + imag * untwist_ref[0])
    z = jnp.concatenate(
        [jnp.concatenate(z_real, axis=1), jnp.concatenate(z_imag, axis=1)], axis=0
    )
    high, low = halves(z)
    y = dot(last_ref[0], high) + dot(last_ref[0], low) + dot(last_ref[1], high)
    rows_ref[...] = y.T
    steps = rows_ref.shape[0] // columns
    for step in range(steps):
        token = rows_ref[pl.ds(step, columns, stride=steps), :].astype(BF16).astype(F32)
        here = pl.ds(step * BASE, BASE)
        cosine, sine = cos_ref[:, here], sin_ref[:, here]
        up, down = token[:8], token[8:]
        turned = jnp.concatenate(
            [up * cosine - down * sine, down * cosine + up * sine], axis=0
        )
        out_ref[:, here] = turned.astype(BF16)


def attend_kernel(q_ref, kv_ref, order_ref, out_ref, *, block, scale):
    parts, _, columns, tokens = kv_ref.shape
    q = q_ref[...]
    rows = q.shape[0]
    count = tokens // block

    def scores(step):
        keys = kv_ref[:, 0, :, pl.ds(step * block, block)].reshape(parts * columns, block)
        return dot(q, keys)

    best = jnp.full((rows, 1), -jnp.inf, F32)
    total = jnp.zeros((rows, 1), F32)
    accum = jnp.zeros((rows, HEAD), F32)
    upcoming = scores(0)
    for step in range(count):
        current = upcoming
        if step + 1 < count:
            upcoming = scores(step + 1)
        fresh = jnp.maximum(best, jnp.max(current, axis=1, keepdims=True))
        shrink = jnp.exp2((best - fresh) * scale)
        expo = jnp.exp2((current - fresh) * scale)
        total = total * shrink + jnp.sum(expo, axis=1, keepdims=True)
        values = kv_ref[:, 1, :, pl.ds(step * block, block)].reshape(parts * columns, block)
        summed = lax.dot_general(
            expo.astype(BF16), values, (((1,), (1,)), ((), ())), preferred_element_type=F32
        )
        accum = accum * shrink + summed
        best = fresh
    result = (accum / total).astype(BF16)
    out_ref[...] = dot(result, order_ref[...]).astype(BF16)


def attend(q, kv, order):
    rows = q.shape[0]
    row_block = 256
    kernel = functools.partial(
        attend_kernel, block=1024, scale=math.log2(math.e) / math.sqrt(HEAD)
    )
    return pl.pallas_call(
        kernel,
        grid=(rows // row_block,),
        in_specs=[
            pl.BlockSpec((row_block, HEAD), lambda i: (i, 0)),
            pl.BlockSpec(kv.shape, lambda i: (0, 0, 0, 0)),
            pl.BlockSpec(order.shape, lambda i: (0, 0)),
        ],
        out_specs=pl.BlockSpec((row_block, HEAD), lambda i: (i, 0)),
        out_shape=jax.ShapeDtypeStruct(q.shape, BF16),
        compiler_params=pltpu.CompilerParams(vmem_limit_bytes=48 * 1024 * 1024),
        name="attend",
    )(q, kv, order)


def on_device(keys, values, queries, positions):
    core = lax.axis_index("core")
    head = lax.axis_index("yhi")
    place = lax.axis_index("z")
    parts = lax.axis_size("z")
    sources = 2 * parts
    tokens = keys.shape[0]

    other = lax.ppermute(jnp.where(core == 0, values, keys), "core", SWAP)
    vmem = pl.BlockSpec(memory_space=pltpu.VMEM)
    packed = pl.pallas_call(
        pack_kernel,
        in_specs=[pl.BlockSpec(memory_space=pltpu.SMEM), vmem, vmem, vmem],
        out_specs=vmem,
        out_shape=jax.ShapeDtypeStruct((sources, COLUMNS, 2 * tokens), BF16),
        name="pack",
    )(core[None].astype(jnp.int32), keys, values, other)
    received = lax.all_to_all(packed, ("yhi", "z"), 0, 0, tiled=True)

    freq = inverse_freq()
    index = jnp.arange(KEPT)
    places = (64 * (index % BASE) + index // BASE).astype(F32)
    angles = lax.dynamic_slice(freq, (8 * place,), (8,))[:, None] * places[None, :]
    cosine = jnp.where(core == 0, jnp.cos(angles), 1.0)
    sine = jnp.where(core == 0, jnp.sin(angles), 0.0)
    first, twist, middle, untwist, last = map(jnp.asarray, transform_tables(sources))
    small = pl.pallas_call(
        transform_kernel,
        in_specs=[vmem] * 8,
        out_specs=vmem,
        out_shape=jax.ShapeDtypeStruct((COLUMNS, KEPT), BF16),
        scratch_shapes=[
            pltpu.VMEM((BASE * COLUMNS, BASE), F32),
            pltpu.VMEM((64 * COLUMNS, BASE), F32),
        ],
        compiler_params=pltpu.CompilerParams(vmem_limit_bytes=40 * 1024 * 1024),
        name="transform",
    )(received, first, twist, middle, untwist, last, cosine, sine)

    angles = positions.astype(F32)[:, None] * freq[None, :]
    cosine, sine = jnp.cos(angles), jnp.sin(angles)
    wide = queries.astype(F32)
    up, down = wide[..., :HALF], wide[..., HALF:]
    turned = jnp.concatenate(
        [up * cosine - down * sine, down * cosine + up * sine], axis=-1
    ).astype(BF16)
    lane = jnp.arange(HEAD)
    order = (
        lane[:, None] == (((lane % 16) // 8) * HALF + (lane // 16) * 8 + lane % 8)[None, :]
    ).astype(BF16)
    turned = jnp.einsum("hqd,de->hqe", turned, order, preferred_element_type=F32).astype(BF16)
    own = jnp.where(head == 0, turned[0], turned[1])
    guest = lax.ppermute(jnp.where(head == 0, turned[1], turned[0]), "yhi", SWAP)

    gathered = lax.all_gather(small, ("z", "core"), axis=0, tiled=True)
    kv = gathered.reshape(parts, 2, COLUMNS, KEPT)
    back = order.T
    returned = lax.ppermute(attend(guest, kv, back), "yhi", SWAP)
    kept = attend(own, kv, back)
    return jnp.where(
        head == 0, jnp.stack([kept, returned]), jnp.stack([returned, kept])
    )


def solution(mesh):
    shape = mesh.devices.shape
    fine = Mesh(
        mesh.devices.reshape(shape[0], shape[1], 2, shape[2] // 4, 2),
        ("user", "heads", "yhi", "z", "core"),
    )
    tokens = ("user", "yhi", "z", "core")
    return jax.shard_map(
        on_device,
        mesh=fine,
        in_specs=(P(tokens, "heads"), P(tokens, "heads"), P("heads", tokens, None), P(tokens)),
        out_specs=P("heads", tokens, None),
        check_vma=False,
    )
```

profile of v0, /device:TPU:1, one launch (start us, length us, event | category | flops | bytes accessed | tf_op | source)
XLA Modules:
  0.0 120.4 jit_solution(14847996127797769291)
XLA Ops:
  6.5 0.0 copy-start.7
  6.5 0.0 copy-start.9
  6.5 1.0 broadcast_select_fusion
  7.6 3.3 %collective-permute-start = (bf16[512,256]{1,0:T(8,128)(2,1)S(1)}, bf16[512,256]{1,0:T(8,128)(2,1)S(1)}, u32[]{:S(2)}, u32[]{:S(2)}) collective-permute-start(bf16[512,256]{1,0:T(8,128)(2,1)S(1)} %broadcast_select_fusion), channel_id=1, source_target_pairs={{0,1},{1,0},{2,3},{3,2},{4,5},{5,4},{6,7},{7,6},{8,9},{9,8},{10,11... | collective-permute-start | bytes 786440 | tf_op jit(solution)/shard_map/ppermute | solution.py:209
  10.9 0.1 dynamic_slice.3
  11.0 1.1 collective-permute-done.other_ref
  12.1 0.0 copy-start.8
  12.1 0.7 copy-done.8
  12.8 2.1 %pack.1 = bf16[16,16,1024]{2,1,0:T(8,128)(2,1)} custom-call(s32[1]{0:T(128)} %bitcast.2.core_ref, bf16[512,256]{1,0:T(8,128)(2,1)} %keys_ref.1, bf16[512,256]{1,0:T(8,128)(2,1)} %values_ref.1, bf16[512,256]{1,0:T(8,128)(2,1)} %copy-done.8), custom_call_target="tpu_custom_call" | custom-call | tf_op jit(solution)/shard_map/pack/pallas_call | solution.py:211
  14.9 9.2 %all-to-all-start = ((bf16[16,16,1024]{2,1,0:T(8,128)(2,1)}), bf16[16,16,1024]{2,1,0:T(8,128)(2,1)S(1)}, u32[]{:S(2)}, u32[]{:S(2)}) async-start(bf16[16,16,1024]{2,1,0:T(8,128)(2,1)} %pack.1), calls=%async_computation | async-start | bytes 1048576 | tf_op jit(solution)/shard_map/all_to_all | solution.py:218
  24.1 0.0 all-gather.2.cloned.1.call-start
  24.1 1.0 fusion.4
  25.1 14.0 %all-to-all-done.x_ref = bf16[16,16,1024]{2,1,0:T(8,128)(2,1)S(1)} async-done(((bf16[16,16,1024]{2,1,0:T(8,128)(2,1)}), bf16[16,16,1024]{2,1,0:T(8,128)(2,1)S(1)}, u32[]{:S(2)}, u32[]{:S(2)}) %all-to-all-start) | async-done | bytes 524320 | tf_op jit(solution)/shard_map/all_to_all | solution.py:218
  39.2 0.0 copy-start.2
  39.2 1.0 copy-done.2
  40.2 0.0 copy-start.3
  40.2 0.9 copy-done.3
  41.1 0.0 copy-start.4
  41.2 0.9 copy-done.4
  42.1 0.0 copy-start.5
  42.1 0.9 copy-done.5
  43.0 0.0 copy-start.6
  43.0 0.9 copy-done.6
  43.9 3.9 %transform.1 = bf16[16,8192]{1,0:T(8,128)(2,1)} custom-call(bf16[16,16,1024]{2,1,0:T(8,128)(2,1)S(1)} %all-to-all-done.x_ref, bf16[272,256]{1,0:T(8,128)(2,1)S(1)} %copy-done.4, f32[2,136,128]{2,1,0:T(8,128)S(1)} %copy-done.5, bf16[2,512,256]{2,1,0:T(8,128)(2,1)S(1)} %copy-done.2, f32[2,136,128]{2,1,0:T(8,128)S(1)} %copy-done.6, ...), custom_call_target="tpu_custom_call" | custom-call | tf_op jit(solution)/shard_map/transform/pallas_call | solution.py:227
  47.7 0.0 all-gather.2.cloned.1.call-update
  47.8 0.0 copy-done.7
  47.8 0.1 convert_element_type.32
  47.8 0.0 copy-done.9
  47.9 1.4 %multiply_cosine_fusion = (f32[768,64]{1,0:T(8,128)S(1)}, f32[768,64]{1,0:T(8,128)S(1)}) fusion(f32[64]{0:T(128)S(1)} %multiply_exponential_fusion, f32[768]{0:T(1024)S(1)} %convert_element_type.33), kind=kLoop, calls=%fused_computation.4 | loop fusion | flops 49152 | bytes 396544 | tf_op jit(solution)/shard_map/cos | solution.py:241
  49.3 0.4 subtract_convert_fusion
  49.7 0.3 convolution_convert_fusion
  50.1 0.3 collective-permute-start.1
  50.3 0.1 fusion.11.order_ref
  50.4 5.8 %collective-permute-done.1.q_ref = bf16[768,128]{1,0:T(8,128)(2,1)S(1)} collective-permute-done((bf16[768,128]{1,0:T(8,128)(2,1)S(1)}, bf16[768,128]{1,0:T(8,128)(2,1)S(1)}, u32[]{:S(2)}, u32[]{:S(2)}) %collective-permute-start.1) | collective-permute-done | bytes 196640 | tf_op jit(solution)/shard_map/ppermute | solution.py:253
  56.2 32.9 %all-gather.2.cloned.1.call-done = bf16[256,8192]{1,0:T(8,128)(2,1)} async-done(((bf16[16,8192]{1,0:T(8,128)(2,1)}), bf16[256,8192]{1,0:T(8,128)(2,1)}) %all-gather.2.cloned.1.call-update) | async-done | bytes 4194320 | tf_op jit(solution)/shard_map/all_gather | solution.py:255
  89.1 0.0 copy-start
  89.1 2.2 %copy-done = bf16[256,8192]{1,0:T(8,128)(2,1)S(1)} copy-done((bf16[256,8192]{1,0:T(8,128)(2,1)S(1)}, bf16[256,8192]{1,0:T(8,128)(2,1)}, u32[]{:S(2)}) %copy-start) | copy-done | bytes 4194328
  91.3 0.0 copy-start.1
  91.3 9.2 %attend.3 = bf16[768,128]{1,0:T(8,128)(2,1)S(1)} custom-call(bf16[768,128]{1,0:T(8,128)(2,1)S(1)} %collective-permute-done.1.q_ref, bf16[8,2,16,8192]{3,2,1,0:T(8,128)(2,1)S(1)} %bitcast.11, bf16[128,128]{1,0:T(8,128)(2,1)S(1)} %fusion.11.order_ref), custom_call_target="tpu_custom_call" | custom-call | tf_op jit(solution)/shard_map/attend/pallas_call | solution.py:186
  100.5 3.0 %collective-permute-start.2 = (bf16[768,128]{1,0:T(8,128)(2,1)S(1)}, bf16[768,128]{1,0:T(8,128)(2,1)S(1)}, u32[]{:S(2)}, u32[]{:S(2)}) collective-permute-start(bf16[768,128]{1,0:T(8,128)(2,1)S(1)} %attend.3), channel_id=1, source_target_pairs={{0,16},{16,0},{1,17},{17,1},{2,18},{18,2},{3,19},{19,3},{4,20},{20... | collective-permute-start | bytes 589832 | tf_op jit(solution)/shard_map/ppermute | solution.py:258
  103.5 0.0 copy-done.1
  103.5 9.2 %attend.2 = bf16[768,128]{1,0:T(8,128)(2,1)S(1)} custom-call(bf16[768,128]{1,0:T(8,128)(2,1)S(1)} %get-tuple-element.7.q_ref, bf16[8,2,16,8192]{3,2,1,0:T(8,128)(2,1)S(1)} %bitcast.12, bf16[128,128]{1,0:T(8,128)(2,1)S(1)} %fusion.11.order_ref), custom_call_target="tpu_custom_call" | custom-call | tf_op jit(solution)/shard_map/attend/pallas_call | solution.py:186
  112.8 0.0 collective-permute-done.2
  112.8 0.8 maximum_select_fusion
  (5 shorter events, 0.1 us)
Async XLA Ops:
  6.5 41.2 %copy-start.7 = (bf16[2,768,128]{2,1,0:T(8,128)(2,1)S(1)}, bf16[2,768,128]{2,1,0:T(8,128)(2,1)}, u32[]{:S(2)}) copy-start(bf16[2,768,128]{2,1,0:T(8,128)(2,1)} %param.11) | copy-start | bytes 1179652
  6.5 41.3 %copy-start.9 = (s32[768]{0:T(1024)S(1)}, s32[768]{0:T(1024)}, u32[]{:S(2)}) copy-start(s32[768]{0:T(1024)} %param.12) | copy-start | bytes 9220
  7.6 4.5 %collective-permute-start = (bf16[512,256]{1,0:T(8,128)(2,1)S(1)}, bf16[512,256]{1,0:T(8,128)(2,1)S(1)}, u32[]{:S(2)}, u32[]{:S(2)}) collective-permute-start(bf16[512,256]{1,0:T(8,128)(2,1)S(1)} %broadcast_select_fusion), channel_id=1, source_target_pairs={{0,1},{1,0},{2,3},{3,2},{4,5},{5,4},{6,7},{7,6},{8,9},{9,8},{10,11... | collective-permute-start | bytes 786440 | tf_op jit(solution)/shard_map/ppermute | solution.py:209
  12.1 0.7 copy-start.8
  14.9 24.3 %all-to-all-start = ((bf16[16,16,1024]{2,1,0:T(8,128)(2,1)}), bf16[16,16,1024]{2,1,0:T(8,128)(2,1)S(1)}, u32[]{:S(2)}, u32[]{:S(2)}) async-start(bf16[16,16,1024]{2,1,0:T(8,128)(2,1)} %pack.1), calls=%async_computation | async-start | bytes 1048576 | tf_op jit(solution)/shard_map/all_to_all | solution.py:218
  24.1 65.1 %all-gather.2.cloned.1.call-start = ((), (), s32[]{:S(2)}) async-start(), calls=%async_computation.1 | async-start | bytes 4456448 | tf_op jit(solution)/shard_map/all_gather | solution.py:255
  39.2 1.0 copy-start.2
  40.2 0.9 copy-start.3
  41.1 0.9 copy-start.4
  42.1 0.9 copy-start.5
  43.0 0.9 copy-start.6
  50.1 6.1 %collective-permute-start.1 = (bf16[768,128]{1,0:T(8,128)(2,1)S(1)}, bf16[768,128]{1,0:T(8,128)(2,1)S(1)}, u32[]{:S(2)}, u32[]{:S(2)}) collective-permute-start(bf16[768,128]{1,0:T(8,128)(2,1)S(1)} %get-tuple-element.8), channel_id=1, source_target_pairs={{0,16},{16,0},{1,17},{17,1},{2,18},{18,2},{3,19},{19,3},{4,20},{20... | collective-permute-start | bytes 589832 | tf_op jit(solution)/shard_map/ppermute | solution.py:253
  89.1 2.2 %copy-start = (bf16[256,8192]{1,0:T(8,128)(2,1)S(1)}, bf16[256,8192]{1,0:T(8,128)(2,1)}, u32[]{:S(2)}) copy-start(bf16[256,8192]{1,0:T(8,128)(2,1)} %all-gather.2.cloned.1.call-done) | copy-start | bytes 12582916
  91.3 12.2 %copy-start.1 = (bf16[256,8192]{1,0:T(8,128)(2,1)S(1)}, bf16[256,8192]{1,0:T(8,128)(2,1)}, u32[]{:S(2)}) copy-start(bf16[256,8192]{1,0:T(8,128)(2,1)} %all-gather.2.cloned.1.call-done) | copy-start | bytes 12582916
  100.5 12.2 %collective-permute-start.2 = (bf16[768,128]{1,0:T(8,128)(2,1)S(1)}, bf16[768,128]{1,0:T(8,128)(2,1)S(1)}, u32[]{:S(2)}, u32[]{:S(2)}) collective-permute-start(bf16[768,128]{1,0:T(8,128)(2,1)S(1)} %attend.3), channel_id=1, source_target_pairs={{0,16},{16,0},{1,17},{17,1},{2,18},{18,2},{3,19},{19,3},{4,20},{20... | collective-permute-start | bytes 589832 | tf_op jit(solution)/shard_map/ppermute | solution.py:258
Sparse Core Ops, SparseCore 0:
  47.9 41.2 all-gather.1
where the time goes:
time: 121 us; the launch traced here: 120 us
  waiting for transfers between devices  53.8 us (44%)
  Pallas kernels  24.4 us (20%)
  starting transfers between devices  15.8 us (13%)
  between operations  13.5 us (11%)
  local copies, waits for them, and re-layouts  7.66 us (6%)
  other arithmetic  4.84 us (4%)
    all_gather x1, waiting for transfers between devices, on_device(): gathered = lax.all_gather(small, ('z', 'core'), axis=0, tiled=True)  32.9 us
    pallas_call x2, Pallas kernels, attend(): pl.pallas_call(kernel, grid=(rows // row_block,), in_specs=[pl.BlockSpec(...  18.4 us
    all_to_all x1, waiting for transfers between devices, on_device(): received = lax.all_to_all(packed, ('yhi', 'z'), 0, 0, tiled=True)  14 us
    all_to_all x1, starting transfers between devices, on_device(): received = lax.all_to_all(packed, ('yhi', 'z'), 0, 0, tiled=True)  9.18 us
    unnamed x20, local copies, waits for them, and re-layouts  7.59 us
    ppermute x1, waiting for transfers between devices, on_device(): lax.ppermute(jnp.where(head == 0, turned[1], turned[0]), 'yhi', SWAP)  5.76 us
    pallas_call x1, Pallas kernels, on_device(): pl.pallas_call(transform_kernel, in_specs=[vmem] * 8, out_specs=vmem, out...  3.85 us
    ppermute x1, starting transfers between devices, on_device(): other = lax.ppermute(jnp.where(core == 0, values, keys), 'core', SWAP)  3.33 us
  transfers between devices with their start and end apart: 5, of which 4 were waited for; matrix products, arithmetic and copies ran while one was open for 3% of the time, Pallas kernels for 8%

commit v1 on v0

--- a/solution.py
+++ b/solution.py
@@ -71,13 +71,25 @@
     return jnp.exp(jnp.arange(HALF).astype(F32) * (-2.0 * math.log(THETA) / HEAD))
 
 
-def pack_kernel(core_ref, keys_ref, values_ref, other_ref, out_ref):
+def choose_kernel(core_ref, keys_ref, values_ref, mine_ref, send_ref, sems):
+    def move(mine, send):
+        first = pltpu.make_async_copy(send, send_ref, sems.at[0])
+        second = pltpu.make_async_copy(mine, mine_ref, sems.at[1])
+        first.start()
+        second.start()
+        first.wait()
+        second.wait()
+
+    pl.when(core_ref[0] == 0)(lambda: move(keys_ref, values_ref))
+    pl.when(core_ref[0] != 0)(lambda: move(values_ref, keys_ref))
+
+
+def pack_kernel(core_ref, mine_ref, other_ref, out_ref):
     core = core_ref[0]
-    tokens = keys_ref.shape[0]
+    tokens = mine_ref.shape[0]
     heads, parts = 2, out_ref.shape[0] // 2
-    mine = jnp.where(core == 0, keys_ref[...].astype(F32), values_ref[...].astype(F32))
-    for block, place in ((mine, core), (other_ref[...].astype(F32), 1 - core)):
-        turned = block.T
+    for block_ref, place in ((mine_ref, core), (other_ref, 1 - core)):
+        turned = block_ref[...].astype(F32).T
         at = pl.multiple_of(place * tokens, 128)
         for head in range(heads):
             for part in range(parts):
@@ -98,9 +110,23 @@
 
 
 def transform_kernel(
-    x_ref, first_ref, twist_ref, middle_ref, untwist_ref, last_ref, cos_ref, sin_ref, out_ref,
-    wide_ref, rows_ref,
+    x_ref, cos_ref, sin_ref, first_hbm, twist_hbm, middle_hbm, untwist_hbm, last_hbm, *refs
 ):
+    *out_refs, first_ref, twist_ref, middle_ref, untwist_ref, last_ref, wide_ref, rows_ref, sems = refs
+    copies = [
+        pltpu.make_async_copy(source, target, sems.at[i])
+        for i, (source, target) in enumerate(
+            (
+                (first_hbm, first_ref),
+                (twist_hbm, twist_ref),
+                (middle_hbm, middle_ref),
+                (untwist_hbm, untwist_ref),
+                (last_hbm, last_ref),
+            )
+        )
+    ]
+    for copy in copies:
+        copy.start()
     sources, columns, run = x_ref.shape
     for source in range(sources):
         block = x_ref[source].astype(F32)
@@ -109,6 +135,8 @@
             wide_ref[pl.ds(at, columns), :] = block[:, i * BASE : i * BASE + BASE]
     pieces = [wide_ref[pl.ds(column, BASE, stride=columns), :] for column in range(columns)]
     x = jnp.concatenate(pieces, axis=1).astype(BF16)
+    for copy in copies:
+        copy.wait()
     cosine, sine = twist_ref[0], twist_ref[1]
     z_real, z_imag = [], []
     for pair in range(columns // 2):
@@ -142,22 +170,21 @@
         turned = jnp.concatenate(
             [up * cosine - down * sine, down * cosine + up * sine], axis=0
         )
-        out_ref[:, here] = turned.astype(BF16)
-
-
-def attend_kernel(q_ref, kv_ref, order_ref, out_ref, *, block, scale):
-    parts, _, columns, tokens = kv_ref.shape
-    q = q_ref[...]
+        chunk, place = divmod(step * BASE, out_refs[0].shape[1])
+        out_refs[chunk][:, pl.ds(place, BASE)] = turned.astype(BF16)
+
+
+def attend_rows(q, kv_ref, core, order, *, block, scale):
+    _, width, tokens = kv_ref.shape
     rows = q.shape[0]
     count = tokens // block
 
     def scores(step):
-        keys = kv_ref[:, 0, :, pl.ds(step * block, block)].reshape(parts * columns, block)
-        return dot(q, keys)
+        return dot(q, kv_ref[core, :, pl.ds(step * block, block)])
 
     best = jnp.full((rows, 1), -jnp.inf, F32)
-    total = jnp.zeros((rows, 1), F32)
-    accum = jnp.zeros((rows, HEAD), F32)
+    accum = jnp.zeros((rows, 2 * HEAD), F32)
+    ones = jnp.ones((HEAD, block), BF16)
     upcoming = scores(0)
     for step in range(count):
         current = upcoming
@@ -165,37 +192,122 @@
             upcoming = scores(step + 1)
         fresh = jnp.maximum(best, jnp.max(current, axis=1, keepdims=True))
         shrink = jnp.exp2((best - fresh) * scale)
-        expo = jnp.exp2((current - fresh) * scale)
-        total = total * shrink + jnp.sum(expo, axis=1, keepdims=True)
-        values = kv_ref[:, 1, :, pl.ds(step * block, block)].reshape(parts * columns, block)
+        expo = jnp.exp2((current - fresh) * scale).astype(BF16)
+        values = kv_ref[1 - core, :, pl.ds(step * block, block)]
         summed = lax.dot_general(
-            expo.astype(BF16), values, (((1,), (1,)), ((), ())), preferred_element_type=F32
+            expo,
+            jnp.concatenate([values, ones], axis=0),
+            (((1,), (1,)), ((), ())),
+            preferred_element_type=F32,
         )
         accum = accum * shrink + summed
         best = fresh
-    result = (accum / total).astype(BF16)
-    out_ref[...] = dot(result, order_ref[...]).astype(BF16)
-
-
-def attend(q, kv, order):
+    result = (accum[:, :HEAD] / accum[:, HEAD:]).astype(BF16)
+    return dot(result, order).astype(BF16)
+
+
+SCALE = math.log2(math.e) / math.sqrt(HEAD)
+ROW_BLOCK = 384
+TOKEN_BLOCK = 2048
+CHUNKS = 1
+
+
+def gather_attend_kernel(core_ref, q_ref, order_ref, *refs):
+    *blocks, out_ref, kv_ref, sems = refs
+    half = len(blocks) // 2
+    columns, run = blocks[0].shape
+
+    @pl.when(pl.program_id(0) == 0)
+    def _():
+        copies = []
+        for i, block in enumerate(blocks):
+            which, at = divmod(i, half)
+            row, chunk = divmod(at, CHUNKS)
+            target = kv_ref.at[which, pl.ds(row * columns, columns), pl.ds(chunk * run, run)]
+            copies.append(pltpu.make_async_copy(block, target, sems.at[i]))
+        for copy in copies:
+            copy.start()
+        for copy in copies:
+            copy.wait()
+
+    out_ref[...] = attend_rows(
+        q_ref[...], kv_ref, core_ref[0], order_ref[...], block=TOKEN_BLOCK, scale=SCALE
+    )
+
+
+def attend_kernel(core_ref, q_ref, order_ref, kv_ref, out_ref):
+    out_ref[...] = attend_rows(
+        q_ref[...], kv_ref, core_ref[0], order_ref[...], block=TOKEN_BLOCK, scale=SCALE
+    )
+
+
+def gather_attend(core, q, order, blocks):
     rows = q.shape[0]
-    row_block = 256
-    kernel = functools.partial(
-        attend_kernel, block=1024, scale=math.log2(math.e) / math.sqrt(HEAD)
-    )
+    columns, run = blocks[0].shape
+    kv_shape = (2, len(blocks) // (2 * CHUNKS) * columns, CHUNKS * run)
     return pl.pallas_call(
-        kernel,
-        grid=(rows // row_block,),
+        gather_attend_kernel,
+        grid=(rows // ROW_BLOCK,),
         in_specs=[
-            pl.BlockSpec((row_block, HEAD), lambda i: (i, 0)),
-            pl.BlockSpec(kv.shape, lambda i: (0, 0, 0, 0)),
+            pl.BlockSpec(memory_space=pltpu.SMEM),
+            pl.BlockSpec((ROW_BLOCK, HEAD), lambda i: (i, 0)),
             pl.BlockSpec(order.shape, lambda i: (0, 0)),
+        ]
+        + [pl.BlockSpec(memory_space=pl.ANY)] * len(blocks),
+        out_specs=[
+            pl.BlockSpec((ROW_BLOCK, HEAD), lambda i: (i, 0)),
+            pl.BlockSpec(memory_space=pltpu.VMEM),
         ],
-        out_specs=pl.BlockSpec((row_block, HEAD), lambda i: (i, 0)),
+        out_shape=[
+            jax.ShapeDtypeStruct(q.shape, BF16),
+            jax.ShapeDtypeStruct(kv_shape, BF16),
+        ],
+        scratch_shapes=[pltpu.SemaphoreType.DMA((len(blocks),))],
+        compiler_params=pltpu.CompilerParams(vmem_limit_bytes=32 * 1024 * 1024),
+        name="gather_attend",
+    )(core, q, order, *blocks)
+
+
+def attend(core, q, order, kv):
+    return pl.pallas_call(
+        attend_kernel,
+        grid=(q.shape[0] // ROW_BLOCK,),
+        in_specs=[
+            pl.BlockSpec(memory_space=pltpu.SMEM),
+            pl.BlockSpec((ROW_BLOCK, HEAD), lambda i: (i, 0)),
+            pl.BlockSpec(order.shape, lambda i: (0, 0)),
+            pl.BlockSpec(memory_space=pltpu.VMEM),
+        ],
+        out_specs=pl.BlockSpec((ROW_BLOCK, HEAD), lambda i: (i, 0)),
         out_shape=jax.ShapeDtypeStruct(q.shape, BF16),
-        compiler_params=pltpu.CompilerParams(vmem_limit_bytes=48 * 1024 * 1024),
+        compiler_params=pltpu.CompilerParams(vmem_limit_bytes=32 * 1024 * 1024),
         name="attend",
-    )(q, kv, order)
+    )(core, q, order, kv)
+
+
+def ring_gather(small, parts):
+    onward = [(2 * i, 2 * ((i + 1) % parts)) for i in range(parts)]
+    onward += [(2 * i + 1, 2 * ((i - 1) % parts) + 1) for i in range(parts)]
+
+    def along(block):
+        return lax.ppermute(block, ("z", "core"), onward)
+
+    def across(block):
+        return lax.ppermute(block, "core", SWAP)
+
+    a = [along(block) for block in small]
+    other = [across(block) for block in small]
+    b = [along(block) for block in other]
+    mine, theirs = list(small), list(other)
+    for step in range(1, parts // 2):
+        a_next = [along(block) for block in a]
+        a_swapped = [across(block) for block in a]
+        b_next = [along(block) for block in b] if step + 1 < parts // 2 else None
+        b_swapped = [across(block) for block in b]
+        mine += a + b_swapped
+        theirs += b + a_swapped
+        a, b = a_next, b_next
+    return mine + a, theirs + [across(block) for block in a]
 
 
 def on_device(keys, values, queries, positions):
@@ -205,38 +317,34 @@
     parts = lax.axis_size("z")
     sources = 2 * parts
     tokens = keys.shape[0]
-
-    other = lax.ppermute(jnp.where(core == 0, values, keys), "core", SWAP)
+    core_here = core[None].astype(jnp.int32)
+
     vmem = pl.BlockSpec(memory_space=pltpu.VMEM)
+    smem = pl.BlockSpec(memory_space=pltpu.SMEM)
+    hbm = pl.BlockSpec(memory_space=pltpu.HBM)
+    chosen = jax.ShapeDtypeStruct(keys.shape, BF16)
+    kept_tokens, send = pl.pallas_call(
+        choose_kernel,
+        in_specs=[smem, hbm, hbm],
+        out_specs=[vmem, vmem],
+        out_shape=[chosen, chosen],
+        scratch_shapes=[pltpu.SemaphoreType.DMA((2,))],
+        compiler_params=pltpu.CompilerParams(vmem_limit_bytes=16 * 1024 * 1024),
+        name="choose",
+    )(core_here, keys, values)
+    other = lax.ppermute(send, "core", SWAP)
     packed = pl.pallas_call(
         pack_kernel,
-        in_specs=[pl.BlockSpec(memory_space=pltpu.SMEM), vmem, vmem, vmem],
+        in_specs=[smem, vmem, vmem],
         out_specs=vmem,
         out_shape=jax.ShapeDtypeStruct((sources, COLUMNS, 2 * tokens), BF16),
+        compiler_params=pltpu.CompilerParams(vmem_limit_bytes=16 * 1024 * 1024),
         name="pack",
-    )(core[None].astype(jnp.int32), keys, values, other)
+    )(core_here, kept_tokens, other)
+    packed, queries, positions = lax.optimization_barrier((packed, queries, positions))
     received = lax.all_to_all(packed, ("yhi", "z"), 0, 0, tiled=True)
 
     freq = inverse_freq()
-    index = jnp.arange(KEPT)
-    places = (64 * (index % BASE) + index // BASE).astype(F32)
-    angles = lax.dynamic_slice(freq, (8 * place,), (8,))[:, None] * places[None, :]
-    cosine = jnp.where(core == 0, jnp.cos(angles), 1.0)
-    sine = jnp.where(core == 0, jnp.sin(angles), 0.0)
-    first, twist, middle, untwist, last = map(jnp.asarray, transform_tables(sources))
-    small = pl.pallas_call(
-        transform_kernel,
-        in_specs=[vmem] * 8,
-        out_specs=vmem,
-        out_shape=jax.ShapeDtypeStruct((COLUMNS, KEPT), BF16),
-        scratch_shapes=[
-            pltpu.VMEM((BASE * COLUMNS, BASE), F32),
-            pltpu.VMEM((64 * COLUMNS, BASE), F32),
-        ],
-        compiler_params=pltpu.CompilerParams(vmem_limit_bytes=40 * 1024 * 1024),
-        name="transform",
-    )(received, first, twist, middle, untwist, last, cosine, sine)
-
     angles = positions.astype(F32)[:, None] * freq[None, :]
     cosine, sine = jnp.cos(angles), jnp.sin(angles)
     wide = queries.astype(F32)
@@ -245,18 +353,44 @@
         [up * cosine - down * sine, down * cosine + up * sine], axis=-1
     ).astype(BF16)
     lane = jnp.arange(HEAD)
-    order = (
-        lane[:, None] == (((lane % 16) // 8) * HALF + (lane // 16) * 8 + lane % 8)[None, :]
-    ).astype(BF16)
+    at = lane // COLUMNS
+    away = jnp.where(at % 2 == 1, -1, 1) * ((at + 1) // 2) * jnp.where(core == 0, 1, -1)
+    owner = (place + away) % parts
+    column = ((lane % COLUMNS) // 8) * HALF + owner * 8 + lane % 8
+    order = (lane[:, None] == column[None, :]).astype(BF16)
     turned = jnp.einsum("hqd,de->hqe", turned, order, preferred_element_type=F32).astype(BF16)
     own = jnp.where(head == 0, turned[0], turned[1])
     guest = lax.ppermute(jnp.where(head == 0, turned[1], turned[0]), "yhi", SWAP)
 
-    gathered = lax.all_gather(small, ("z", "core"), axis=0, tiled=True)
-    kv = gathered.reshape(parts, 2, COLUMNS, KEPT)
+    index = jnp.arange(KEPT)
+    places = (64 * (index % BASE) + index // BASE).astype(F32)
+    angles = lax.dynamic_slice(freq, (8 * place,), (8,))[:, None] * places[None, :]
+    cosine = jnp.where(core == 0, jnp.cos(angles), 1.0)
+    sine = jnp.where(core == 0, jnp.sin(angles), 0.0)
+    received, own, guest, cosine, sine = lax.optimization_barrier(
+        (received, own, guest, cosine, sine)
+    )
+    tables = transform_tables(sources)
+    small = pl.pallas_call(
+        transform_kernel,
+        in_specs=[vmem] * 3 + [hbm] * 5,
+        out_specs=[vmem] * CHUNKS,
+        out_shape=[jax.ShapeDtypeStruct((COLUMNS, KEPT // CHUNKS), BF16)] * CHUNKS,
+        scratch_shapes=[pltpu.VMEM(t.shape, t.dtype) for t in tables]
+        + [
+            pltpu.VMEM((BASE * COLUMNS, BASE), F32),
+            pltpu.VMEM((64 * COLUMNS, BASE), F32),
+            pltpu.SemaphoreType.DMA((len(tables),)),
+        ],
+        compiler_params=pltpu.CompilerParams(vmem_limit_bytes=32 * 1024 * 1024),
+        name="transform",
+    )(received, cosine, sine, *map(jnp.asarray, tables))
+
+    mine, theirs = ring_gather(small, parts)
     back = order.T
-    returned = lax.ppermute(attend(guest, kv, back), "yhi", SWAP)
-    kept = attend(own, kv, back)
+    first, kv = gather_attend(core_here, guest, back, mine + theirs)
+    returned = lax.ppermute(first, "yhi", SWAP)
+    kept = attend(core_here, own, back, kv)
     return jnp.where(
         head == 0, jnp.stack([kept, returned]), jnp.stack([returned, kept])
     )

time: 121 us -> 90.5 us (0.75)
  waiting for transfers between devices: 53.8 us -> 12.8 us
  starting transfers between devices: 15.8 us -> 47.2 us
  between operations: 13.5 us -> 0.19 us
  local copies, waits for them, and re-layouts: 7.66 us -> 2 us
  Pallas kernels: 24.4 us -> 22.1 us
    all_gather x1 -> x0, waiting for transfers between devices: 32.9 us -> none  [on_device(): gathered = lax.all_gather(small, ('z', 'core'), axis=0, tiled=True)]
    ppermute x2 -> x17, starting transfers between devices: 6.33 us -> 34.9 us  [the longest x7 18.1 us: along(): return lax.ppermute(block, ('z', 'core'), onward)]
    all_to_all x1, waiting for transfers between devices: 14 us -> 1.88 us  [on_device(): received = lax.all_to_all(packed, ('yhi', 'z'), 0, 0, tiled=True)]
    unnamed x20 -> x14, local copies, waits for them, and re-layouts: 7.59 us -> 1.92 us
    ppermute x2 -> x17, waiting for transfers between devices: 1.06 us -> 4.93 us  [the longest x7 2.83 us: along(): return lax.ppermute(block, ('z', 'core'), onward)]
    ppermute x1, starting transfers between devices: 0.27 us -> 2.96 us  [on_device(): lax.ppermute(jnp.where(head == 0, turned[1], turned[0]), 'yhi', SWAP)]
    pallas_call x4 -> x5, Pallas kernels: 24.4 us -> 22.1 us  [the longest x1 8.57 us: gather_attend(): pl.pallas_call(gather_attend_kernel, grid=(rows // ROW_BLOCK,), in_specs=...]
  transfers between devices with their start and end apart: 5 -> 19, of which waited for: 4 -> 7; matrix products, arithmetic and copies ran while one was open for 3% -> 5% of each run, Pallas kernels for 8% -> 9%
where the time goes in v1:
time: 90.5 us; the launch traced here: 90.2 us
  starting transfers between devices  47.2 us (52%)
  Pallas kernels  22.1 us (24%)
  waiting for transfers between devices  12.8 us (14%)
  other arithmetic  5.51 us (6%)
  local copies, waits for them, and re-layouts  2 us (2%)
    ppermute x7, starting transfers between devices, along(): return lax.ppermute(block, ('z', 'core'), onward)  18.1 us
    ppermute x8, starting transfers between devices, across(): return lax.ppermute(block, 'core', SWAP)  12.4 us
    all_to_all x1, starting transfers between devices, on_device(): received = lax.all_to_all(packed, ('yhi', 'z'), 0, 0, tiled=True)  9.33 us
    pallas_call x1, Pallas kernels, gather_attend(): pl.pallas_call(gather_attend_kernel, grid=(rows // ROW_BLOCK,), in_specs=...  8.57 us
    pallas_call x1, Pallas kernels, attend(): pl.pallas_call(attend_kernel, grid=(q.shape[0] // ROW_BLOCK,), in_specs=[...  8.12 us
    ppermute x1, waiting for transfers between devices, on_device(): lax.ppermute(jnp.where(head == 0, turned[1], turned[0]), 'yhi', SWAP)  5.98 us
    pallas_call x1, Pallas kernels, on_device(): pl.pallas_call(transform_kernel, in_specs=[vmem] * 3 + [hbm] * 5, out_spe...  4.36 us
    ppermute x1, starting transfers between devices, on_device(): other = lax.ppermute(send, 'core', SWAP)  3.33 us
  transfers between devices with their start and end apart: 19, of which 7 were waited for; matrix products, arithmetic and copies ran while one was open for 5% of the time, Pallas kernels for 9%

profile of v1, /device:TPU:1, one launch (start us, length us, event | category | flops | bytes accessed | tf_op | source)
XLA Modules:
  0.0 90.2 jit_solution(4790048876416558108)
XLA Ops:
  0.0 0.9 %copy-done.1 = bf16[512,256]{1,0:T(8,128)(2,1)S(1)} copy-done((bf16[512,256]{1,0:T(8,128)(2,1)S(1)}, bf16[512,256]{1,0:T(8,128)(2,1)}, u32[]{:S(2)}) %copy-start.1) | copy-done | bytes 262168
  1.0 0.9 %copy-done.2 = bf16[512,256]{1,0:T(8,128)(2,1)S(1)} copy-done((bf16[512,256]{1,0:T(8,128)(2,1)S(1)}, bf16[512,256]{1,0:T(8,128)(2,1)}, u32[]{:S(2)}) %copy-start.2) | copy-done | bytes 262168
  1.9 0.1 choose.1
  2.0 3.3 %collective-permute-start = (bf16[512,256]{1,0:T(8,128)(2,1)S(1)}, bf16[512,256]{1,0:T(8,128)(2,1)S(1)}, u32[]{:S(2)}, u32[]{:S(2)}) collective-permute-start(bf16[512,256]{1,0:T(8,128)(2,1)S(1)} %get-tuple-element.18), channel_id=1, source_target_pairs={{0,1},{1,0},{2,3},{3,2},{4,5},{5,4},{6,7},{7,6},{8,9},{9,8},{10,11... | collective-permute-start | bytes 786440 | tf_op jit(solution)/shard_map/ppermute | solution.py:335
  5.3 0.1 dynamic_slice.3
  5.4 1.0 %collective-permute-done.other_ref = bf16[512,256]{1,0:T(8,128)(2,1)S(1)} collective-permute-done((bf16[512,256]{1,0:T(8,128)(2,1)S(1)}, bf16[512,256]{1,0:T(8,128)(2,1)S(1)}, u32[]{:S(2)}, u32[]{:S(2)}) %collective-permute-start) | collective-permute-done | bytes 262176 | tf_op jit(solution)/shard_map/ppermute | solution.py:335
  6.5 1.0 %pack.1 = bf16[16,16,1024]{2,1,0:T(8,128)(2,1)} custom-call(s32[1]{0:T(128)} %bitcast.core_ref, bf16[512,256]{1,0:T(8,128)(2,1)S(1)} %get-tuple-element.17.mine_ref, bf16[512,256]{1,0:T(8,128)(2,1)S(1)} %collective-permute-done.other_ref), custom_call_target="tpu_custom_call" | custom-call | tf_op jit(solution)/shard_map/pack/pallas_call | solution.py:336
  7.5 0.7 convert_element_type.31
  8.2 0.0 copy-start.6
  8.2 9.3 %all-to-all-start = ((bf16[16,16,1024]{2,1,0:T(8,128)(2,1)}), bf16[16,16,1024]{2,1,0:T(8,128)(2,1)S(1)}, u32[]{:S(2)}, u32[]{:S(2)}) async-start(bf16[16,16,1024]{2,1,0:T(8,128)(2,1)} %pack.1), calls=%async_computation | async-start | bytes 1048576 | tf_op jit(solution)/shard_map/all_to_all | solution.py:345
  17.5 1.4 %multiply_cosine_fusion = (f32[768,64]{1,0:T(8,128)S(1)}, f32[768,64]{1,0:T(8,128)S(1)}) fusion(f32[64]{0:T(128)S(1)} %multiply_exponential_fusion, f32[768]{0:T(1024)S(1)} %convert_element_type.31), kind=kLoop, calls=%fused_computation.4 | loop fusion | flops 49152 | bytes 396544 | tf_op jit(solution)/shard_map/cos | solution.py:349
  19.0 1.1 %convert_element_type.30 = f32[2,768,128]{2,1,0:T(8,128)S(1)} convert(bf16[2,768,128]{2,1,0:T(8,128)(2,1)} %param.11) | non-fusion elementwise | flops 196608 | bytes 1179648 | tf_op jit(solution)/shard_map/convert_element_type | solution.py:350
  20.0 0.4 subtract_convert_fusion
  20.4 0.3 convolution_convert_fusion
  20.8 3.0 %collective-permute-start.1 = (bf16[768,128]{1,0:T(8,128)(2,1)S(1)}, bf16[768,128]{1,0:T(8,128)(2,1)S(1)}, u32[]{:S(2)}, u32[]{:S(2)}) collective-permute-start(bf16[768,128]{1,0:T(8,128)(2,1)S(1)} %get-tuple-element.31), channel_id=1, source_target_pairs={{0,16},{16,0},{1,17},{17,1},{2,18},{18,2},{3,19},{19,3},{4,20},{20... | collective-permute-start | bytes 589832 | tf_op jit(solution)/shard_map/ppermute | solution.py:363
  23.8 1.0 %fusion.4 = (f32[8,8192]{1,0:T(8,128)S(1)}, f32[8,8192]{1,0:T(8,128)S(1)}) fusion(f32[8192]{0:T(1024)S(1)} %fusion.15, f32[8]{0:T(128)S(1)} %dynamic_slice.3, pred[]{:T(512)S(6)} %eq.47), kind=kLoop, calls=%fused_computation.12 | loop fusion | flops 196608 | bytes 557089 | tf_op jit(solution)/shard_map/jit(_where)/select_n | solution.py:369
  24.8 6.0 %collective-permute-done.1.q_ref = bf16[768,128]{1,0:T(8,128)(2,1)S(1)} collective-permute-done((bf16[768,128]{1,0:T(8,128)(2,1)S(1)}, bf16[768,128]{1,0:T(8,128)(2,1)S(1)}, u32[]{:S(2)}, u32[]{:S(2)}) %collective-permute-start.1) | collective-permute-done | bytes 196640 | tf_op jit(solution)/shard_map/ppermute | solution.py:363
  30.7 1.9 %all-to-all-done.x_ref = bf16[16,16,1024]{2,1,0:T(8,128)(2,1)S(1)} async-done(((bf16[16,16,1024]{2,1,0:T(8,128)(2,1)}), bf16[16,16,1024]{2,1,0:T(8,128)(2,1)S(1)}, u32[]{:S(2)}, u32[]{:S(2)}) %all-to-all-start) | async-done | bytes 524320 | tf_op jit(solution)/shard_map/all_to_all | solution.py:345
  32.7 4.4 %transform.1.refs_0_ = bf16[16,8192]{1,0:T(8,128)(2,1)S(1)} custom-call(bf16[16,16,1024]{2,1,0:T(8,128)(2,1)S(1)} %all-to-all-done.x_ref, f32[8,8192]{1,0:T(8,128)S(1)} %get-tuple-element.25.cos_ref, f32[8,8192]{1,0:T(8,128)S(1)} %get-tuple-element.26.sin_ref, bf16[272,256]{1,0:T(8,128)(2,1)S(1)} %copy-done.6, f32[2,136,128]{2,1,0:T(8,128)S(1)} %copy-done.5, ...), custom_call_target="tpu_custom_call" | custom-call | tf_op jit(solution)/shard_map/transform/pallas_call | solution.py:374
  37.0 2.9 %collective-permute-start.3 = (bf16[16,8192]{1,0:T(8,128)(2,1)S(1)}, bf16[16,8192]{1,0:T(8,128)(2,1)S(1)}, u32[]{:S(2)}, u32[]{:S(2)}) collective-permute-start(bf16[16,8192]{1,0:T(8,128)(2,1)S(1)} %transform.1.refs_0_), channel_id=1, source_target_pairs={{0,1},{1,0},{2,3},{3,2},{4,5},{5,4},{6,7},{7,6},{8,9},{9,8},{10,11... | collective-permute-start | bytes 786440 | tf_op jit(solution)/shard_map/ppermute | solution.py:296
  39.9 2.2 %collective-permute-start.2 = (bf16[16,8192]{1,0:T(8,128)(2,1)S(1)}, bf16[16,8192]{1,0:T(8,128)(2,1)S(1)}, u32[]{:S(2)}, u32[]{:S(2)}) collective-permute-start(bf16[16,8192]{1,0:T(8,128)(2,1)S(1)} %transform.1.refs_0_), channel_id=1, source_target_pairs={{0,2},{2,4},{4,6},{6,8},{8,10},{10,12},{12,14},{14,0},{1,15},{3,1}... | collective-permute-start | bytes 786440 | tf_op jit(solution)/shard_map/ppermute | solution.py:293
  42.1 0.0 collective-permute-done.3.refs_8_
  42.1 1.2 %collective-permute-start.4 = (bf16[16,8192]{1,0:T(8,128)(2,1)S(1)}, bf16[16,8192]{1,0:T(8,128)(2,1)S(1)}, u32[]{:S(2)}, u32[]{:S(2)}) collective-permute-start(bf16[16,8192]{1,0:T(8,128)(2,1)S(1)} %collective-permute-done.3.refs_8_), channel_id=1, source_target_pairs={{0,2},{2,4},{4,6},{6,8},{8,10},{10,12},{12,14},{14,0},{1,15},{3,1}... | collective-permute-start | bytes 786440 | tf_op jit(solution)/shard_map/ppermute | solution.py:293
  43.2 2.2 %collective-permute-done.2.refs_1_ = bf16[16,8192]{1,0:T(8,128)(2,1)S(1)} collective-permute-done((bf16[16,8192]{1,0:T(8,128)(2,1)S(1)}, bf16[16,8192]{1,0:T(8,128)(2,1)S(1)}, u32[]{:S(2)}, u32[]{:S(2)}) %collective-permute-start.2) | collective-permute-done | bytes 262176 | tf_op jit(solution)/shard_map/ppermute | solution.py:293
  45.4 3.1 %collective-permute-start.6 = (bf16[16,8192]{1,0:T(8,128)(2,1)S(1)}, bf16[16,8192]{1,0:T(8,128)(2,1)S(1)}, u32[]{:S(2)}, u32[]{:S(2)}) collective-permute-start(bf16[16,8192]{1,0:T(8,128)(2,1)S(1)} %collective-permute-done.2.refs_1_), channel_id=1, source_target_pairs={{0,2},{2,4},{4,6},{6,8},{8,10},{10,12},{12,14},{14,0},{1,15},{3,1}... | collective-permute-start | bytes 786440 | tf_op jit(solution)/shard_map/ppermute | solution.py:293
  48.5 2.8 %collective-permute-start.7 = (bf16[16,8192]{1,0:T(8,128)(2,1)S(1)}, bf16[16,8192]{1,0:T(8,128)(2,1)S(1)}, u32[]{:S(2)}, u32[]{:S(2)}) collective-permute-start(bf16[16,8192]{1,0:T(8,128)(2,1)S(1)} %collective-permute-done.4.refs_9_), channel_id=1, source_target_pairs={{0,2},{2,4},{4,6},{6,8},{8,10},{10,12},{12,14},{14,0},{1,15},{3,1}... | collective-permute-start | bytes 786440 | tf_op jit(solution)/shard_map/ppermute | solution.py:293
  51.3 0.5 collective-permute-done.6.refs_3_
  51.8 3.1 %collective-permute-start.9 = (bf16[16,8192]{1,0:T(8,128)(2,1)S(1)}, bf16[16,8192]{1,0:T(8,128)(2,1)S(1)}, u32[]{:S(2)}, u32[]{:S(2)}) collective-permute-start(bf16[16,8192]{1,0:T(8,128)(2,1)S(1)} %collective-permute-done.6.refs_3_), channel_id=1, source_target_pairs={{0,2},{2,4},{4,6},{6,8},{8,10},{10,12},{12,14},{14,0},{1,15},{3,1}... | collective-permute-start | bytes 786440 | tf_op jit(solution)/shard_map/ppermute | solution.py:293
  54.9 0.2 collective-permute-start.13
  55.2 0.3 collective-permute-start.5
  55.5 0.0 collective-permute-done.7.refs_11_
  55.5 2.7 %collective-permute-start.10 = (bf16[16,8192]{1,0:T(8,128)(2,1)S(1)}, bf16[16,8192]{1,0:T(8,128)(2,1)S(1)}, u32[]{:S(2)}, u32[]{:S(2)}) collective-permute-start(bf16[16,8192]{1,0:T(8,128)(2,1)S(1)} %collective-permute-done.7.refs_11_), channel_id=1, source_target_pairs={{0,2},{2,4},{4,6},{6,8},{8,10},{10,12},{12,14},{14,0},{1,15},{3,1}... | collective-permute-start | bytes 786440 | tf_op jit(solution)/shard_map/ppermute | solution.py:293
  58.1 0.1 collective-permute-done.9.refs_5_
  58.3 3.1 %collective-permute-start.12 = (bf16[16,8192]{1,0:T(8,128)(2,1)S(1)}, bf16[16,8192]{1,0:T(8,128)(2,1)S(1)}, u32[]{:S(2)}, u32[]{:S(2)}) collective-permute-start(bf16[16,8192]{1,0:T(8,128)(2,1)S(1)} %collective-permute-done.9.refs_5_), channel_id=1, source_target_pairs={{0,2},{2,4},{4,6},{6,8},{8,10},{10,12},{12,14},{14,0},{1,15},{3,1}... | collective-permute-start | bytes 786440 | tf_op jit(solution)/shard_map/ppermute | solution.py:293
  61.4 1.4 %collective-permute-start.14 = (bf16[16,8192]{1,0:T(8,128)(2,1)S(1)}, bf16[16,8192]{1,0:T(8,128)(2,1)S(1)}, u32[]{:S(2)}, u32[]{:S(2)}) collective-permute-start(bf16[16,8192]{1,0:T(8,128)(2,1)S(1)} %collective-permute-done.6.refs_3_), channel_id=1, source_target_pairs={{0,1},{1,0},{2,3},{3,2},{4,5},{5,4},{6,7},{7,6},{8,9},{9,8},{10,11... | collective-permute-start | bytes 786440 | tf_op jit(solution)/shard_map/ppermute | solution.py:296
  62.8 0.1 collective-permute-start.8
  62.9 0.0 collective-permute-done.5.refs_2_
  62.9 0.4 collective-permute-start.15
  63.3 2.3 %collective-permute-start.11 = (bf16[16,8192]{1,0:T(8,128)(2,1)S(1)}, bf16[16,8192]{1,0:T(8,128)(2,1)S(1)}, u32[]{:S(2)}, u32[]{:S(2)}) collective-permute-start(bf16[16,8192]{1,0:T(8,128)(2,1)S(1)} %collective-permute-done.10.refs_13_), channel_id=1, source_target_pairs={{0,1},{1,0},{2,3},{3,2},{4,5},{5,4},{6,7},{7,6},{8,9},{9,8},{10,11... | collective-permute-start | bytes 786440 | tf_op jit(solution)/shard_map/ppermute | solution.py:296
  65.6 4.8 %collective-permute-start.16 = (bf16[16,8192]{1,0:T(8,128)(2,1)S(1)}, bf16[16,8192]{1,0:T(8,128)(2,1)S(1)}, u32[]{:S(2)}, u32[]{:S(2)}) collective-permute-start(bf16[16,8192]{1,0:T(8,128)(2,1)S(1)} %collective-permute-done.12.refs_7_), channel_id=1, source_target_pairs={{0,1},{1,0},{2,3},{3,2},{4,5},{5,4},{6,7},{7,6},{8,9},{9,8},{10,11... | collective-permute-start | bytes 786440 | tf_op jit(solution)/shard_map/ppermute | solution.py:296
  70.3 0.1 fusion.11.order_ref
  70.4 0.0 collective-permute-done.8.refs_4_
  70.5 0.0 collective-permute-done.15.refs_14_
  70.5 1.0 %collective-permute-done.16.refs_15_ = bf16[16,8192]{1,0:T(8,128)(2,1)S(1)} collective-permute-done((bf16[16,8192]{1,0:T(8,128)(2,1)S(1)}, bf16[16,8192]{1,0:T(8,128)(2,1)S(1)}, u32[]{:S(2)}, u32[]{:S(2)}) %collective-permute-start.16) | collective-permute-done | bytes 262176 | tf_op jit(solution)/shard_map/ppermute | solution.py:296
  71.5 8.6 %gather_attend.1 = (bf16[768,128]{1,0:T(8,128)(2,1)S(1)}, bf16[2,128,8192]{2,1,0:T(8,128)(2,1)S(1)}) custom-call(s32[1]{0:T(128)} %bitcast.core_ref, bf16[768,128]{1,0:T(8,128)(2,1)S(1)} %collective-permute-done.1.q_ref, bf16[128,128]{1,0:T(8,128)(2,1)S(1)} %fusion.11.order_ref, bf16[16,8192]{1,0:T(8,128)(2,1)S(1)} %transform.1.refs_0_, ...), custom_call_target="tpu_custom_call" | custom-call | tf_op jit(solution)/shard_map/gather_attend/pallas_call | solution.py:248
  80.1 1.1 %collective-permute-start.17 = (bf16[768,128]{1,0:T(8,128)(2,1)S(1)}, bf16[768,128]{1,0:T(8,128)(2,1)S(1)}, u32[]{:S(2)}, u32[]{:S(2)}) collective-permute-start(bf16[768,128]{1,0:T(8,128)(2,1)S(1)} %get-tuple-element.28), channel_id=1, source_target_pairs={{0,16},{16,0},{1,17},{17,1},{2,18},{18,2},{3,19},{19,3},{4,20},{20... | collective-permute-start | bytes 589832 | tf_op jit(solution)/shard_map/ppermute | solution.py:392
  81.2 8.1 %attend.1 = bf16[768,128]{1,0:T(8,128)(2,1)S(1)} custom-call(s32[1]{0:T(128)} %bitcast.core_ref, bf16[768,128]{1,0:T(8,128)(2,1)S(1)} %get-tuple-element.22.q_ref, bf16[128,128]{1,0:T(8,128)(2,1)S(1)} %fusion.11.order_ref, bf16[2,128,8192]{2,1,0:T(8,128)(2,1)S(1)} %get-tuple-element.27.kv_ref), custom_call_target="tpu_custom_call" | custom-call | tf_op jit(solution)/shard_map/attend/pallas_call | solution.py:272
  89.4 0.8 maximum_select_fusion
  (22 shorter events, 0.1 us)
Async XLA Ops:
  0.0 0.9 %copy-start.1 = (bf16[512,256]{1,0:T(8,128)(2,1)S(1)}, bf16[512,256]{1,0:T(8,128)(2,1)}, u32[]{:S(2)}) copy-start(bf16[512,256]{1,0:T(8,128)(2,1)} %keys_ref.1) | copy-start | bytes 786436
  1.0 0.9 %copy-start.2 = (bf16[512,256]{1,0:T(8,128)(2,1)S(1)}, bf16[512,256]{1,0:T(8,128)(2,1)}, u32[]{:S(2)}) copy-start(bf16[512,256]{1,0:T(8,128)(2,1)} %values_ref.1) | copy-start | bytes 786436
  2.0 4.5 %collective-permute-start = (bf16[512,256]{1,0:T(8,128)(2,1)S(1)}, bf16[512,256]{1,0:T(8,128)(2,1)S(1)}, u32[]{:S(2)}, u32[]{:S(2)}) collective-permute-start(bf16[512,256]{1,0:T(8,128)(2,1)S(1)} %get-tuple-element.18), channel_id=1, source_target_pairs={{0,1},{1,0},{2,3},{3,2},{4,5},{5,4},{6,7},{7,6},{8,9},{9,8},{10,11... | collective-permute-start | bytes 786440 | tf_op jit(solution)/shard_map/ppermute | solution.py:335
  8.2 24.5 %copy-start = (bf16[2,512,256]{2,1,0:T(8,128)(2,1)S(1)}, bf16[2,512,256]{2,1,0:T(8,128)(2,1)}, u32[]{:S(2)}) copy-start(bf16[2,512,256]{2,1,0:T(8,128)(2,1)} %constant.141.clone.middle_hbm) | copy-start | bytes 1572868
  8.2 24.5 %copy-start.3 = (bf16[2,128,272]{2,1,0:T(8,128)(2,1)S(1)}, bf16[2,128,272]{2,1,0:T(8,128)(2,1)}, u32[]{:S(2)}) copy-start(bf16[2,128,272]{2,1,0:T(8,128)(2,1)} %constant.143.clone.last_hbm) | copy-start | bytes 417796
  8.2 24.5 %copy-start.4 = (f32[2,136,128]{2,1,0:T(8,128)S(1)}, f32[2,136,128]{2,1,0:T(8,128)}, u32[]{:S(2)}) copy-start(f32[2,136,128]{2,1,0:T(8,128)} %constant.142.clone.untwist_hbm) | copy-start | bytes 417796
  8.2 24.5 %copy-start.5 = (f32[2,136,128]{2,1,0:T(8,128)S(1)}, f32[2,136,128]{2,1,0:T(8,128)}, u32[]{:S(2)}) copy-start(f32[2,136,128]{2,1,0:T(8,128)} %constant.140.clone.twist_hbm) | copy-start | bytes 417796
  8.2 24.5 %copy-start.6 = (bf16[272,256]{1,0:T(8,128)(2,1)S(1)}, bf16[272,256]{1,0:T(8,128)(2,1)}, u32[]{:S(2)}) copy-start(bf16[272,256]{1,0:T(8,128)(2,1)} %constant.139.clone.first_hbm) | copy-start | bytes 417796
  8.2 24.4 %all-to-all-start = ((bf16[16,16,1024]{2,1,0:T(8,128)(2,1)}), bf16[16,16,1024]{2,1,0:T(8,128)(2,1)S(1)}, u32[]{:S(2)}, u32[]{:S(2)}) async-start(bf16[16,16,1024]{2,1,0:T(8,128)(2,1)} %pack.1), calls=%async_computation | async-start | bytes 1048576 | tf_op jit(solution)/shard_map/all_to_all | solution.py:345
  20.8 9.9 %collective-permute-start.1 = (bf16[768,128]{1,0:T(8,128)(2,1)S(1)}, bf16[768,128]{1,0:T(8,128)(2,1)S(1)}, u32[]{:S(2)}, u32[]{:S(2)}) collective-permute-start(bf16[768,128]{1,0:T(8,128)(2,1)S(1)} %get-tuple-element.31), channel_id=1, source_target_pairs={{0,16},{16,0},{1,17},{17,1},{2,18},{18,2},{3,19},{19,3},{4,20},{20... | collective-permute-start | bytes 589832 | tf_op jit(solution)/shard_map/ppermute | solution.py:363
  37.0 5.1 %collective-permute-start.3 = (bf16[16,8192]{1,0:T(8,128)(2,1)S(1)}, bf16[16,8192]{1,0:T(8,128)(2,1)S(1)}, u32[]{:S(2)}, u32[]{:S(2)}) collective-permute-start(bf16[16,8192]{1,0:T(8,128)(2,1)S(1)} %transform.1.refs_0_), channel_id=1, source_target_pairs={{0,1},{1,0},{2,3},{3,2},{4,5},{5,4},{6,7},{7,6},{8,9},{9,8},{10,11... | collective-permute-start | bytes 786440 | tf_op jit(solution)/shard_map/ppermute | solution.py:296
  39.9 5.5 %collective-permute-start.2 = (bf16[16,8192]{1,0:T(8,128)(2,1)S(1)}, bf16[16,8192]{1,0:T(8,128)(2,1)S(1)}, u32[]{:S(2)}, u32[]{:S(2)}) collective-permute-start(bf16[16,8192]{1,0:T(8,128)(2,1)S(1)} %transform.1.refs_0_), channel_id=1, source_target_pairs={{0,2},{2,4},{4,6},{6,8},{8,10},{10,12},{12,14},{14,0},{1,15},{3,1}... | collective-permute-start | bytes 786440 | tf_op jit(solution)/shard_map/ppermute | solution.py:293
  42.1 6.4 %collective-permute-start.4 = (bf16[16,8192]{1,0:T(8,128)(2,1)S(1)}, bf16[16,8192]{1,0:T(8,128)(2,1)S(1)}, u32[]{:S(2)}, u32[]{:S(2)}) collective-permute-start(bf16[16,8192]{1,0:T(8,128)(2,1)S(1)} %collective-permute-done.3.refs_8_), channel_id=1, source_target_pairs={{0,2},{2,4},{4,6},{6,8},{8,10},{10,12},{12,14},{14,0},{1,15},{3,1}... | collective-permute-start | bytes 786440 | tf_op jit(solution)/shard_map/ppermute | solution.py:293
  45.4 6.4 %collective-permute-start.6 = (bf16[16,8192]{1,0:T(8,128)(2,1)S(1)}, bf16[16,8192]{1,0:T(8,128)(2,1)S(1)}, u32[]{:S(2)}, u32[]{:S(2)}) collective-permute-start(bf16[16,8192]{1,0:T(8,128)(2,1)S(1)} %collective-permute-done.2.refs_1_), channel_id=1, source_target_pairs={{0,2},{2,4},{4,6},{6,8},{8,10},{10,12},{12,14},{14,0},{1,15},{3,1}... | collective-permute-start | bytes 786440 | tf_op jit(solution)/shard_map/ppermute | solution.py:293
  48.5 6.9 %collective-permute-start.7 = (bf16[16,8192]{1,0:T(8,128)(2,1)S(1)}, bf16[16,8192]{1,0:T(8,128)(2,1)S(1)}, u32[]{:S(2)}, u32[]{:S(2)}) collective-permute-start(bf16[16,8192]{1,0:T(8,128)(2,1)S(1)} %collective-permute-done.4.refs_9_), channel_id=1, source_target_pairs={{0,2},{2,4},{4,6},{6,8},{8,10},{10,12},{12,14},{14,0},{1,15},{3,1}... | collective-permute-start | bytes 786440 | tf_op jit(solution)/shard_map/ppermute | solution.py:293
  51.8 6.4 %collective-permute-start.9 = (bf16[16,8192]{1,0:T(8,128)(2,1)S(1)}, bf16[16,8192]{1,0:T(8,128)(2,1)S(1)}, u32[]{:S(2)}, u32[]{:S(2)}) collective-permute-start(bf16[16,8192]{1,0:T(8,128)(2,1)S(1)} %collective-permute-done.6.refs_3_), channel_id=1, source_target_pairs={{0,2},{2,4},{4,6},{6,8},{8,10},{10,12},{12,14},{14,0},{1,15},{3,1}... | collective-permute-start | bytes 786440 | tf_op jit(solution)/shard_map/ppermute | solution.py:293
  54.9 7.8 %collective-permute-start.13 = (bf16[16,8192]{1,0:T(8,128)(2,1)S(1)}, bf16[16,8192]{1,0:T(8,128)(2,1)S(1)}, u32[]{:S(2)}, u32[]{:S(2)}) collective-permute-start(bf16[16,8192]{1,0:T(8,128)(2,1)S(1)} %collective-permute-done.2.refs_1_), channel_id=1, source_target_pairs={{0,1},{1,0},{2,3},{3,2},{4,5},{5,4},{6,7},{7,6},{8,9},{9,8},{10,11... | collective-permute-start | bytes 786440 | tf_op jit(solution)/shard_map/ppermute | solution.py:296
  55.2 7.7 %collective-permute-start.5 = (bf16[16,8192]{1,0:T(8,128)(2,1)S(1)}, bf16[16,8192]{1,0:T(8,128)(2,1)S(1)}, u32[]{:S(2)}, u32[]{:S(2)}) collective-permute-start(bf16[16,8192]{1,0:T(8,128)(2,1)S(1)} %collective-permute-done.4.refs_9_), channel_id=1, source_target_pairs={{0,1},{1,0},{2,3},{3,2},{4,5},{5,4},{6,7},{7,6},{8,9},{9,8},{10,11... | collective-permute-start | bytes 786440 | tf_op jit(solution)/shard_map/ppermute | solution.py:296
  55.5 7.8 %collective-permute-start.10 = (bf16[16,8192]{1,0:T(8,128)(2,1)S(1)}, bf16[16,8192]{1,0:T(8,128)(2,1)S(1)}, u32[]{:S(2)}, u32[]{:S(2)}) collective-permute-start(bf16[16,8192]{1,0:T(8,128)(2,1)S(1)} %collective-permute-done.7.refs_11_), channel_id=1, source_target_pairs={{0,2},{2,4},{4,6},{6,8},{8,10},{10,12},{12,14},{14,0},{1,15},{3,1}... | collective-permute-start | bytes 786440 | tf_op jit(solution)/shard_map/ppermute | solution.py:293
  58.3 7.3 %collective-permute-start.12 = (bf16[16,8192]{1,0:T(8,128)(2,1)S(1)}, bf16[16,8192]{1,0:T(8,128)(2,1)S(1)}, u32[]{:S(2)}, u32[]{:S(2)}) collective-permute-start(bf16[16,8192]{1,0:T(8,128)(2,1)S(1)} %collective-permute-done.9.refs_5_), channel_id=1, source_target_pairs={{0,2},{2,4},{4,6},{6,8},{8,10},{10,12},{12,14},{14,0},{1,15},{3,1}... | collective-permute-start | bytes 786440 | tf_op jit(solution)/shard_map/ppermute | solution.py:293
  61.4 9.1 %collective-permute-start.14 = (bf16[16,8192]{1,0:T(8,128)(2,1)S(1)}, bf16[16,8192]{1,0:T(8,128)(2,1)S(1)}, u32[]{:S(2)}, u32[]{:S(2)}) collective-permute-start(bf16[16,8192]{1,0:T(8,128)(2,1)S(1)} %collective-permute-done.6.refs_3_), channel_id=1, source_target_pairs={{0,1},{1,0},{2,3},{3,2},{4,5},{5,4},{6,7},{7,6},{8,9},{9,8},{10,11... | collective-permute-start | bytes 786440 | tf_op jit(solution)/shard_map/ppermute | solution.py:296
  62.8 7.7 %collective-permute-start.8 = (bf16[16,8192]{1,0:T(8,128)(2,1)S(1)}, bf16[16,8192]{1,0:T(8,128)(2,1)S(1)}, u32[]{:S(2)}, u32[]{:S(2)}) collective-permute-start(bf16[16,8192]{1,0:T(8,128)(2,1)S(1)} %collective-permute-done.7.refs_11_), channel_id=1, source_target_pairs={{0,1},{1,0},{2,3},{3,2},{4,5},{5,4},{6,7},{7,6},{8,9},{9,8},{10,11... | collective-permute-start | bytes 786440 | tf_op jit(solution)/shard_map/ppermute | solution.py:296
  62.9 7.6 %collective-permute-start.15 = (bf16[16,8192]{1,0:T(8,128)(2,1)S(1)}, bf16[16,8192]{1,0:T(8,128)(2,1)S(1)}, u32[]{:S(2)}, u32[]{:S(2)}) collective-permute-start(bf16[16,8192]{1,0:T(8,128)(2,1)S(1)} %collective-permute-done.9.refs_5_), channel_id=1, source_target_pairs={{0,1},{1,0},{2,3},{3,2},{4,5},{5,4},{6,7},{7,6},{8,9},{9,8},{10,11... | collective-permute-start | bytes 786440 | tf_op jit(solution)/shard_map/ppermute | solution.py:296
  63.3 7.2 %collective-permute-start.11 = (bf16[16,8192]{1,0:T(8,128)(2,1)S(1)}, bf16[16,8192]{1,0:T(8,128)(2,1)S(1)}, u32[]{:S(2)}, u32[]{:S(2)}) collective-permute-start(bf16[16,8192]{1,0:T(8,128)(2,1)S(1)} %collective-permute-done.10.refs_13_), channel_id=1, source_target_pairs={{0,1},{1,0},{2,3},{3,2},{4,5},{5,4},{6,7},{7,6},{8,9},{9,8},{10,11... | collective-permute-start | bytes 786440 | tf_op jit(solution)/shard_map/ppermute | solution.py:296
  65.6 5.9 %collective-permute-start.16 = (bf16[16,8192]{1,0:T(8,128)(2,1)S(1)}, bf16[16,8192]{1,0:T(8,128)(2,1)S(1)}, u32[]{:S(2)}, u32[]{:S(2)}) collective-permute-start(bf16[16,8192]{1,0:T(8,128)(2,1)S(1)} %collective-permute-done.12.refs_7_), channel_id=1, source_target_pairs={{0,1},{1,0},{2,3},{3,2},{4,5},{5,4},{6,7},{7,6},{8,9},{9,8},{10,11... | collective-permute-start | bytes 786440 | tf_op jit(solution)/shard_map/ppermute | solution.py:296
  80.1 9.3 %collective-permute-start.17 = (bf16[768,128]{1,0:T(8,128)(2,1)S(1)}, bf16[768,128]{1,0:T(8,128)(2,1)S(1)}, u32[]{:S(2)}, u32[]{:S(2)}) collective-permute-start(bf16[768,128]{1,0:T(8,128)(2,1)S(1)} %get-tuple-element.28), channel_id=1, source_target_pairs={{0,16},{16,0},{1,17},{17,1},{2,18},{18,2},{3,19},{19,3},{4,20},{20... | collective-permute-start | bytes 589832 | tf_op jit(solution)/shard_map/ppermute | solution.py:392

commit v2 on v1

--- a/solution.py
+++ b/solution.py
@@ -61,8 +61,9 @@
     weight = np.where((k0 == 0) | (k0 == BASE), 1.0 / WINDOW, 2.0 / WINDOW)[:, None] * live
     angle = np.pi * np.outer(k0, 2 * np.tile(t0, 2) + 1) / WINDOW
     untwist = np.stack([weight * np.cos(angle), weight * np.sin(angle)]).astype(np.float32)
-    angle = 2 * np.pi * (np.outer(t1, k0) % 256) / 256
-    last = np.concatenate([np.cos(angle) * live.T, -np.sin(angle) * live.T], axis=1)
+    angle = 2 * np.pi * (np.outer(t1, k0[:BASE]) % 256) / 256
+    last = np.concatenate([np.cos(angle), -np.sin(angle)], axis=1)
+    last[:, BASE] = (-1.0) ** t1
     last = np.stack(split(last))
     return first, twist, middle, untwist, last
 
@@ -138,23 +139,28 @@
     for copy in copies:
         copy.wait()
     cosine, sine = twist_ref[0], twist_ref[1]
-    z_real, z_imag = [], []
+    parts = []
     for pair in range(columns // 2):
         xp = x[:, pair * 256 : pair * 256 + 256]
         one = dot(first_ref[...], jnp.concatenate([xp, xp], axis=0))
-        parts = []
+        part = []
         for which in range(2):
             real = one[:ROWS, which * BASE : which * BASE + BASE]
             imag = one[ROWS:, which * BASE : which * BASE + BASE]
-            parts.append(real * cosine + imag * sine)
-            parts.append(imag * cosine - real * sine)
-        high, low = halves(jnp.concatenate(parts, axis=1))
-        two = (
-            dot(high, middle_ref[0]) + dot(low, middle_ref[0]) + dot(high, middle_ref[1])
-        )
-        real, imag = two[:, :BASE], two[:, BASE:]
-        z_real.append(real * untwist_ref[0] - imag * untwist_ref[1])
-        z_imag.append(real * untwist_ref[1] + imag * untwist_ref[0])
+            part.append(real * cosine + imag * sine)
+            part.append(imag * cosine - real * sine)
+        parts.append(jnp.concatenate(part, axis=1))
+    high, low = halves(jnp.concatenate(parts, axis=0))
+    two = dot(high, middle_ref[0]) + dot(low, middle_ref[0]) + dot(high, middle_ref[1])
+    top = lax.broadcasted_iota(jnp.int32, (BASE, BASE), 0) == 0
+    z_real, z_imag = [], []
+    for pair in range(columns // 2):
+        real = two[pair * ROWS : pair * ROWS + ROWS, :BASE]
+        imag = two[pair * ROWS : pair * ROWS + ROWS, BASE:]
+        up = real * untwist_ref[0] - imag * untwist_ref[1]
+        down = real * untwist_ref[1] + imag * untwist_ref[0]
+        z_real.append(up[:BASE])
+        z_imag.append(jnp.where(top, up[BASE : BASE + 1], down[:BASE]))
     z = jnp.concatenate(
         [jnp.concatenate(z_real, axis=1), jnp.concatenate(z_imag, axis=1)], axis=0
     )
@@ -207,7 +213,7 @@
 
 
 SCALE = math.log2(math.e) / math.sqrt(HEAD)
-ROW_BLOCK = 384
+ROW_BLOCK = 768
 TOKEN_BLOCK = 2048
 CHUNKS = 1
 
@@ -341,11 +347,12 @@
         compiler_params=pltpu.CompilerParams(vmem_limit_bytes=16 * 1024 * 1024),
         name="pack",
     )(core_here, kept_tokens, other)
-    packed, queries, positions = lax.optimization_barrier((packed, queries, positions))
+    places_here = positions.astype(F32)
+    packed, queries, places_here = lax.optimization_barrier((packed, queries, places_here))
     received = lax.all_to_all(packed, ("yhi", "z"), 0, 0, tiled=True)
 
     freq = inverse_freq()
-    angles = positions.astype(F32)[:, None] * freq[None, :]
+    angles = places_here[:, None] * freq[None, :]
     cosine, sine = jnp.cos(angles), jnp.sin(angles)
     wide = queries.astype(F32)
     up, down = wide[..., :HALF], wide[..., HALF:]

time: 90.5 us -> 88.4 us (0.977)
  Pallas kernels: 22.1 us -> 20.7 us
  transfers between devices with their start and end apart: 19 -> 19, of which waited for: 7 -> 7; matrix products, arithmetic and copies ran while one was open for 5% -> 6% of each run, Pallas kernels for 9% -> 9%
where the time goes in v2:
time: 88.4 us; the launch traced here: 88.1 us
  starting transfers between devices  47.2 us (53%)
  Pallas kernels  20.7 us (23%)
  waiting for transfers between devices  12.1 us (14%)
  other arithmetic  5.51 us (6%)
  local copies, waits for them, and re-layouts  1.99 us (2%)
    ppermute x7, starting transfers between devices, along(): return lax.ppermute(block, ('z', 'core'), onward)  18.1 us
    ppermute x8, starting transfers between devices, across(): return lax.ppermute(block, 'core', SWAP)  12.3 us
    all_to_all x1, starting transfers between devices, on_device(): received = lax.all_to_all(packed, ('yhi', 'z'), 0, 0, tiled=True)  9.33 us
    pallas_call x1, Pallas kernels, gather_attend(): pl.pallas_call(gather_attend_kernel, grid=(rows // ROW_BLOCK,), in_specs=...  8.19 us
    pallas_call x1, Pallas kernels, attend(): pl.pallas_call(attend_kernel, grid=(q.shape[0] // ROW_BLOCK,), in_specs=[...  7.7 us
    ppermute x1, waiting for transfers between devices, on_device(): lax.ppermute(jnp.where(head == 0, turned[1], turned[0]), 'yhi', SWAP)  5.97 us
    pallas_call x1, Pallas kernels, on_device(): pl.pallas_call(transform_kernel, in_specs=[vmem] * 3 + [hbm] * 5, out_spe...  3.77 us
    ppermute x1, starting transfers between devices, on_device(): other = lax.ppermute(send, 'core', SWAP)  3.33 us
  transfers between devices with their start and end apart: 19, of which 7 were waited for; matrix products, arithmetic and copies ran while one was open for 6% of the time, Pallas kernels for 9%

profile of v2, /device:TPU:1, one launch (start us, length us, event | category | flops | bytes accessed | tf_op | source)
XLA Modules:
  0.0 88.1 jit_solution(3724126276696064542)
XLA Ops:
  0.0 0.9 %copy-done.1 = bf16[512,256]{1,0:T(8,128)(2,1)S(1)} copy-done((bf16[512,256]{1,0:T(8,128)(2,1)S(1)}, bf16[512,256]{1,0:T(8,128)(2,1)}, u32[]{:S(2)}) %copy-start.1) | copy-done | bytes 262168
  1.0 0.9 %copy-done.2 = bf16[512,256]{1,0:T(8,128)(2,1)S(1)} copy-done((bf16[512,256]{1,0:T(8,128)(2,1)S(1)}, bf16[512,256]{1,0:T(8,128)(2,1)}, u32[]{:S(2)}) %copy-start.2) | copy-done | bytes 262168
  1.9 0.1 choose.1
  2.0 3.3 %collective-permute-start = (bf16[512,256]{1,0:T(8,128)(2,1)S(1)}, bf16[512,256]{1,0:T(8,128)(2,1)S(1)}, u32[]{:S(2)}, u32[]{:S(2)}) collective-permute-start(bf16[512,256]{1,0:T(8,128)(2,1)S(1)} %get-tuple-element.18), channel_id=1, source_target_pairs={{0,1},{1,0},{2,3},{3,2},{4,5},{5,4},{6,7},{7,6},{8,9},{9,8},{10,11... | collective-permute-start | bytes 786440 | tf_op jit(solution)/shard_map/ppermute | solution.py:341
  5.3 0.7 convert_element_type.30
  6.0 0.1 dynamic_slice.3
  6.1 0.4 collective-permute-done.other_ref
  6.5 1.0 %pack.1 = bf16[16,16,1024]{2,1,0:T(8,128)(2,1)} custom-call(s32[1]{0:T(128)} %bitcast.core_ref, bf16[512,256]{1,0:T(8,128)(2,1)S(1)} %get-tuple-element.17.mine_ref, bf16[512,256]{1,0:T(8,128)(2,1)S(1)} %collective-permute-done.other_ref), custom_call_target="tpu_custom_call" | custom-call | tf_op jit(solution)/shard_map/pack/pallas_call | solution.py:342
  7.5 0.0 copy-start.6
  7.5 9.3 %all-to-all-start = ((bf16[16,16,1024]{2,1,0:T(8,128)(2,1)}), bf16[16,16,1024]{2,1,0:T(8,128)(2,1)S(1)}, u32[]{:S(2)}, u32[]{:S(2)}) async-start(bf16[16,16,1024]{2,1,0:T(8,128)(2,1)} %pack.1), calls=%async_computation | async-start | bytes 1048576 | tf_op jit(solution)/shard_map/all_to_all | solution.py:352
  16.8 1.4 %multiply_cosine_fusion = (f32[768,64]{1,0:T(8,128)S(1)}, f32[768,64]{1,0:T(8,128)S(1)}) fusion(f32[64]{0:T(128)S(1)} %multiply_exponential_fusion, f32[768]{0:T(1024)S(1)} %convert_element_type.30), kind=kLoop, calls=%fused_computation.4 | loop fusion | flops 49152 | bytes 396544 | tf_op jit(solution)/shard_map/cos | solution.py:356
  18.3 1.1 %convert_element_type.31 = f32[2,768,128]{2,1,0:T(8,128)S(1)} convert(bf16[2,768,128]{2,1,0:T(8,128)(2,1)} %param.11) | non-fusion elementwise | flops 196608 | bytes 1179648 | tf_op jit(solution)/shard_map/convert_element_type | solution.py:357
  19.3 0.4 subtract_convert_fusion
  19.7 0.3 convolution_convert_fusion
  20.1 3.0 %collective-permute-start.1 = (bf16[768,128]{1,0:T(8,128)(2,1)S(1)}, bf16[768,128]{1,0:T(8,128)(2,1)S(1)}, u32[]{:S(2)}, u32[]{:S(2)}) collective-permute-start(bf16[768,128]{1,0:T(8,128)(2,1)S(1)} %get-tuple-element.31), channel_id=1, source_target_pairs={{0,16},{16,0},{1,17},{17,1},{2,18},{18,2},{3,19},{19,3},{4,20},{20... | collective-permute-start | bytes 589832 | tf_op jit(solution)/shard_map/ppermute | solution.py:370
  23.1 1.0 %fusion.4 = (f32[8,8192]{1,0:T(8,128)S(1)}, f32[8,8192]{1,0:T(8,128)S(1)}) fusion(f32[8192]{0:T(1024)S(1)} %fusion.15, f32[8]{0:T(128)S(1)} %dynamic_slice.3, pred[]{:T(512)S(6)} %eq.47), kind=kLoop, calls=%fused_computation.12 | loop fusion | flops 196608 | bytes 557089 | tf_op jit(solution)/shard_map/jit(_where)/select_n | solution.py:376
  24.1 6.0 %collective-permute-done.1.q_ref = bf16[768,128]{1,0:T(8,128)(2,1)S(1)} collective-permute-done((bf16[768,128]{1,0:T(8,128)(2,1)S(1)}, bf16[768,128]{1,0:T(8,128)(2,1)S(1)}, u32[]{:S(2)}, u32[]{:S(2)}) %collective-permute-start.1) | collective-permute-done | bytes 196640 | tf_op jit(solution)/shard_map/ppermute | solution.py:370
  30.0 1.9 %all-to-all-done.x_ref = bf16[16,16,1024]{2,1,0:T(8,128)(2,1)S(1)} async-done(((bf16[16,16,1024]{2,1,0:T(8,128)(2,1)}), bf16[16,16,1024]{2,1,0:T(8,128)(2,1)S(1)}, u32[]{:S(2)}, u32[]{:S(2)}) %all-to-all-start) | async-done | bytes 524320 | tf_op jit(solution)/shard_map/all_to_all | solution.py:352
  32.0 3.8 %transform.1.refs_0_ = bf16[16,8192]{1,0:T(8,128)(2,1)S(1)} custom-call(bf16[16,16,1024]{2,1,0:T(8,128)(2,1)S(1)} %all-to-all-done.x_ref, f32[8,8192]{1,0:T(8,128)S(1)} %get-tuple-element.25.cos_ref, f32[8,8192]{1,0:T(8,128)S(1)} %get-tuple-element.26.sin_ref, bf16[272,256]{1,0:T(8,128)(2,1)S(1)} %copy-done.5, f32[2,136,128]{2,1,0:T(8,128)S(1)} %copy-done.4, ...), custom_call_target="tpu_custom_call" | custom-call | tf_op jit(solution)/shard_map/transform/pallas_call | solution.py:381
  35.7 2.9 %collective-permute-start.3 = (bf16[16,8192]{1,0:T(8,128)(2,1)S(1)}, bf16[16,8192]{1,0:T(8,128)(2,1)S(1)}, u32[]{:S(2)}, u32[]{:S(2)}) collective-permute-start(bf16[16,8192]{1,0:T(8,128)(2,1)S(1)} %transform.1.refs_0_), channel_id=1, source_target_pairs={{0,1},{1,0},{2,3},{3,2},{4,5},{5,4},{6,7},{7,6},{8,9},{9,8},{10,11... | collective-permute-start | bytes 786440 | tf_op jit(solution)/shard_map/ppermute | solution.py:302
  38.6 2.2 %collective-permute-start.2 = (bf16[16,8192]{1,0:T(8,128)(2,1)S(1)}, bf16[16,8192]{1,0:T(8,128)(2,1)S(1)}, u32[]{:S(2)}, u32[]{:S(2)}) collective-permute-start(bf16[16,8192]{1,0:T(8,128)(2,1)S(1)} %transform.1.refs_0_), channel_id=1, source_target_pairs={{0,2},{2,4},{4,6},{6,8},{8,10},{10,12},{12,14},{14,0},{1,15},{3,1}... | collective-permute-start | bytes 786440 | tf_op jit(solution)/shard_map/ppermute | solution.py:299
  40.8 1.2 %collective-permute-start.4 = (bf16[16,8192]{1,0:T(8,128)(2,1)S(1)}, bf16[16,8192]{1,0:T(8,128)(2,1)S(1)}, u32[]{:S(2)}, u32[]{:S(2)}) collective-permute-start(bf16[16,8192]{1,0:T(8,128)(2,1)S(1)} %collective-permute-done.3.refs_8_), channel_id=1, source_target_pairs={{0,2},{2,4},{4,6},{6,8},{8,10},{10,12},{12,14},{14,0},{1,15},{3,1}... | collective-permute-start | bytes 786440 | tf_op jit(solution)/shard_map/ppermute | solution.py:299
  42.0 2.2 %collective-permute-done.2.refs_1_ = bf16[16,8192]{1,0:T(8,128)(2,1)S(1)} collective-permute-done((bf16[16,8192]{1,0:T(8,128)(2,1)S(1)}, bf16[16,8192]{1,0:T(8,128)(2,1)S(1)}, u32[]{:S(2)}, u32[]{:S(2)}) %collective-permute-start.2) | collective-permute-done | bytes 262176 | tf_op jit(solution)/shard_map/ppermute | solution.py:299
  44.1 3.1 %collective-permute-start.6 = (bf16[16,8192]{1,0:T(8,128)(2,1)S(1)}, bf16[16,8192]{1,0:T(8,128)(2,1)S(1)}, u32[]{:S(2)}, u32[]{:S(2)}) collective-permute-start(bf16[16,8192]{1,0:T(8,128)(2,1)S(1)} %collective-permute-done.2.refs_1_), channel_id=1, source_target_pairs={{0,2},{2,4},{4,6},{6,8},{8,10},{10,12},{12,14},{14,0},{1,15},{3,1}... | collective-permute-start | bytes 786440 | tf_op jit(solution)/shard_map/ppermute | solution.py:299
  47.2 2.8 %collective-permute-start.7 = (bf16[16,8192]{1,0:T(8,128)(2,1)S(1)}, bf16[16,8192]{1,0:T(8,128)(2,1)S(1)}, u32[]{:S(2)}, u32[]{:S(2)}) collective-permute-start(bf16[16,8192]{1,0:T(8,128)(2,1)S(1)} %collective-permute-done.4.refs_9_), channel_id=1, source_target_pairs={{0,2},{2,4},{4,6},{6,8},{8,10},{10,12},{12,14},{14,0},{1,15},{3,1}... | collective-permute-start | bytes 786440 | tf_op jit(solution)/shard_map/ppermute | solution.py:299
  50.0 0.5 collective-permute-done.6.refs_3_
  50.5 3.1 %collective-permute-start.9 = (bf16[16,8192]{1,0:T(8,128)(2,1)S(1)}, bf16[16,8192]{1,0:T(8,128)(2,1)S(1)}, u32[]{:S(2)}, u32[]{:S(2)}) collective-permute-start(bf16[16,8192]{1,0:T(8,128)(2,1)S(1)} %collective-permute-done.6.refs_3_), channel_id=1, source_target_pairs={{0,2},{2,4},{4,6},{6,8},{8,10},{10,12},{12,14},{14,0},{1,15},{3,1}... | collective-permute-start | bytes 786440 | tf_op jit(solution)/shard_map/ppermute | solution.py:299
  53.7 0.2 collective-permute-start.13
  53.9 0.3 collective-permute-start.5
  54.2 0.0 collective-permute-done.7.refs_11_
  54.2 2.7 %collective-permute-start.10 = (bf16[16,8192]{1,0:T(8,128)(2,1)S(1)}, bf16[16,8192]{1,0:T(8,128)(2,1)S(1)}, u32[]{:S(2)}, u32[]{:S(2)}) collective-permute-start(bf16[16,8192]{1,0:T(8,128)(2,1)S(1)} %collective-permute-done.7.refs_11_), channel_id=1, source_target_pairs={{0,2},{2,4},{4,6},{6,8},{8,10},{10,12},{12,14},{14,0},{1,15},{3,1}... | collective-permute-start | bytes 786440 | tf_op jit(solution)/shard_map/ppermute | solution.py:299
  56.9 0.1 collective-permute-done.9.refs_5_
  57.0 3.1 %collective-permute-start.12 = (bf16[16,8192]{1,0:T(8,128)(2,1)S(1)}, bf16[16,8192]{1,0:T(8,128)(2,1)S(1)}, u32[]{:S(2)}, u32[]{:S(2)}) collective-permute-start(bf16[16,8192]{1,0:T(8,128)(2,1)S(1)} %collective-permute-done.9.refs_5_), channel_id=1, source_target_pairs={{0,2},{2,4},{4,6},{6,8},{8,10},{10,12},{12,14},{14,0},{1,15},{3,1}... | collective-permute-start | bytes 786440 | tf_op jit(solution)/shard_map/ppermute | solution.py:299
  60.1 1.4 %collective-permute-start.14 = (bf16[16,8192]{1,0:T(8,128)(2,1)S(1)}, bf16[16,8192]{1,0:T(8,128)(2,1)S(1)}, u32[]{:S(2)}, u32[]{:S(2)}) collective-permute-start(bf16[16,8192]{1,0:T(8,128)(2,1)S(1)} %collective-permute-done.6.refs_3_), channel_id=1, source_target_pairs={{0,1},{1,0},{2,3},{3,2},{4,5},{5,4},{6,7},{7,6},{8,9},{9,8},{10,11... | collective-permute-start | bytes 786440 | tf_op jit(solution)/shard_map/ppermute | solution.py:302
  61.5 0.0 collective-permute-done.13.refs_10_
  61.5 0.1 collective-permute-start.8
  61.6 0.4 collective-permute-start.15
  62.0 0.0 collective-permute-done.10.refs_13_
  62.0 2.3 %collective-permute-start.11 = (bf16[16,8192]{1,0:T(8,128)(2,1)S(1)}, bf16[16,8192]{1,0:T(8,128)(2,1)S(1)}, u32[]{:S(2)}, u32[]{:S(2)}) collective-permute-start(bf16[16,8192]{1,0:T(8,128)(2,1)S(1)} %collective-permute-done.10.refs_13_), channel_id=1, source_target_pairs={{0,1},{1,0},{2,3},{3,2},{4,5},{5,4},{6,7},{7,6},{8,9},{9,8},{10,11... | collective-permute-start | bytes 786440 | tf_op jit(solution)/shard_map/ppermute | solution.py:302
  64.3 0.0 collective-permute-done.12.refs_7_
  64.3 4.8 %collective-permute-start.16 = (bf16[16,8192]{1,0:T(8,128)(2,1)S(1)}, bf16[16,8192]{1,0:T(8,128)(2,1)S(1)}, u32[]{:S(2)}, u32[]{:S(2)}) collective-permute-start(bf16[16,8192]{1,0:T(8,128)(2,1)S(1)} %collective-permute-done.12.refs_7_), channel_id=1, source_target_pairs={{0,1},{1,0},{2,3},{3,2},{4,5},{5,4},{6,7},{7,6},{8,9},{9,8},{10,11... | collective-permute-start | bytes 786440 | tf_op jit(solution)/shard_map/ppermute | solution.py:302
  69.1 0.1 fusion.11.order_ref
  69.2 0.0 collective-permute-done.15.refs_14_
  69.2 1.0 %collective-permute-done.16.refs_15_ = bf16[16,8192]{1,0:T(8,128)(2,1)S(1)} collective-permute-done((bf16[16,8192]{1,0:T(8,128)(2,1)S(1)}, bf16[16,8192]{1,0:T(8,128)(2,1)S(1)}, u32[]{:S(2)}, u32[]{:S(2)}) %collective-permute-start.16) | collective-permute-done | bytes 262176 | tf_op jit(solution)/shard_map/ppermute | solution.py:302
  70.2 8.2 %gather_attend.1 = (bf16[768,128]{1,0:T(8,128)(2,1)S(1)}, bf16[2,128,8192]{2,1,0:T(8,128)(2,1)S(1)}) custom-call(s32[1]{0:T(128)} %bitcast.core_ref, bf16[768,128]{1,0:T(8,128)(2,1)S(1)} %collective-permute-done.1.q_ref, bf16[128,128]{1,0:T(8,128)(2,1)S(1)} %fusion.11.order_ref, bf16[16,8192]{1,0:T(8,128)(2,1)S(1)} %transform.1.refs_0_, ...), custom_call_target="tpu_custom_call" | custom-call | tf_op jit(solution)/shard_map/gather_attend/pallas_call | solution.py:254
  78.4 1.2 %collective-permute-start.17 = (bf16[768,128]{1,0:T(8,128)(2,1)S(1)}, bf16[768,128]{1,0:T(8,128)(2,1)S(1)}, u32[]{:S(2)}, u32[]{:S(2)}) collective-permute-start(bf16[768,128]{1,0:T(8,128)(2,1)S(1)} %get-tuple-element.28), channel_id=1, source_target_pairs={{0,16},{16,0},{1,17},{17,1},{2,18},{18,2},{3,19},{19,3},{4,20},{20... | collective-permute-start | bytes 589832 | tf_op jit(solution)/shard_map/ppermute | solution.py:399
  79.6 7.7 %attend.1 = bf16[768,128]{1,0:T(8,128)(2,1)S(1)} custom-call(s32[1]{0:T(128)} %bitcast.core_ref, bf16[768,128]{1,0:T(8,128)(2,1)S(1)} %get-tuple-element.22.q_ref, bf16[128,128]{1,0:T(8,128)(2,1)S(1)} %fusion.11.order_ref, bf16[2,128,8192]{2,1,0:T(8,128)(2,1)S(1)} %get-tuple-element.27.kv_ref), custom_call_target="tpu_custom_call" | custom-call | tf_op jit(solution)/shard_map/attend/pallas_call | solution.py:278
  87.3 0.8 maximum_select_fusion
  (22 shorter events, 0.1 us)
Async XLA Ops:
  0.0 0.9 %copy-start.1 = (bf16[512,256]{1,0:T(8,128)(2,1)S(1)}, bf16[512,256]{1,0:T(8,128)(2,1)}, u32[]{:S(2)}) copy-start(bf16[512,256]{1,0:T(8,128)(2,1)} %keys_ref.1) | copy-start | bytes 786436
  1.0 0.9 %copy-start.2 = (bf16[512,256]{1,0:T(8,128)(2,1)S(1)}, bf16[512,256]{1,0:T(8,128)(2,1)}, u32[]{:S(2)}) copy-start(bf16[512,256]{1,0:T(8,128)(2,1)} %values_ref.1) | copy-start | bytes 786436
  2.0 4.5 %collective-permute-start = (bf16[512,256]{1,0:T(8,128)(2,1)S(1)}, bf16[512,256]{1,0:T(8,128)(2,1)S(1)}, u32[]{:S(2)}, u32[]{:S(2)}) collective-permute-start(bf16[512,256]{1,0:T(8,128)(2,1)S(1)} %get-tuple-element.18), channel_id=1, source_target_pairs={{0,1},{1,0},{2,3},{3,2},{4,5},{5,4},{6,7},{7,6},{8,9},{9,8},{10,11... | collective-permute-start | bytes 786440 | tf_op jit(solution)/shard_map/ppermute | solution.py:341
  7.5 24.5 %copy-start = (bf16[2,512,256]{2,1,0:T(8,128)(2,1)S(1)}, bf16[2,512,256]{2,1,0:T(8,128)(2,1)}, u32[]{:S(2)}) copy-start(bf16[2,512,256]{2,1,0:T(8,128)(2,1)} %constant.141.clone.middle_hbm) | copy-start | bytes 1572868
  7.5 24.5 %copy-start.3 = (f32[2,136,128]{2,1,0:T(8,128)S(1)}, f32[2,136,128]{2,1,0:T(8,128)}, u32[]{:S(2)}) copy-start(f32[2,136,128]{2,1,0:T(8,128)} %constant.142.clone.untwist_hbm) | copy-start | bytes 417796
  7.5 24.5 %copy-start.4 = (f32[2,136,128]{2,1,0:T(8,128)S(1)}, f32[2,136,128]{2,1,0:T(8,128)}, u32[]{:S(2)}) copy-start(f32[2,136,128]{2,1,0:T(8,128)} %constant.140.clone.twist_hbm) | copy-start | bytes 417796
  7.5 24.5 %copy-start.5 = (bf16[272,256]{1,0:T(8,128)(2,1)S(1)}, bf16[272,256]{1,0:T(8,128)(2,1)}, u32[]{:S(2)}) copy-start(bf16[272,256]{1,0:T(8,128)(2,1)} %constant.139.clone.first_hbm) | copy-start | bytes 417796
  7.5 24.5 %copy-start.6 = (bf16[2,128,256]{2,1,0:T(8,128)(2,1)S(1)}, bf16[2,128,256]{2,1,0:T(8,128)(2,1)}, u32[]{:S(2)}) copy-start(bf16[2,128,256]{2,1,0:T(8,128)(2,1)} %constant.143.clone.last_hbm) | copy-start | bytes 393220
  7.5 24.4 %all-to-all-start = ((bf16[16,16,1024]{2,1,0:T(8,128)(2,1)}), bf16[16,16,1024]{2,1,0:T(8,128)(2,1)S(1)}, u32[]{:S(2)}, u32[]{:S(2)}) async-start(bf16[16,16,1024]{2,1,0:T(8,128)(2,1)} %pack.1), calls=%async_computation | async-start | bytes 1048576 | tf_op jit(solution)/shard_map/all_to_all | solution.py:352
  20.1 9.9 %collective-permute-start.1 = (bf16[768,128]{1,0:T(8,128)(2,1)S(1)}, bf16[768,128]{1,0:T(8,128)(2,1)S(1)}, u32[]{:S(2)}, u32[]{:S(2)}) collective-permute-start(bf16[768,128]{1,0:T(8,128)(2,1)S(1)} %get-tuple-element.31), channel_id=1, source_target_pairs={{0,16},{16,0},{1,17},{17,1},{2,18},{18,2},{3,19},{19,3},{4,20},{20... | collective-permute-start | bytes 589832 | tf_op jit(solution)/shard_map/ppermute | solution.py:370
  35.7 5.1 %collective-permute-start.3 = (bf16[16,8192]{1,0:T(8,128)(2,1)S(1)}, bf16[16,8192]{1,0:T(8,128)(2,1)S(1)}, u32[]{:S(2)}, u32[]{:S(2)}) collective-permute-start(bf16[16,8192]{1,0:T(8,128)(2,1)S(1)} %transform.1.refs_0_), channel_id=1, source_target_pairs={{0,1},{1,0},{2,3},{3,2},{4,5},{5,4},{6,7},{7,6},{8,9},{9,8},{10,11... | collective-permute-start | bytes 786440 | tf_op jit(solution)/shard_map/ppermute | solution.py:302
  38.6 5.5 %collective-permute-start.2 = (bf16[16,8192]{1,0:T(8,128)(2,1)S(1)}, bf16[16,8192]{1,0:T(8,128)(2,1)S(1)}, u32[]{:S(2)}, u32[]{:S(2)}) collective-permute-start(bf16[16,8192]{1,0:T(8,128)(2,1)S(1)} %transform.1.refs_0_), channel_id=1, source_target_pairs={{0,2},{2,4},{4,6},{6,8},{8,10},{10,12},{12,14},{14,0},{1,15},{3,1}... | collective-permute-start | bytes 786440 | tf_op jit(solution)/shard_map/ppermute | solution.py:299
  40.8 6.4 %collective-permute-start.4 = (bf16[16,8192]{1,0:T(8,128)(2,1)S(1)}, bf16[16,8192]{1,0:T(8,128)(2,1)S(1)}, u32[]{:S(2)}, u32[]{:S(2)}) collective-permute-start(bf16[16,8192]{1,0:T(8,128)(2,1)S(1)} %collective-permute-done.3.refs_8_), channel_id=1, source_target_pairs={{0,2},{2,4},{4,6},{6,8},{8,10},{10,12},{12,14},{14,0},{1,15},{3,1}... | collective-permute-start | bytes 786440 | tf_op jit(solution)/shard_map/ppermute | solution.py:299
  44.1 6.4 %collective-permute-start.6 = (bf16[16,8192]{1,0:T(8,128)(2,1)S(1)}, bf16[16,8192]{1,0:T(8,128)(2,1)S(1)}, u32[]{:S(2)}, u32[]{:S(2)}) collective-permute-start(bf16[16,8192]{1,0:T(8,128)(2,1)S(1)} %collective-permute-done.2.refs_1_), channel_id=1, source_target_pairs={{0,2},{2,4},{4,6},{6,8},{8,10},{10,12},{12,14},{14,0},{1,15},{3,1}... | collective-permute-start | bytes 786440 | tf_op jit(solution)/shard_map/ppermute | solution.py:299
  47.2 6.9 %collective-permute-start.7 = (bf16[16,8192]{1,0:T(8,128)(2,1)S(1)}, bf16[16,8192]{1,0:T(8,128)(2,1)S(1)}, u32[]{:S(2)}, u32[]{:S(2)}) collective-permute-start(bf16[16,8192]{1,0:T(8,128)(2,1)S(1)} %collective-permute-done.4.refs_9_), channel_id=1, source_target_pairs={{0,2},{2,4},{4,6},{6,8},{8,10},{10,12},{12,14},{14,0},{1,15},{3,1}... | collective-permute-start | bytes 786440 | tf_op jit(solution)/shard_map/ppermute | solution.py:299
  50.5 6.4 %collective-permute-start.9 = (bf16[16,8192]{1,0:T(8,128)(2,1)S(1)}, bf16[16,8192]{1,0:T(8,128)(2,1)S(1)}, u32[]{:S(2)}, u32[]{:S(2)}) collective-permute-start(bf16[16,8192]{1,0:T(8,128)(2,1)S(1)} %collective-permute-done.6.refs_3_), channel_id=1, source_target_pairs={{0,2},{2,4},{4,6},{6,8},{8,10},{10,12},{12,14},{14,0},{1,15},{3,1}... | collective-permute-start | bytes 786440 | tf_op jit(solution)/shard_map/ppermute | solution.py:299
  53.7 7.8 %collective-permute-start.13 = (bf16[16,8192]{1,0:T(8,128)(2,1)S(1)}, bf16[16,8192]{1,0:T(8,128)(2,1)S(1)}, u32[]{:S(2)}, u32[]{:S(2)}) collective-permute-start(bf16[16,8192]{1,0:T(8,128)(2,1)S(1)} %collective-permute-done.2.refs_1_), channel_id=1, source_target_pairs={{0,1},{1,0},{2,3},{3,2},{4,5},{5,4},{6,7},{7,6},{8,9},{9,8},{10,11... | collective-permute-start | bytes 786440 | tf_op jit(solution)/shard_map/ppermute | solution.py:302
  53.9 7.7 %collective-permute-start.5 = (bf16[16,8192]{1,0:T(8,128)(2,1)S(1)}, bf16[16,8192]{1,0:T(8,128)(2,1)S(1)}, u32[]{:S(2)}, u32[]{:S(2)}) collective-permute-start(bf16[16,8192]{1,0:T(8,128)(2,1)S(1)} %collective-permute-done.4.refs_9_), channel_id=1, source_target_pairs={{0,1},{1,0},{2,3},{3,2},{4,5},{5,4},{6,7},{7,6},{8,9},{9,8},{10,11... | collective-permute-start | bytes 786440 | tf_op jit(solution)/shard_map/ppermute | solution.py:302
  54.2 7.8 %collective-permute-start.10 = (bf16[16,8192]{1,0:T(8,128)(2,1)S(1)}, bf16[16,8192]{1,0:T(8,128)(2,1)S(1)}, u32[]{:S(2)}, u32[]{:S(2)}) collective-permute-start(bf16[16,8192]{1,0:T(8,128)(2,1)S(1)} %collective-permute-done.7.refs_11_), channel_id=1, source_target_pairs={{0,2},{2,4},{4,6},{6,8},{8,10},{10,12},{12,14},{14,0},{1,15},{3,1}... | collective-permute-start | bytes 786440 | tf_op jit(solution)/shard_map/ppermute | solution.py:299
  57.0 7.3 %collective-permute-start.12 = (bf16[16,8192]{1,0:T(8,128)(2,1)S(1)}, bf16[16,8192]{1,0:T(8,128)(2,1)S(1)}, u32[]{:S(2)}, u32[]{:S(2)}) collective-permute-start(bf16[16,8192]{1,0:T(8,128)(2,1)S(1)} %collective-permute-done.9.refs_5_), channel_id=1, source_target_pairs={{0,2},{2,4},{4,6},{6,8},{8,10},{10,12},{12,14},{14,0},{1,15},{3,1}... | collective-permute-start | bytes 786440 | tf_op jit(solution)/shard_map/ppermute | solution.py:299
  60.1 9.1 %collective-permute-start.14 = (bf16[16,8192]{1,0:T(8,128)(2,1)S(1)}, bf16[16,8192]{1,0:T(8,128)(2,1)S(1)}, u32[]{:S(2)}, u32[]{:S(2)}) collective-permute-start(bf16[16,8192]{1,0:T(8,128)(2,1)S(1)} %collective-permute-done.6.refs_3_), channel_id=1, source_target_pairs={{0,1},{1,0},{2,3},{3,2},{4,5},{5,4},{6,7},{7,6},{8,9},{9,8},{10,11... | collective-permute-start | bytes 786440 | tf_op jit(solution)/shard_map/ppermute | solution.py:302
  61.5 7.7 %collective-permute-start.8 = (bf16[16,8192]{1,0:T(8,128)(2,1)S(1)}, bf16[16,8192]{1,0:T(8,128)(2,1)S(1)}, u32[]{:S(2)}, u32[]{:S(2)}) collective-permute-start(bf16[16,8192]{1,0:T(8,128)(2,1)S(1)} %collective-permute-done.7.refs_11_), channel_id=1, source_target_pairs={{0,1},{1,0},{2,3},{3,2},{4,5},{5,4},{6,7},{7,6},{8,9},{9,8},{10,11... | collective-permute-start | bytes 786440 | tf_op jit(solution)/shard_map/ppermute | solution.py:302
  61.6 7.6 %collective-permute-start.15 = (bf16[16,8192]{1,0:T(8,128)(2,1)S(1)}, bf16[16,8192]{1,0:T(8,128)(2,1)S(1)}, u32[]{:S(2)}, u32[]{:S(2)}) collective-permute-start(bf16[16,8192]{1,0:T(8,128)(2,1)S(1)} %collective-permute-done.9.refs_5_), channel_id=1, source_target_pairs={{0,1},{1,0},{2,3},{3,2},{4,5},{5,4},{6,7},{7,6},{8,9},{9,8},{10,11... | collective-permute-start | bytes 786440 | tf_op jit(solution)/shard_map/ppermute | solution.py:302
  62.0 7.2 %collective-permute-start.11 = (bf16[16,8192]{1,0:T(8,128)(2,1)S(1)}, bf16[16,8192]{1,0:T(8,128)(2,1)S(1)}, u32[]{:S(2)}, u32[]{:S(2)}) collective-permute-start(bf16[16,8192]{1,0:T(8,128)(2,1)S(1)} %collective-permute-done.10.refs_13_), channel_id=1, source_target_pairs={{0,1},{1,0},{2,3},{3,2},{4,5},{5,4},{6,7},{7,6},{8,9},{9,8},{10,11... | collective-permute-start | bytes 786440 | tf_op jit(solution)/shard_map/ppermute | solution.py:302
  64.3 5.9 %collective-permute-start.16 = (bf16[16,8192]{1,0:T(8,128)(2,1)S(1)}, bf16[16,8192]{1,0:T(8,128)(2,1)S(1)}, u32[]{:S(2)}, u32[]{:S(2)}) collective-permute-start(bf16[16,8192]{1,0:T(8,128)(2,1)S(1)} %collective-permute-done.12.refs_7_), channel_id=1, source_target_pairs={{0,1},{1,0},{2,3},{3,2},{4,5},{5,4},{6,7},{7,6},{8,9},{9,8},{10,11... | collective-permute-start | bytes 786440 | tf_op jit(solution)/shard_map/ppermute | solution.py:302
  78.4 8.9 %collective-permute-start.17 = (bf16[768,128]{1,0:T(8,128)(2,1)S(1)}, bf16[768,128]{1,0:T(8,128)(2,1)S(1)}, u32[]{:S(2)}, u32[]{:S(2)}) collective-permute-start(bf16[768,128]{1,0:T(8,128)(2,1)S(1)} %get-tuple-element.28), channel_id=1, source_target_pairs={{0,16},{16,0},{1,17},{17,1},{2,18},{18,2},{3,19},{19,3},{4,20},{20... | collective-permute-start | bytes 589832 | tf_op jit(solution)/shard_map/ppermute | solution.py:399

commit v3 on v2

--- a/solution.py
+++ b/solution.py
@@ -70,19 +70,6 @@
 
 def inverse_freq():
     return jnp.exp(jnp.arange(HALF).astype(F32) * (-2.0 * math.log(THETA) / HEAD))
-
-
-def choose_kernel(core_ref, keys_ref, values_ref, mine_ref, send_ref, sems):
-    def move(mine, send):
-        first = pltpu.make_async_copy(send, send_ref, sems.at[0])
-        second = pltpu.make_async_copy(mine, mine_ref, sems.at[1])
-        first.start()
-        second.start()
-        first.wait()
-        second.wait()
-
-    pl.when(core_ref[0] == 0)(lambda: move(keys_ref, values_ref))
-    pl.when(core_ref[0] != 0)(lambda: move(values_ref, keys_ref))
 
 
 def pack_kernel(core_ref, mine_ref, other_ref, out_ref):
@@ -328,16 +315,9 @@
     vmem = pl.BlockSpec(memory_space=pltpu.VMEM)
     smem = pl.BlockSpec(memory_space=pltpu.SMEM)
     hbm = pl.BlockSpec(memory_space=pltpu.HBM)
-    chosen = jax.ShapeDtypeStruct(keys.shape, BF16)
-    kept_tokens, send = pl.pallas_call(
-        choose_kernel,
-        in_specs=[smem, hbm, hbm],
-        out_specs=[vmem, vmem],
-        out_shape=[chosen, chosen],
-        scratch_shapes=[pltpu.SemaphoreType.DMA((2,))],
-        compiler_params=pltpu.CompilerParams(vmem_limit_bytes=16 * 1024 * 1024),
-        name="choose",
-    )(core_here, keys, values)
+    kept_tokens = jnp.where(core == 0, keys, values)
+    send = jnp.where(core == 0, values, keys)
+    kept_tokens, send = lax.optimization_barrier((kept_tokens, send))
     other = lax.ppermute(send, "core", SWAP)
     packed = pl.pallas_call(
         pack_kernel,

time: 88.4 us -> 87.5 us (0.990)
  local copies, waits for them, and re-layouts: 1.99 us -> 0.1 us
  waiting for transfers between devices: 12.1 us -> 13.1 us
    unnamed x14 -> x12, local copies, waits for them, and re-layouts: 1.92 us -> 0.03 us
    select_n x0 -> x1, other arithmetic: none -> 1.12 us  [on_device(): send = jnp.where(core == 0, values, keys)]
    ppermute x1, waiting for transfers between devices: 5.97 us -> 6.98 us  [on_device(): lax.ppermute(jnp.where(head == 0, turned[1], turned[0]), 'yhi', SWAP)]
    convert_element_type x1, other arithmetic: 1.05 us -> 0.05 us  [on_device(): wide = queries.astype(F32)]
  transfers between devices with their start and end apart: 19 -> 19, of which waited for: 7 -> 7; matrix products, arithmetic and copies ran while one was open for 6% -> 5% of each run, Pallas kernels for 9% -> 9%
where the time goes in v3:
time: 87.5 us; the launch traced here: 87.2 us
  starting transfers between devices  47.2 us (54%)
  Pallas kernels  20.7 us (24%)
  waiting for transfers between devices  13.1 us (15%)
  other arithmetic  5.63 us (6%)
    ppermute x7, starting transfers between devices, along(): return lax.ppermute(block, ('z', 'core'), onward)  18.1 us
    ppermute x8, starting transfers between devices, across(): return lax.ppermute(block, 'core', SWAP)  12.4 us
    all_to_all x1, starting transfers between devices, on_device(): received = lax.all_to_all(packed, ('yhi', 'z'), 0, 0, tiled=True)  9.33 us
    pallas_call x1, Pallas kernels, gather_attend(): pl.pallas_call(gather_attend_kernel, grid=(rows // ROW_BLOCK,), in_specs=...  8.19 us
    pallas_call x1, Pallas kernels, attend(): pl.pallas_call(attend_kernel, grid=(q.shape[0] // ROW_BLOCK,), in_specs=[...  7.7 us
    ppermute x1, waiting for transfers between devices, on_device(): lax.ppermute(jnp.where(head == 0, turned[1], turned[0]), 'yhi', SWAP)  6.98 us
    pallas_call x1, Pallas kernels, on_device(): pl.pallas_call(transform_kernel, in_specs=[vmem] * 3 + [hbm] * 5, out_spe...  3.76 us
    ppermute x1, starting transfers between devices, on_device(): other = lax.ppermute(send, 'core', SWAP)  3.33 us
  transfers between devices with their start and end apart: 19, of which 7 were waited for; matrix products, arithmetic and copies ran while one was open for 5% of the time, Pallas kernels for 9%

profile of v3, /device:TPU:1, one launch (start us, length us, event | category | flops | bytes accessed | tf_op | source)
XLA Modules:
  0.0 87.2 jit_solution(7271173504181695511)
XLA Ops:
  0.0 1.1 %broadcast_select_fusion = (bf16[512,256]{1,0:T(8,128)(2,1)S(1)}, bf16[512,256]{1,0:T(8,128)(2,1)S(1)}) fusion(bf16[512,256]{1,0:T(8,128)(2,1)} %param.10, bf16[512,256]{1,0:T(8,128)(2,1)} %param.9, pred[]{:T(512)S(6)} %eq.47), kind=kLoop, calls=%fused_computation.13 | loop fusion | flops 262144 | bytes 1048577 | tf_op jit(solution)/shard_map/jit(_where)/select_n | solution.py:319
  1.1 3.3 %collective-permute-start = (bf16[512,256]{1,0:T(8,128)(2,1)S(1)}, bf16[512,256]{1,0:T(8,128)(2,1)S(1)}, u32[]{:S(2)}, u32[]{:S(2)}) collective-permute-start(bf16[512,256]{1,0:T(8,128)(2,1)S(1)} %get-tuple-element.18), channel_id=1, source_target_pairs={{0,1},{1,0},{2,3},{3,2},{4,5},{5,4},{6,7},{7,6},{8,9},{9,8},{10,11... | collective-permute-start | bytes 786440 | tf_op jit(solution)/shard_map/ppermute | solution.py:321
  4.5 0.7 convert_element_type.30
  5.2 0.1 dynamic_slice.3
  5.3 0.4 collective-permute-done.other_ref
  5.6 1.0 %pack.1 = bf16[16,16,1024]{2,1,0:T(8,128)(2,1)} custom-call(s32[1]{0:T(128)} %bitcast.core_ref, bf16[512,256]{1,0:T(8,128)(2,1)S(1)} %get-tuple-element.17.mine_ref, bf16[512,256]{1,0:T(8,128)(2,1)S(1)} %collective-permute-done.other_ref), custom_call_target="tpu_custom_call" | custom-call | tf_op jit(solution)/shard_map/pack/pallas_call | solution.py:322
  6.6 0.0 copy-start.4
  6.7 9.3 %all-to-all-start = ((bf16[16,16,1024]{2,1,0:T(8,128)(2,1)}), bf16[16,16,1024]{2,1,0:T(8,128)(2,1)S(1)}, u32[]{:S(2)}, u32[]{:S(2)}) async-start(bf16[16,16,1024]{2,1,0:T(8,128)(2,1)} %pack.1), calls=%async_computation | async-start | bytes 1048576 | tf_op jit(solution)/shard_map/all_to_all | solution.py:332
  16.0 1.4 %multiply_cosine_fusion = (f32[768,64]{1,0:T(8,128)S(1)}, f32[768,64]{1,0:T(8,128)S(1)}) fusion(f32[64]{0:T(128)S(1)} %multiply_exponential_fusion, f32[768]{0:T(1024)S(1)} %convert_element_type.30), kind=kLoop, calls=%fused_computation.4 | loop fusion | flops 49152 | bytes 396544 | tf_op jit(solution)/shard_map/cos | solution.py:336
  17.4 0.1 convert_element_type.31
  17.5 0.4 subtract_convert_fusion
  17.9 0.3 convolution_convert_fusion
  18.3 3.0 %collective-permute-start.1 = (bf16[768,128]{1,0:T(8,128)(2,1)S(1)}, bf16[768,128]{1,0:T(8,128)(2,1)S(1)}, u32[]{:S(2)}, u32[]{:S(2)}) collective-permute-start(bf16[768,128]{1,0:T(8,128)(2,1)S(1)} %get-tuple-element.33), channel_id=1, source_target_pairs={{0,16},{16,0},{1,17},{17,1},{2,18},{18,2},{3,19},{19,3},{4,20},{20... | collective-permute-start | bytes 589832 | tf_op jit(solution)/shard_map/ppermute | solution.py:350
  21.2 1.0 %fusion.4 = (f32[8,8192]{1,0:T(8,128)S(1)}, f32[8,8192]{1,0:T(8,128)S(1)}) fusion(f32[8192]{0:T(1024)S(1)} %fusion.15, f32[8]{0:T(128)S(1)} %dynamic_slice.3, pred[]{:T(512)S(6)} %eq.47), kind=kLoop, calls=%fused_computation.12 | loop fusion | flops 196608 | bytes 557089 | tf_op jit(solution)/shard_map/jit(_where)/select_n | solution.py:356
  22.2 7.0 %collective-permute-done.1.q_ref = bf16[768,128]{1,0:T(8,128)(2,1)S(1)} collective-permute-done((bf16[768,128]{1,0:T(8,128)(2,1)S(1)}, bf16[768,128]{1,0:T(8,128)(2,1)S(1)}, u32[]{:S(2)}, u32[]{:S(2)}) %collective-permute-start.1) | collective-permute-done | bytes 196640 | tf_op jit(solution)/shard_map/ppermute | solution.py:350
  29.2 1.9 %all-to-all-done.x_ref = bf16[16,16,1024]{2,1,0:T(8,128)(2,1)S(1)} async-done(((bf16[16,16,1024]{2,1,0:T(8,128)(2,1)}), bf16[16,16,1024]{2,1,0:T(8,128)(2,1)S(1)}, u32[]{:S(2)}, u32[]{:S(2)}) %all-to-all-start) | async-done | bytes 524320 | tf_op jit(solution)/shard_map/all_to_all | solution.py:332
  31.1 3.8 %transform.1.refs_0_ = bf16[16,8192]{1,0:T(8,128)(2,1)S(1)} custom-call(bf16[16,16,1024]{2,1,0:T(8,128)(2,1)S(1)} %all-to-all-done.x_ref, f32[8,8192]{1,0:T(8,128)S(1)} %get-tuple-element.25.cos_ref, f32[8,8192]{1,0:T(8,128)S(1)} %get-tuple-element.26.sin_ref, bf16[272,256]{1,0:T(8,128)(2,1)S(1)} %copy-done.3, f32[2,136,128]{2,1,0:T(8,128)S(1)} %copy-done.2, ...), custom_call_target="tpu_custom_call" | custom-call | tf_op jit(solution)/shard_map/transform/pallas_call | solution.py:361
  34.9 2.9 %collective-permute-start.3 = (bf16[16,8192]{1,0:T(8,128)(2,1)S(1)}, bf16[16,8192]{1,0:T(8,128)(2,1)S(1)}, u32[]{:S(2)}, u32[]{:S(2)}) collective-permute-start(bf16[16,8192]{1,0:T(8,128)(2,1)S(1)} %transform.1.refs_0_), channel_id=1, source_target_pairs={{0,1},{1,0},{2,3},{3,2},{4,5},{5,4},{6,7},{7,6},{8,9},{9,8},{10,11... | collective-permute-start | bytes 786440 | tf_op jit(solution)/shard_map/ppermute | solution.py:289
  37.8 2.2 %collective-permute-start.2 = (bf16[16,8192]{1,0:T(8,128)(2,1)S(1)}, bf16[16,8192]{1,0:T(8,128)(2,1)S(1)}, u32[]{:S(2)}, u32[]{:S(2)}) collective-permute-start(bf16[16,8192]{1,0:T(8,128)(2,1)S(1)} %transform.1.refs_0_), channel_id=1, source_target_pairs={{0,2},{2,4},{4,6},{6,8},{8,10},{10,12},{12,14},{14,0},{1,15},{3,1}... | collective-permute-start | bytes 786440 | tf_op jit(solution)/shard_map/ppermute | solution.py:286
  39.9 0.0 collective-permute-done.3.refs_8_
  40.0 1.2 %collective-permute-start.4 = (bf16[16,8192]{1,0:T(8,128)(2,1)S(1)}, bf16[16,8192]{1,0:T(8,128)(2,1)S(1)}, u32[]{:S(2)}, u32[]{:S(2)}) collective-permute-start(bf16[16,8192]{1,0:T(8,128)(2,1)S(1)} %collective-permute-done.3.refs_8_), channel_id=1, source_target_pairs={{0,2},{2,4},{4,6},{6,8},{8,10},{10,12},{12,14},{14,0},{1,15},{3,1}... | collective-permute-start | bytes 786440 | tf_op jit(solution)/shard_map/ppermute | solution.py:286
  41.1 2.2 %collective-permute-done.2.refs_1_ = bf16[16,8192]{1,0:T(8,128)(2,1)S(1)} collective-permute-done((bf16[16,8192]{1,0:T(8,128)(2,1)S(1)}, bf16[16,8192]{1,0:T(8,128)(2,1)S(1)}, u32[]{:S(2)}, u32[]{:S(2)}) %collective-permute-start.2) | collective-permute-done | bytes 262176 | tf_op jit(solution)/shard_map/ppermute | solution.py:286
  43.3 3.1 %collective-permute-start.6 = (bf16[16,8192]{1,0:T(8,128)(2,1)S(1)}, bf16[16,8192]{1,0:T(8,128)(2,1)S(1)}, u32[]{:S(2)}, u32[]{:S(2)}) collective-permute-start(bf16[16,8192]{1,0:T(8,128)(2,1)S(1)} %collective-permute-done.2.refs_1_), channel_id=1, source_target_pairs={{0,2},{2,4},{4,6},{6,8},{8,10},{10,12},{12,14},{14,0},{1,15},{3,1}... | collective-permute-start | bytes 786440 | tf_op jit(solution)/shard_map/ppermute | solution.py:286
  46.4 0.0 collective-permute-done.4.refs_9_
  46.4 2.8 %collective-permute-start.7 = (bf16[16,8192]{1,0:T(8,128)(2,1)S(1)}, bf16[16,8192]{1,0:T(8,128)(2,1)S(1)}, u32[]{:S(2)}, u32[]{:S(2)}) collective-permute-start(bf16[16,8192]{1,0:T(8,128)(2,1)S(1)} %collective-permute-done.4.refs_9_), channel_id=1, source_target_pairs={{0,2},{2,4},{4,6},{6,8},{8,10},{10,12},{12,14},{14,0},{1,15},{3,1}... | collective-permute-start | bytes 786440 | tf_op jit(solution)/shard_map/ppermute | solution.py:286
  49.2 0.5 collective-permute-done.6.refs_3_
  49.7 3.1 %collective-permute-start.9 = (bf16[16,8192]{1,0:T(8,128)(2,1)S(1)}, bf16[16,8192]{1,0:T(8,128)(2,1)S(1)}, u32[]{:S(2)}, u32[]{:S(2)}) collective-permute-start(bf16[16,8192]{1,0:T(8,128)(2,1)S(1)} %collective-permute-done.6.refs_3_), channel_id=1, source_target_pairs={{0,2},{2,4},{4,6},{6,8},{8,10},{10,12},{12,14},{14,0},{1,15},{3,1}... | collective-permute-start | bytes 786440 | tf_op jit(solution)/shard_map/ppermute | solution.py:286
  52.8 0.2 collective-permute-start.13
  53.1 0.3 collective-permute-start.5
  53.3 0.0 collective-permute-done.7.refs_11_
  53.3 2.7 %collective-permute-start.10 = (bf16[16,8192]{1,0:T(8,128)(2,1)S(1)}, bf16[16,8192]{1,0:T(8,128)(2,1)S(1)}, u32[]{:S(2)}, u32[]{:S(2)}) collective-permute-start(bf16[16,8192]{1,0:T(8,128)(2,1)S(1)} %collective-permute-done.7.refs_11_), channel_id=1, source_target_pairs={{0,2},{2,4},{4,6},{6,8},{8,10},{10,12},{12,14},{14,0},{1,15},{3,1}... | collective-permute-start | bytes 786440 | tf_op jit(solution)/shard_map/ppermute | solution.py:286
  56.0 0.1 collective-permute-done.9.refs_5_
  56.1 3.1 %collective-permute-start.12 = (bf16[16,8192]{1,0:T(8,128)(2,1)S(1)}, bf16[16,8192]{1,0:T(8,128)(2,1)S(1)}, u32[]{:S(2)}, u32[]{:S(2)}) collective-permute-start(bf16[16,8192]{1,0:T(8,128)(2,1)S(1)} %collective-permute-done.9.refs_5_), channel_id=1, source_target_pairs={{0,2},{2,4},{4,6},{6,8},{8,10},{10,12},{12,14},{14,0},{1,15},{3,1}... | collective-permute-start | bytes 786440 | tf_op jit(solution)/shard_map/ppermute | solution.py:286
  59.2 1.4 %collective-permute-start.14 = (bf16[16,8192]{1,0:T(8,128)(2,1)S(1)}, bf16[16,8192]{1,0:T(8,128)(2,1)S(1)}, u32[]{:S(2)}, u32[]{:S(2)}) collective-permute-start(bf16[16,8192]{1,0:T(8,128)(2,1)S(1)} %collective-permute-done.6.refs_3_), channel_id=1, source_target_pairs={{0,1},{1,0},{2,3},{3,2},{4,5},{5,4},{6,7},{7,6},{8,9},{9,8},{10,11... | collective-permute-start | bytes 786440 | tf_op jit(solution)/shard_map/ppermute | solution.py:289
  60.6 0.0 collective-permute-done.13.refs_10_
  60.6 0.1 collective-permute-start.8
  60.7 0.0 collective-permute-done.5.refs_2_
  60.7 0.4 collective-permute-start.15
  61.2 2.3 %collective-permute-start.11 = (bf16[16,8192]{1,0:T(8,128)(2,1)S(1)}, bf16[16,8192]{1,0:T(8,128)(2,1)S(1)}, u32[]{:S(2)}, u32[]{:S(2)}) collective-permute-start(bf16[16,8192]{1,0:T(8,128)(2,1)S(1)} %collective-permute-done.10.refs_13_), channel_id=1, source_target_pairs={{0,1},{1,0},{2,3},{3,2},{4,5},{5,4},{6,7},{7,6},{8,9},{9,8},{10,11... | collective-permute-start | bytes 786440 | tf_op jit(solution)/shard_map/ppermute | solution.py:289
  63.4 4.8 %collective-permute-start.16 = (bf16[16,8192]{1,0:T(8,128)(2,1)S(1)}, bf16[16,8192]{1,0:T(8,128)(2,1)S(1)}, u32[]{:S(2)}, u32[]{:S(2)}) collective-permute-start(bf16[16,8192]{1,0:T(8,128)(2,1)S(1)} %collective-permute-done.12.refs_7_), channel_id=1, source_target_pairs={{0,1},{1,0},{2,3},{3,2},{4,5},{5,4},{6,7},{7,6},{8,9},{9,8},{10,11... | collective-permute-start | bytes 786440 | tf_op jit(solution)/shard_map/ppermute | solution.py:289
  68.2 0.1 fusion.11.order_ref
  68.3 0.0 collective-permute-done.8.refs_4_
  68.3 1.0 %collective-permute-done.16.refs_15_ = bf16[16,8192]{1,0:T(8,128)(2,1)S(1)} collective-permute-done((bf16[16,8192]{1,0:T(8,128)(2,1)S(1)}, bf16[16,8192]{1,0:T(8,128)(2,1)S(1)}, u32[]{:S(2)}, u32[]{:S(2)}) %collective-permute-start.16) | collective-permute-done | bytes 262176 | tf_op jit(solution)/shard_map/ppermute | solution.py:289
  69.4 8.2 %gather_attend.1 = (bf16[768,128]{1,0:T(8,128)(2,1)S(1)}, bf16[2,128,8192]{2,1,0:T(8,128)(2,1)S(1)}) custom-call(s32[1]{0:T(128)} %bitcast.core_ref, bf16[768,128]{1,0:T(8,128)(2,1)S(1)} %collective-permute-done.1.q_ref, bf16[128,128]{1,0:T(8,128)(2,1)S(1)} %fusion.11.order_ref, bf16[16,8192]{1,0:T(8,128)(2,1)S(1)} %transform.1.refs_0_, ...), custom_call_target="tpu_custom_call" | custom-call | tf_op jit(solution)/shard_map/gather_attend/pallas_call | solution.py:241
  77.6 1.1 %collective-permute-start.17 = (bf16[768,128]{1,0:T(8,128)(2,1)S(1)}, bf16[768,128]{1,0:T(8,128)(2,1)S(1)}, u32[]{:S(2)}, u32[]{:S(2)}) collective-permute-start(bf16[768,128]{1,0:T(8,128)(2,1)S(1)} %get-tuple-element.28), channel_id=1, source_target_pairs={{0,16},{16,0},{1,17},{17,1},{2,18},{18,2},{3,19},{19,3},{4,20},{20... | collective-permute-start | bytes 589832 | tf_op jit(solution)/shard_map/ppermute | solution.py:379
  78.7 7.7 %attend.1 = bf16[768,128]{1,0:T(8,128)(2,1)S(1)} custom-call(s32[1]{0:T(128)} %bitcast.core_ref, bf16[768,128]{1,0:T(8,128)(2,1)S(1)} %get-tuple-element.22.q_ref, bf16[128,128]{1,0:T(8,128)(2,1)S(1)} %fusion.11.order_ref, bf16[2,128,8192]{2,1,0:T(8,128)(2,1)S(1)} %get-tuple-element.27.kv_ref), custom_call_target="tpu_custom_call" | custom-call | tf_op jit(solution)/shard_map/attend/pallas_call | solution.py:265
  86.4 0.0 collective-permute-done.17
  86.4 0.8 maximum_select_fusion
  (20 shorter events, 0.1 us)
Async XLA Ops:
  0.0 17.4 %copy-start.5 = (bf16[2,768,128]{2,1,0:T(8,128)(2,1)S(1)}, bf16[2,768,128]{2,1,0:T(8,128)(2,1)}, u32[]{:S(2)}) copy-start(bf16[2,768,128]{2,1,0:T(8,128)(2,1)} %param.11) | copy-start | bytes 1179652
  1.1 4.5 %collective-permute-start = (bf16[512,256]{1,0:T(8,128)(2,1)S(1)}, bf16[512,256]{1,0:T(8,128)(2,1)S(1)}, u32[]{:S(2)}, u32[]{:S(2)}) collective-permute-start(bf16[512,256]{1,0:T(8,128)(2,1)S(1)} %get-tuple-element.18), channel_id=1, source_target_pairs={{0,1},{1,0},{2,3},{3,2},{4,5},{5,4},{6,7},{7,6},{8,9},{9,8},{10,11... | collective-permute-start | bytes 786440 | tf_op jit(solution)/shard_map/ppermute | solution.py:321
  6.6 24.5 %copy-start = (bf16[2,512,256]{2,1,0:T(8,128)(2,1)S(1)}, bf16[2,512,256]{2,1,0:T(8,128)(2,1)}, u32[]{:S(2)}) copy-start(bf16[2,512,256]{2,1,0:T(8,128)(2,1)} %constant.141.clone.middle_hbm) | copy-start | bytes 1572868
  6.6 24.5 %copy-start.1 = (f32[2,136,128]{2,1,0:T(8,128)S(1)}, f32[2,136,128]{2,1,0:T(8,128)}, u32[]{:S(2)}) copy-start(f32[2,136,128]{2,1,0:T(8,128)} %constant.142.clone.untwist_hbm) | copy-start | bytes 417796
  6.6 24.5 %copy-start.2 = (f32[2,136,128]{2,1,0:T(8,128)S(1)}, f32[2,136,128]{2,1,0:T(8,128)}, u32[]{:S(2)}) copy-start(f32[2,136,128]{2,1,0:T(8,128)} %constant.140.clone.twist_hbm) | copy-start | bytes 417796
  6.6 24.5 %copy-start.3 = (bf16[272,256]{1,0:T(8,128)(2,1)S(1)}, bf16[272,256]{1,0:T(8,128)(2,1)}, u32[]{:S(2)}) copy-start(bf16[272,256]{1,0:T(8,128)(2,1)} %constant.139.clone.first_hbm) | copy-start | bytes 417796
  6.6 24.5 %copy-start.4 = (bf16[2,128,256]{2,1,0:T(8,128)(2,1)S(1)}, bf16[2,128,256]{2,1,0:T(8,128)(2,1)}, u32[]{:S(2)}) copy-start(bf16[2,128,256]{2,1,0:T(8,128)(2,1)} %constant.143.clone.last_hbm) | copy-start | bytes 393220
  6.7 24.4 %all-to-all-start = ((bf16[16,16,1024]{2,1,0:T(8,128)(2,1)}), bf16[16,16,1024]{2,1,0:T(8,128)(2,1)S(1)}, u32[]{:S(2)}, u32[]{:S(2)}) async-start(bf16[16,16,1024]{2,1,0:T(8,128)(2,1)} %pack.1), calls=%async_computation | async-start | bytes 1048576 | tf_op jit(solution)/shard_map/all_to_all | solution.py:332
  18.3 10.9 %collective-permute-start.1 = (bf16[768,128]{1,0:T(8,128)(2,1)S(1)}, bf16[768,128]{1,0:T(8,128)(2,1)S(1)}, u32[]{:S(2)}, u32[]{:S(2)}) collective-permute-start(bf16[768,128]{1,0:T(8,128)(2,1)S(1)} %get-tuple-element.33), channel_id=1, source_target_pairs={{0,16},{16,0},{1,17},{17,1},{2,18},{18,2},{3,19},{19,3},{4,20},{20... | collective-permute-start | bytes 589832 | tf_op jit(solution)/shard_map/ppermute | solution.py:350
  34.9 5.1 %collective-permute-start.3 = (bf16[16,8192]{1,0:T(8,128)(2,1)S(1)}, bf16[16,8192]{1,0:T(8,128)(2,1)S(1)}, u32[]{:S(2)}, u32[]{:S(2)}) collective-permute-start(bf16[16,8192]{1,0:T(8,128)(2,1)S(1)} %transform.1.refs_0_), channel_id=1, source_target_pairs={{0,1},{1,0},{2,3},{3,2},{4,5},{5,4},{6,7},{7,6},{8,9},{9,8},{10,11... | collective-permute-start | bytes 786440 | tf_op jit(solution)/shard_map/ppermute | solution.py:289
  37.8 5.5 %collective-permute-start.2 = (bf16[16,8192]{1,0:T(8,128)(2,1)S(1)}, bf16[16,8192]{1,0:T(8,128)(2,1)S(1)}, u32[]{:S(2)}, u32[]{:S(2)}) collective-permute-start(bf16[16,8192]{1,0:T(8,128)(2,1)S(1)} %transform.1.refs_0_), channel_id=1, source_target_pairs={{0,2},{2,4},{4,6},{6,8},{8,10},{10,12},{12,14},{14,0},{1,15},{3,1}... | collective-permute-start | bytes 786440 | tf_op jit(solution)/shard_map/ppermute | solution.py:286
  40.0 6.4 %collective-permute-start.4 = (bf16[16,8192]{1,0:T(8,128)(2,1)S(1)}, bf16[16,8192]{1,0:T(8,128)(2,1)S(1)}, u32[]{:S(2)}, u32[]{:S(2)}) collective-permute-start(bf16[16,8192]{1,0:T(8,128)(2,1)S(1)} %collective-permute-done.3.refs_8_), channel_id=1, source_target_pairs={{0,2},{2,4},{4,6},{6,8},{8,10},{10,12},{12,14},{14,0},{1,15},{3,1}... | collective-permute-start | bytes 786440 | tf_op jit(solution)/shard_map/ppermute | solution.py:286
  43.3 6.4 %collective-permute-start.6 = (bf16[16,8192]{1,0:T(8,128)(2,1)S(1)}, bf16[16,8192]{1,0:T(8,128)(2,1)S(1)}, u32[]{:S(2)}, u32[]{:S(2)}) collective-permute-start(bf16[16,8192]{1,0:T(8,128)(2,1)S(1)} %collective-permute-done.2.refs_1_), channel_id=1, source_target_pairs={{0,2},{2,4},{4,6},{6,8},{8,10},{10,12},{12,14},{14,0},{1,15},{3,1}... | collective-permute-start | bytes 786440 | tf_op jit(solution)/shard_map/ppermute | solution.py:286
  46.4 6.9 %collective-permute-start.7 = (bf16[16,8192]{1,0:T(8,128)(2,1)S(1)}, bf16[16,8192]{1,0:T(8,128)(2,1)S(1)}, u32[]{:S(2)}, u32[]{:S(2)}) collective-permute-start(bf16[16,8192]{1,0:T(8,128)(2,1)S(1)} %collective-permute-done.4.refs_9_), channel_id=1, source_target_pairs={{0,2},{2,4},{4,6},{6,8},{8,10},{10,12},{12,14},{14,0},{1,15},{3,1}... | collective-permute-start | bytes 786440 | tf_op jit(solution)/shard_map/ppermute | solution.py:286
  49.7 6.4 %collective-permute-start.9 = (bf16[16,8192]{1,0:T(8,128)(2,1)S(1)}, bf16[16,8192]{1,0:T(8,128)(2,1)S(1)}, u32[]{:S(2)}, u32[]{:S(2)}) collective-permute-start(bf16[16,8192]{1,0:T(8,128)(2,1)S(1)} %collective-permute-done.6.refs_3_), channel_id=1, source_target_pairs={{0,2},{2,4},{4,6},{6,8},{8,10},{10,12},{12,14},{14,0},{1,15},{3,1}... | collective-permute-start | bytes 786440 | tf_op jit(solution)/shard_map/ppermute | solution.py:286
  52.8 7.8 %collective-permute-start.13 = (bf16[16,8192]{1,0:T(8,128)(2,1)S(1)}, bf16[16,8192]{1,0:T(8,128)(2,1)S(1)}, u32[]{:S(2)}, u32[]{:S(2)}) collective-permute-start(bf16[16,8192]{1,0:T(8,128)(2,1)S(1)} %collective-permute-done.2.refs_1_), channel_id=1, source_target_pairs={{0,1},{1,0},{2,3},{3,2},{4,5},{5,4},{6,7},{7,6},{8,9},{9,8},{10,11... | collective-permute-start | bytes 786440 | tf_op jit(solution)/shard_map/ppermute | solution.py:289
  53.1 7.7 %collective-permute-start.5 = (bf16[16,8192]{1,0:T(8,128)(2,1)S(1)}, bf16[16,8192]{1,0:T(8,128)(2,1)S(1)}, u32[]{:S(2)}, u32[]{:S(2)}) collective-permute-start(bf16[16,8192]{1,0:T(8,128)(2,1)S(1)} %collective-permute-done.4.refs_9_), channel_id=1, source_target_pairs={{0,1},{1,0},{2,3},{3,2},{4,5},{5,4},{6,7},{7,6},{8,9},{9,8},{10,11... | collective-permute-start | bytes 786440 | tf_op jit(solution)/shard_map/ppermute | solution.py:289
  53.3 7.8 %collective-permute-start.10 = (bf16[16,8192]{1,0:T(8,128)(2,1)S(1)}, bf16[16,8192]{1,0:T(8,128)(2,1)S(1)}, u32[]{:S(2)}, u32[]{:S(2)}) collective-permute-start(bf16[16,8192]{1,0:T(8,128)(2,1)S(1)} %collective-permute-done.7.refs_11_), channel_id=1, source_target_pairs={{0,2},{2,4},{4,6},{6,8},{8,10},{10,12},{12,14},{14,0},{1,15},{3,1}... | collective-permute-start | bytes 786440 | tf_op jit(solution)/shard_map/ppermute | solution.py:286
  56.1 7.3 %collective-permute-start.12 = (bf16[16,8192]{1,0:T(8,128)(2,1)S(1)}, bf16[16,8192]{1,0:T(8,128)(2,1)S(1)}, u32[]{:S(2)}, u32[]{:S(2)}) collective-permute-start(bf16[16,8192]{1,0:T(8,128)(2,1)S(1)} %collective-permute-done.9.refs_5_), channel_id=1, source_target_pairs={{0,2},{2,4},{4,6},{6,8},{8,10},{10,12},{12,14},{14,0},{1,15},{3,1}... | collective-permute-start | bytes 786440 | tf_op jit(solution)/shard_map/ppermute | solution.py:286
  59.2 9.1 %collective-permute-start.14 = (bf16[16,8192]{1,0:T(8,128)(2,1)S(1)}, bf16[16,8192]{1,0:T(8,128)(2,1)S(1)}, u32[]{:S(2)}, u32[]{:S(2)}) collective-permute-start(bf16[16,8192]{1,0:T(8,128)(2,1)S(1)} %collective-permute-done.6.refs_3_), channel_id=1, source_target_pairs={{0,1},{1,0},{2,3},{3,2},{4,5},{5,4},{6,7},{7,6},{8,9},{9,8},{10,11... | collective-permute-start | bytes 786440 | tf_op jit(solution)/shard_map/ppermute | solution.py:289
  60.6 7.7 %collective-permute-start.8 = (bf16[16,8192]{1,0:T(8,128)(2,1)S(1)}, bf16[16,8192]{1,0:T(8,128)(2,1)S(1)}, u32[]{:S(2)}, u32[]{:S(2)}) collective-permute-start(bf16[16,8192]{1,0:T(8,128)(2,1)S(1)} %collective-permute-done.7.refs_11_), channel_id=1, source_target_pairs={{0,1},{1,0},{2,3},{3,2},{4,5},{5,4},{6,7},{7,6},{8,9},{9,8},{10,11... | collective-permute-start | bytes 786440 | tf_op jit(solution)/shard_map/ppermute | solution.py:289
  60.7 7.6 %collective-permute-start.15 = (bf16[16,8192]{1,0:T(8,128)(2,1)S(1)}, bf16[16,8192]{1,0:T(8,128)(2,1)S(1)}, u32[]{:S(2)}, u32[]{:S(2)}) collective-permute-start(bf16[16,8192]{1,0:T(8,128)(2,1)S(1)} %collective-permute-done.9.refs_5_), channel_id=1, source_target_pairs={{0,1},{1,0},{2,3},{3,2},{4,5},{5,4},{6,7},{7,6},{8,9},{9,8},{10,11... | collective-permute-start | bytes 786440 | tf_op jit(solution)/shard_map/ppermute | solution.py:289
  61.2 7.2 %collective-permute-start.11 = (bf16[16,8192]{1,0:T(8,128)(2,1)S(1)}, bf16[16,8192]{1,0:T(8,128)(2,1)S(1)}, u32[]{:S(2)}, u32[]{:S(2)}) collective-permute-start(bf16[16,8192]{1,0:T(8,128)(2,1)S(1)} %collective-permute-done.10.refs_13_), channel_id=1, source_target_pairs={{0,1},{1,0},{2,3},{3,2},{4,5},{5,4},{6,7},{7,6},{8,9},{9,8},{10,11... | collective-permute-start | bytes 786440 | tf_op jit(solution)/shard_map/ppermute | solution.py:289
  63.4 5.9 %collective-permute-start.16 = (bf16[16,8192]{1,0:T(8,128)(2,1)S(1)}, bf16[16,8192]{1,0:T(8,128)(2,1)S(1)}, u32[]{:S(2)}, u32[]{:S(2)}) collective-permute-start(bf16[16,8192]{1,0:T(8,128)(2,1)S(1)} %collective-permute-done.12.refs_7_), channel_id=1, source_target_pairs={{0,1},{1,0},{2,3},{3,2},{4,5},{5,4},{6,7},{7,6},{8,9},{9,8},{10,11... | collective-permute-start | bytes 786440 | tf_op jit(solution)/shard_map/ppermute | solution.py:289
  77.6 8.9 %collective-permute-start.17 = (bf16[768,128]{1,0:T(8,128)(2,1)S(1)}, bf16[768,128]{1,0:T(8,128)(2,1)S(1)}, u32[]{:S(2)}, u32[]{:S(2)}) collective-permute-start(bf16[768,128]{1,0:T(8,128)(2,1)S(1)} %get-tuple-element.28), channel_id=1, source_target_pairs={{0,16},{16,0},{1,17},{17,1},{2,18},{18,2},{3,19},{19,3},{4,20},{20... | collective-permute-start | bytes 589832 | tf_op jit(solution)/shard_map/ppermute | solution.py:379

commit v4 on v3

--- a/solution.py
+++ b/solution.py
@@ -152,7 +152,8 @@
         [jnp.concatenate(z_real, axis=1), jnp.concatenate(z_imag, axis=1)], axis=0
     )
     high, low = halves(z)
-    y = dot(last_ref[0], high) + dot(last_ref[0], low) + dot(last_ref[1], high)
+    both = dot(jnp.concatenate([last_ref[0], last_ref[1]], axis=0), high)
+    y = both[:BASE] + both[BASE:] + dot(last_ref[0], low)
     rows_ref[...] = y.T
     steps = rows_ref.shape[0] // columns
     for step in range(steps):
@@ -206,22 +207,16 @@
 
 
 def gather_attend_kernel(core_ref, q_ref, order_ref, *refs):
-    *blocks, out_ref, kv_ref, sems = refs
+    *blocks, out_ref, kv_ref = refs
     half = len(blocks) // 2
     columns, run = blocks[0].shape
 
     @pl.when(pl.program_id(0) == 0)
     def _():
-        copies = []
         for i, block in enumerate(blocks):
             which, at = divmod(i, half)
             row, chunk = divmod(at, CHUNKS)
-            target = kv_ref.at[which, pl.ds(row * columns, columns), pl.ds(chunk * run, run)]
-            copies.append(pltpu.make_async_copy(block, target, sems.at[i]))
-        for copy in copies:
-            copy.start()
-        for copy in copies:
-            copy.wait()
+            kv_ref[which, pl.ds(row * columns, columns), pl.ds(chunk * run, run)] = block[...]
 
     out_ref[...] = attend_rows(
         q_ref[...], kv_ref, core_ref[0], order_ref[...], block=TOKEN_BLOCK, scale=SCALE
@@ -246,7 +241,7 @@
             pl.BlockSpec((ROW_BLOCK, HEAD), lambda i: (i, 0)),
             pl.BlockSpec(order.shape, lambda i: (0, 0)),
         ]
-        + [pl.BlockSpec(memory_space=pl.ANY)] * len(blocks),
+        + [pl.BlockSpec(memory_space=pltpu.VMEM)] * len(blocks),
         out_specs=[
             pl.BlockSpec((ROW_BLOCK, HEAD), lambda i: (i, 0)),
             pl.BlockSpec(memory_space=pltpu.VMEM),
@@ -255,7 +250,6 @@
             jax.ShapeDtypeStruct(q.shape, BF16),
             jax.ShapeDtypeStruct(kv_shape, BF16),
         ],
-        scratch_shapes=[pltpu.SemaphoreType.DMA((len(blocks),))],
         compiler_params=pltpu.CompilerParams(vmem_limit_bytes=32 * 1024 * 1024),
         name="gather_attend",
     )(core, q, order, *blocks)

time: 87.5 us -> 87.1 us (level)
  no operation moved by 1% of the time
where the time goes in v4:
time: 87.1 us; the launch traced here: 86.9 us
  starting transfers between devices  47.2 us (54%)
  Pallas kernels  20.3 us (23%)
  waiting for transfers between devices  13.1 us (15%)
  other arithmetic  5.63 us (6%)
    ppermute x7, starting transfers between devices, along(): return lax.ppermute(block, ('z', 'core'), onward)  18.1 us
    ppermute x8, starting transfers between devices, across(): return lax.ppermute(block, 'core', SWAP)  12.4 us
    all_to_all x1, starting transfers between devices, on_device(): received = lax.all_to_all(packed, ('yhi', 'z'), 0, 0, tiled=True)  9.33 us
    pallas_call x1, Pallas kernels, gather_attend(): pl.pallas_call(gather_attend_kernel, grid=(rows // ROW_BLOCK,), in_specs=...  7.98 us
    pallas_call x1, Pallas kernels, attend(): pl.pallas_call(attend_kernel, grid=(q.shape[0] // ROW_BLOCK,), in_specs=[...  7.71 us
    ppermute x1, waiting for transfers between devices, on_device(): lax.ppermute(jnp.where(head == 0, turned[1], turned[0]), 'yhi', SWAP)  6.98 us
    pallas_call x1, Pallas kernels, on_device(): pl.pallas_call(transform_kernel, in_specs=[vmem] * 3 + [hbm] * 5, out_spe...  3.64 us
    ppermute x1, starting transfers between devices, on_device(): other = lax.ppermute(send, 'core', SWAP)  3.33 us
  transfers between devices with their start and end apart: 19, of which 7 were waited for; matrix products, arithmetic and copies ran while one was open for 5% of the time, Pallas kernels for 9%

profile of v4, /device:TPU:1, one launch (start us, length us, event | category | flops | bytes accessed | tf_op | source)
XLA Modules:
  0.0 86.9 jit_solution(5314881311887813203)
XLA Ops:
  0.0 1.1 %broadcast_select_fusion = (bf16[512,256]{1,0:T(8,128)(2,1)S(1)}, bf16[512,256]{1,0:T(8,128)(2,1)S(1)}) fusion(bf16[512,256]{1,0:T(8,128)(2,1)} %param.10, bf16[512,256]{1,0:T(8,128)(2,1)} %param.9, pred[]{:T(512)S(6)} %eq.47), kind=kLoop, calls=%fused_computation.13 | loop fusion | flops 262144 | bytes 1048577 | tf_op jit(solution)/shard_map/jit(_where)/select_n | solution.py:313
  1.1 3.3 %collective-permute-start = (bf16[512,256]{1,0:T(8,128)(2,1)S(1)}, bf16[512,256]{1,0:T(8,128)(2,1)S(1)}, u32[]{:S(2)}, u32[]{:S(2)}) collective-permute-start(bf16[512,256]{1,0:T(8,128)(2,1)S(1)} %get-tuple-element.18), channel_id=1, source_target_pairs={{0,1},{1,0},{2,3},{3,2},{4,5},{5,4},{6,7},{7,6},{8,9},{9,8},{10,11... | collective-permute-start | bytes 786440 | tf_op jit(solution)/shard_map/ppermute | solution.py:315
  4.5 0.7 convert_element_type.30
  5.2 0.1 dynamic_slice.3
  5.3 0.4 collective-permute-done.other_ref
  5.6 1.0 %pack.1 = bf16[16,16,1024]{2,1,0:T(8,128)(2,1)} custom-call(s32[1]{0:T(128)} %bitcast.core_ref, bf16[512,256]{1,0:T(8,128)(2,1)S(1)} %get-tuple-element.17.mine_ref, bf16[512,256]{1,0:T(8,128)(2,1)S(1)} %collective-permute-done.other_ref), custom_call_target="tpu_custom_call" | custom-call | tf_op jit(solution)/shard_map/pack/pallas_call | solution.py:316
  6.6 0.0 copy-start.4
  6.7 9.3 %all-to-all-start = ((bf16[16,16,1024]{2,1,0:T(8,128)(2,1)}), bf16[16,16,1024]{2,1,0:T(8,128)(2,1)S(1)}, u32[]{:S(2)}, u32[]{:S(2)}) async-start(bf16[16,16,1024]{2,1,0:T(8,128)(2,1)} %pack.1), calls=%async_computation | async-start | bytes 1048576 | tf_op jit(solution)/shard_map/all_to_all | solution.py:326
  16.0 1.4 %multiply_cosine_fusion = (f32[768,64]{1,0:T(8,128)S(1)}, f32[768,64]{1,0:T(8,128)S(1)}) fusion(f32[64]{0:T(128)S(1)} %multiply_exponential_fusion, f32[768]{0:T(1024)S(1)} %convert_element_type.30), kind=kLoop, calls=%fused_computation.4 | loop fusion | flops 49152 | bytes 396544 | tf_op jit(solution)/shard_map/cos | solution.py:330
  17.4 0.1 convert_element_type.31
  17.5 0.4 subtract_convert_fusion
  17.9 0.3 convolution_convert_fusion
  18.3 3.0 %collective-permute-start.1 = (bf16[768,128]{1,0:T(8,128)(2,1)S(1)}, bf16[768,128]{1,0:T(8,128)(2,1)S(1)}, u32[]{:S(2)}, u32[]{:S(2)}) collective-permute-start(bf16[768,128]{1,0:T(8,128)(2,1)S(1)} %get-tuple-element.33), channel_id=1, source_target_pairs={{0,16},{16,0},{1,17},{17,1},{2,18},{18,2},{3,19},{19,3},{4,20},{20... | collective-permute-start | bytes 589832 | tf_op jit(solution)/shard_map/ppermute | solution.py:344
  21.2 1.0 %fusion.4 = (f32[8,8192]{1,0:T(8,128)S(1)}, f32[8,8192]{1,0:T(8,128)S(1)}) fusion(f32[8192]{0:T(1024)S(1)} %fusion.15, f32[8]{0:T(128)S(1)} %dynamic_slice.3, pred[]{:T(512)S(6)} %eq.47), kind=kLoop, calls=%fused_computation.12 | loop fusion | flops 196608 | bytes 557089 | tf_op jit(solution)/shard_map/jit(_where)/select_n | solution.py:350
  22.2 7.0 %collective-permute-done.1.q_ref = bf16[768,128]{1,0:T(8,128)(2,1)S(1)} collective-permute-done((bf16[768,128]{1,0:T(8,128)(2,1)S(1)}, bf16[768,128]{1,0:T(8,128)(2,1)S(1)}, u32[]{:S(2)}, u32[]{:S(2)}) %collective-permute-start.1) | collective-permute-done | bytes 196640 | tf_op jit(solution)/shard_map/ppermute | solution.py:344
  29.2 1.9 %all-to-all-done.x_ref = bf16[16,16,1024]{2,1,0:T(8,128)(2,1)S(1)} async-done(((bf16[16,16,1024]{2,1,0:T(8,128)(2,1)}), bf16[16,16,1024]{2,1,0:T(8,128)(2,1)S(1)}, u32[]{:S(2)}, u32[]{:S(2)}) %all-to-all-start) | async-done | bytes 524320 | tf_op jit(solution)/shard_map/all_to_all | solution.py:326
  31.1 3.6 %transform.1.refs_0_ = bf16[16,8192]{1,0:T(8,128)(2,1)S(1)} custom-call(bf16[16,16,1024]{2,1,0:T(8,128)(2,1)S(1)} %all-to-all-done.x_ref, f32[8,8192]{1,0:T(8,128)S(1)} %get-tuple-element.25.cos_ref, f32[8,8192]{1,0:T(8,128)S(1)} %get-tuple-element.26.sin_ref, bf16[272,256]{1,0:T(8,128)(2,1)S(1)} %copy-done.3, f32[2,136,128]{2,1,0:T(8,128)S(1)} %copy-done.2, ...), custom_call_target="tpu_custom_call" | custom-call | tf_op jit(solution)/shard_map/transform/pallas_call | solution.py:355
  34.8 2.9 %collective-permute-start.3 = (bf16[16,8192]{1,0:T(8,128)(2,1)S(1)}, bf16[16,8192]{1,0:T(8,128)(2,1)S(1)}, u32[]{:S(2)}, u32[]{:S(2)}) collective-permute-start(bf16[16,8192]{1,0:T(8,128)(2,1)S(1)} %transform.1.refs_0_), channel_id=1, source_target_pairs={{0,1},{1,0},{2,3},{3,2},{4,5},{5,4},{6,7},{7,6},{8,9},{9,8},{10,11... | collective-permute-start | bytes 786440 | tf_op jit(solution)/shard_map/ppermute | solution.py:283
  37.7 2.2 %collective-permute-start.2 = (bf16[16,8192]{1,0:T(8,128)(2,1)S(1)}, bf16[16,8192]{1,0:T(8,128)(2,1)S(1)}, u32[]{:S(2)}, u32[]{:S(2)}) collective-permute-start(bf16[16,8192]{1,0:T(8,128)(2,1)S(1)} %transform.1.refs_0_), channel_id=1, source_target_pairs={{0,2},{2,4},{4,6},{6,8},{8,10},{10,12},{12,14},{14,0},{1,15},{3,1}... | collective-permute-start | bytes 786440 | tf_op jit(solution)/shard_map/ppermute | solution.py:280
  39.8 0.0 collective-permute-done.3.refs_8_
  39.8 1.2 %collective-permute-start.4 = (bf16[16,8192]{1,0:T(8,128)(2,1)S(1)}, bf16[16,8192]{1,0:T(8,128)(2,1)S(1)}, u32[]{:S(2)}, u32[]{:S(2)}) collective-permute-start(bf16[16,8192]{1,0:T(8,128)(2,1)S(1)} %collective-permute-done.3.refs_8_), channel_id=1, source_target_pairs={{0,2},{2,4},{4,6},{6,8},{8,10},{10,12},{12,14},{14,0},{1,15},{3,1}... | collective-permute-start | bytes 786440 | tf_op jit(solution)/shard_map/ppermute | solution.py:280
  41.0 2.2 %collective-permute-done.2.refs_1_ = bf16[16,8192]{1,0:T(8,128)(2,1)S(1)} collective-permute-done((bf16[16,8192]{1,0:T(8,128)(2,1)S(1)}, bf16[16,8192]{1,0:T(8,128)(2,1)S(1)}, u32[]{:S(2)}, u32[]{:S(2)}) %collective-permute-start.2) | collective-permute-done | bytes 262176 | tf_op jit(solution)/shard_map/ppermute | solution.py:280
  43.2 3.1 %collective-permute-start.6 = (bf16[16,8192]{1,0:T(8,128)(2,1)S(1)}, bf16[16,8192]{1,0:T(8,128)(2,1)S(1)}, u32[]{:S(2)}, u32[]{:S(2)}) collective-permute-start(bf16[16,8192]{1,0:T(8,128)(2,1)S(1)} %collective-permute-done.2.refs_1_), channel_id=1, source_target_pairs={{0,2},{2,4},{4,6},{6,8},{8,10},{10,12},{12,14},{14,0},{1,15},{3,1}... | collective-permute-start | bytes 786440 | tf_op jit(solution)/shard_map/ppermute | solution.py:280
  46.3 0.0 collective-permute-done.4.refs_9_
  46.3 2.8 %collective-permute-start.7 = (bf16[16,8192]{1,0:T(8,128)(2,1)S(1)}, bf16[16,8192]{1,0:T(8,128)(2,1)S(1)}, u32[]{:S(2)}, u32[]{:S(2)}) collective-permute-start(bf16[16,8192]{1,0:T(8,128)(2,1)S(1)} %collective-permute-done.4.refs_9_), channel_id=1, source_target_pairs={{0,2},{2,4},{4,6},{6,8},{8,10},{10,12},{12,14},{14,0},{1,15},{3,1}... | collective-permute-start | bytes 786440 | tf_op jit(solution)/shard_map/ppermute | solution.py:280
  49.1 0.5 collective-permute-done.6.refs_3_
  49.6 3.1 %collective-permute-start.9 = (bf16[16,8192]{1,0:T(8,128)(2,1)S(1)}, bf16[16,8192]{1,0:T(8,128)(2,1)S(1)}, u32[]{:S(2)}, u32[]{:S(2)}) collective-permute-start(bf16[16,8192]{1,0:T(8,128)(2,1)S(1)} %collective-permute-done.6.refs_3_), channel_id=1, source_target_pairs={{0,2},{2,4},{4,6},{6,8},{8,10},{10,12},{12,14},{14,0},{1,15},{3,1}... | collective-permute-start | bytes 786440 | tf_op jit(solution)/shard_map/ppermute | solution.py:280
  52.7 0.2 collective-permute-start.13
  52.9 0.3 collective-permute-start.5
  53.2 0.0 collective-permute-done.7.refs_11_
  53.2 2.7 %collective-permute-start.10 = (bf16[16,8192]{1,0:T(8,128)(2,1)S(1)}, bf16[16,8192]{1,0:T(8,128)(2,1)S(1)}, u32[]{:S(2)}, u32[]{:S(2)}) collective-permute-start(bf16[16,8192]{1,0:T(8,128)(2,1)S(1)} %collective-permute-done.7.refs_11_), channel_id=1, source_target_pairs={{0,2},{2,4},{4,6},{6,8},{8,10},{10,12},{12,14},{14,0},{1,15},{3,1}... | collective-permute-start | bytes 786440 | tf_op jit(solution)/shard_map/ppermute | solution.py:280
  55.9 0.1 collective-permute-done.9.refs_5_
  56.0 3.1 %collective-permute-start.12 = (bf16[16,8192]{1,0:T(8,128)(2,1)S(1)}, bf16[16,8192]{1,0:T(8,128)(2,1)S(1)}, u32[]{:S(2)}, u32[]{:S(2)}) collective-permute-start(bf16[16,8192]{1,0:T(8,128)(2,1)S(1)} %collective-permute-done.9.refs_5_), channel_id=1, source_target_pairs={{0,2},{2,4},{4,6},{6,8},{8,10},{10,12},{12,14},{14,0},{1,15},{3,1}... | collective-permute-start | bytes 786440 | tf_op jit(solution)/shard_map/ppermute | solution.py:280
  59.1 1.4 %collective-permute-start.14 = (bf16[16,8192]{1,0:T(8,128)(2,1)S(1)}, bf16[16,8192]{1,0:T(8,128)(2,1)S(1)}, u32[]{:S(2)}, u32[]{:S(2)}) collective-permute-start(bf16[16,8192]{1,0:T(8,128)(2,1)S(1)} %collective-permute-done.6.refs_3_), channel_id=1, source_target_pairs={{0,1},{1,0},{2,3},{3,2},{4,5},{5,4},{6,7},{7,6},{8,9},{9,8},{10,11... | collective-permute-start | bytes 786440 | tf_op jit(solution)/shard_map/ppermute | solution.py:283
  60.5 0.0 collective-permute-done.13.refs_10_
  60.5 0.1 collective-permute-start.8
  60.6 0.4 collective-permute-start.15
  61.0 0.0 collective-permute-done.10.refs_13_
  61.0 2.3 %collective-permute-start.11 = (bf16[16,8192]{1,0:T(8,128)(2,1)S(1)}, bf16[16,8192]{1,0:T(8,128)(2,1)S(1)}, u32[]{:S(2)}, u32[]{:S(2)}) collective-permute-start(bf16[16,8192]{1,0:T(8,128)(2,1)S(1)} %collective-permute-done.10.refs_13_), channel_id=1, source_target_pairs={{0,1},{1,0},{2,3},{3,2},{4,5},{5,4},{6,7},{7,6},{8,9},{9,8},{10,11... | collective-permute-start | bytes 786440 | tf_op jit(solution)/shard_map/ppermute | solution.py:283
  63.3 4.8 %collective-permute-start.16 = (bf16[16,8192]{1,0:T(8,128)(2,1)S(1)}, bf16[16,8192]{1,0:T(8,128)(2,1)S(1)}, u32[]{:S(2)}, u32[]{:S(2)}) collective-permute-start(bf16[16,8192]{1,0:T(8,128)(2,1)S(1)} %collective-permute-done.12.refs_7_), channel_id=1, source_target_pairs={{0,1},{1,0},{2,3},{3,2},{4,5},{5,4},{6,7},{7,6},{8,9},{9,8},{10,11... | collective-permute-start | bytes 786440 | tf_op jit(solution)/shard_map/ppermute | solution.py:283
  68.1 0.1 fusion.11.order_ref
  68.2 0.0 collective-permute-done.8.refs_4_
  68.2 0.0 collective-permute-done.15.refs_14_
  68.2 1.0 %collective-permute-done.16.refs_15_ = bf16[16,8192]{1,0:T(8,128)(2,1)S(1)} collective-permute-done((bf16[16,8192]{1,0:T(8,128)(2,1)S(1)}, bf16[16,8192]{1,0:T(8,128)(2,1)S(1)}, u32[]{:S(2)}, u32[]{:S(2)}) %collective-permute-start.16) | collective-permute-done | bytes 262176 | tf_op jit(solution)/shard_map/ppermute | solution.py:283
  69.3 8.0 %gather_attend.1 = (bf16[768,128]{1,0:T(8,128)(2,1)S(1)}, bf16[2,128,8192]{2,1,0:T(8,128)(2,1)S(1)}) custom-call(s32[1]{0:T(128)} %bitcast.core_ref, bf16[768,128]{1,0:T(8,128)(2,1)S(1)} %collective-permute-done.1.q_ref, bf16[128,128]{1,0:T(8,128)(2,1)S(1)} %fusion.11.order_ref, bf16[16,8192]{1,0:T(8,128)(2,1)S(1)} %transform.1.refs_0_, ...), custom_call_target="tpu_custom_call" | custom-call | tf_op jit(solution)/shard_map/gather_attend/pallas_call | solution.py:236
  77.2 1.1 %collective-permute-start.17 = (bf16[768,128]{1,0:T(8,128)(2,1)S(1)}, bf16[768,128]{1,0:T(8,128)(2,1)S(1)}, u32[]{:S(2)}, u32[]{:S(2)}) collective-permute-start(bf16[768,128]{1,0:T(8,128)(2,1)S(1)} %get-tuple-element.28), channel_id=1, source_target_pairs={{0,16},{16,0},{1,17},{17,1},{2,18},{18,2},{3,19},{19,3},{4,20},{20... | collective-permute-start | bytes 589832 | tf_op jit(solution)/shard_map/ppermute | solution.py:373
  78.4 7.7 %attend.1 = bf16[768,128]{1,0:T(8,128)(2,1)S(1)} custom-call(s32[1]{0:T(128)} %bitcast.core_ref, bf16[768,128]{1,0:T(8,128)(2,1)S(1)} %get-tuple-element.22.q_ref, bf16[128,128]{1,0:T(8,128)(2,1)S(1)} %fusion.11.order_ref, bf16[2,128,8192]{2,1,0:T(8,128)(2,1)S(1)} %get-tuple-element.27.kv_ref), custom_call_target="tpu_custom_call" | custom-call | tf_op jit(solution)/shard_map/attend/pallas_call | solution.py:259
  86.1 0.8 maximum_select_fusion
  (20 shorter events, 0.1 us)
Async XLA Ops:
  0.0 17.4 %copy-start.5 = (bf16[2,768,128]{2,1,0:T(8,128)(2,1)S(1)}, bf16[2,768,128]{2,1,0:T(8,128)(2,1)}, u32[]{:S(2)}) copy-start(bf16[2,768,128]{2,1,0:T(8,128)(2,1)} %param.11) | copy-start | bytes 1179652
  1.1 4.5 %collective-permute-start = (bf16[512,256]{1,0:T(8,128)(2,1)S(1)}, bf16[512,256]{1,0:T(8,128)(2,1)S(1)}, u32[]{:S(2)}, u32[]{:S(2)}) collective-permute-start(bf16[512,256]{1,0:T(8,128)(2,1)S(1)} %get-tuple-element.18), channel_id=1, source_target_pairs={{0,1},{1,0},{2,3},{3,2},{4,5},{5,4},{6,7},{7,6},{8,9},{9,8},{10,11... | collective-permute-start | bytes 786440 | tf_op jit(solution)/shard_map/ppermute | solution.py:315
  6.6 24.5 %copy-start = (bf16[2,512,256]{2,1,0:T(8,128)(2,1)S(1)}, bf16[2,512,256]{2,1,0:T(8,128)(2,1)}, u32[]{:S(2)}) copy-start(bf16[2,512,256]{2,1,0:T(8,128)(2,1)} %constant.141.clone.middle_hbm) | copy-start | bytes 1572868
  6.6 24.5 %copy-start.1 = (f32[2,136,128]{2,1,0:T(8,128)S(1)}, f32[2,136,128]{2,1,0:T(8,128)}, u32[]{:S(2)}) copy-start(f32[2,136,128]{2,1,0:T(8,128)} %constant.142.clone.untwist_hbm) | copy-start | bytes 417796
  6.6 24.5 %copy-start.2 = (f32[2,136,128]{2,1,0:T(8,128)S(1)}, f32[2,136,128]{2,1,0:T(8,128)}, u32[]{:S(2)}) copy-start(f32[2,136,128]{2,1,0:T(8,128)} %constant.140.clone.twist_hbm) | copy-start | bytes 417796
  6.6 24.5 %copy-start.3 = (bf16[272,256]{1,0:T(8,128)(2,1)S(1)}, bf16[272,256]{1,0:T(8,128)(2,1)}, u32[]{:S(2)}) copy-start(bf16[272,256]{1,0:T(8,128)(2,1)} %constant.139.clone.first_hbm) | copy-start | bytes 417796
  6.6 24.5 %copy-start.4 = (bf16[2,128,256]{2,1,0:T(8,128)(2,1)S(1)}, bf16[2,128,256]{2,1,0:T(8,128)(2,1)}, u32[]{:S(2)}) copy-start(bf16[2,128,256]{2,1,0:T(8,128)(2,1)} %constant.143.clone.last_hbm) | copy-start | bytes 393220
  6.7 24.4 %all-to-all-start = ((bf16[16,16,1024]{2,1,0:T(8,128)(2,1)}), bf16[16,16,1024]{2,1,0:T(8,128)(2,1)S(1)}, u32[]{:S(2)}, u32[]{:S(2)}) async-start(bf16[16,16,1024]{2,1,0:T(8,128)(2,1)} %pack.1), calls=%async_computation | async-start | bytes 1048576 | tf_op jit(solution)/shard_map/all_to_all | solution.py:326
  18.3 10.9 %collective-permute-start.1 = (bf16[768,128]{1,0:T(8,128)(2,1)S(1)}, bf16[768,128]{1,0:T(8,128)(2,1)S(1)}, u32[]{:S(2)}, u32[]{:S(2)}) collective-permute-start(bf16[768,128]{1,0:T(8,128)(2,1)S(1)} %get-tuple-element.33), channel_id=1, source_target_pairs={{0,16},{16,0},{1,17},{17,1},{2,18},{18,2},{3,19},{19,3},{4,20},{20... | collective-permute-start | bytes 589832 | tf_op jit(solution)/shard_map/ppermute | solution.py:344
  34.8 5.1 %collective-permute-start.3 = (bf16[16,8192]{1,0:T(8,128)(2,1)S(1)}, bf16[16,8192]{1,0:T(8,128)(2,1)S(1)}, u32[]{:S(2)}, u32[]{:S(2)}) collective-permute-start(bf16[16,8192]{1,0:T(8,128)(2,1)S(1)} %transform.1.refs_0_), channel_id=1, source_target_pairs={{0,1},{1,0},{2,3},{3,2},{4,5},{5,4},{6,7},{7,6},{8,9},{9,8},{10,11... | collective-permute-start | bytes 786440 | tf_op jit(solution)/shard_map/ppermute | solution.py:283
  37.7 5.5 %collective-permute-start.2 = (bf16[16,8192]{1,0:T(8,128)(2,1)S(1)}, bf16[16,8192]{1,0:T(8,128)(2,1)S(1)}, u32[]{:S(2)}, u32[]{:S(2)}) collective-permute-start(bf16[16,8192]{1,0:T(8,128)(2,1)S(1)} %transform.1.refs_0_), channel_id=1, source_target_pairs={{0,2},{2,4},{4,6},{6,8},{8,10},{10,12},{12,14},{14,0},{1,15},{3,1}... | collective-permute-start | bytes 786440 | tf_op jit(solution)/shard_map/ppermute | solution.py:280
  39.8 6.4 %collective-permute-start.4 = (bf16[16,8192]{1,0:T(8,128)(2,1)S(1)}, bf16[16,8192]{1,0:T(8,128)(2,1)S(1)}, u32[]{:S(2)}, u32[]{:S(2)}) collective-permute-start(bf16[16,8192]{1,0:T(8,128)(2,1)S(1)} %collective-permute-done.3.refs_8_), channel_id=1, source_target_pairs={{0,2},{2,4},{4,6},{6,8},{8,10},{10,12},{12,14},{14,0},{1,15},{3,1}... | collective-permute-start | bytes 786440 | tf_op jit(solution)/shard_map/ppermute | solution.py:280
  43.2 6.4 %collective-permute-start.6 = (bf16[16,8192]{1,0:T(8,128)(2,1)S(1)}, bf16[16,8192]{1,0:T(8,128)(2,1)S(1)}, u32[]{:S(2)}, u32[]{:S(2)}) collective-permute-start(bf16[16,8192]{1,0:T(8,128)(2,1)S(1)} %collective-permute-done.2.refs_1_), channel_id=1, source_target_pairs={{0,2},{2,4},{4,6},{6,8},{8,10},{10,12},{12,14},{14,0},{1,15},{3,1}... | collective-permute-start | bytes 786440 | tf_op jit(solution)/shard_map/ppermute | solution.py:280
  46.3 6.9 %collective-permute-start.7 = (bf16[16,8192]{1,0:T(8,128)(2,1)S(1)}, bf16[16,8192]{1,0:T(8,128)(2,1)S(1)}, u32[]{:S(2)}, u32[]{:S(2)}) collective-permute-start(bf16[16,8192]{1,0:T(8,128)(2,1)S(1)} %collective-permute-done.4.refs_9_), channel_id=1, source_target_pairs={{0,2},{2,4},{4,6},{6,8},{8,10},{10,12},{12,14},{14,0},{1,15},{3,1}... | collective-permute-start | bytes 786440 | tf_op jit(solution)/shard_map/ppermute | solution.py:280
  49.6 6.4 %collective-permute-start.9 = (bf16[16,8192]{1,0:T(8,128)(2,1)S(1)}, bf16[16,8192]{1,0:T(8,128)(2,1)S(1)}, u32[]{:S(2)}, u32[]{:S(2)}) collective-permute-start(bf16[16,8192]{1,0:T(8,128)(2,1)S(1)} %collective-permute-done.6.refs_3_), channel_id=1, source_target_pairs={{0,2},{2,4},{4,6},{6,8},{8,10},{10,12},{12,14},{14,0},{1,15},{3,1}... | collective-permute-start | bytes 786440 | tf_op jit(solution)/shard_map/ppermute | solution.py:280
  52.7 7.8 %collective-permute-start.13 = (bf16[16,8192]{1,0:T(8,128)(2,1)S(1)}, bf16[16,8192]{1,0:T(8,128)(2,1)S(1)}, u32[]{:S(2)}, u32[]{:S(2)}) collective-permute-start(bf16[16,8192]{1,0:T(8,128)(2,1)S(1)} %collective-permute-done.2.refs_1_), channel_id=1, source_target_pairs={{0,1},{1,0},{2,3},{3,2},{4,5},{5,4},{6,7},{7,6},{8,9},{9,8},{10,11... | collective-permute-start | bytes 786440 | tf_op jit(solution)/shard_map/ppermute | solution.py:283
  52.9 7.7 %collective-permute-start.5 = (bf16[16,8192]{1,0:T(8,128)(2,1)S(1)}, bf16[16,8192]{1,0:T(8,128)(2,1)S(1)}, u32[]{:S(2)}, u32[]{:S(2)}) collective-permute-start(bf16[16,8192]{1,0:T(8,128)(2,1)S(1)} %collective-permute-done.4.refs_9_), channel_id=1, source_target_pairs={{0,1},{1,0},{2,3},{3,2},{4,5},{5,4},{6,7},{7,6},{8,9},{9,8},{10,11... | collective-permute-start | bytes 786440 | tf_op jit(solution)/shard_map/ppermute | solution.py:283
  53.2 7.8 %collective-permute-start.10 = (bf16[16,8192]{1,0:T(8,128)(2,1)S(1)}, bf16[16,8192]{1,0:T(8,128)(2,1)S(1)}, u32[]{:S(2)}, u32[]{:S(2)}) collective-permute-start(bf16[16,8192]{1,0:T(8,128)(2,1)S(1)} %collective-permute-done.7.refs_11_), channel_id=1, source_target_pairs={{0,2},{2,4},{4,6},{6,8},{8,10},{10,12},{12,14},{14,0},{1,15},{3,1}... | collective-permute-start | bytes 786440 | tf_op jit(solution)/shard_map/ppermute | solution.py:280
  56.0 7.3 %collective-permute-start.12 = (bf16[16,8192]{1,0:T(8,128)(2,1)S(1)}, bf16[16,8192]{1,0:T(8,128)(2,1)S(1)}, u32[]{:S(2)}, u32[]{:S(2)}) collective-permute-start(bf16[16,8192]{1,0:T(8,128)(2,1)S(1)} %collective-permute-done.9.refs_5_), channel_id=1, source_target_pairs={{0,2},{2,4},{4,6},{6,8},{8,10},{10,12},{12,14},{14,0},{1,15},{3,1}... | collective-permute-start | bytes 786440 | tf_op jit(solution)/shard_map/ppermute | solution.py:280
  59.1 9.1 %collective-permute-start.14 = (bf16[16,8192]{1,0:T(8,128)(2,1)S(1)}, bf16[16,8192]{1,0:T(8,128)(2,1)S(1)}, u32[]{:S(2)}, u32[]{:S(2)}) collective-permute-start(bf16[16,8192]{1,0:T(8,128)(2,1)S(1)} %collective-permute-done.6.refs_3_), channel_id=1, source_target_pairs={{0,1},{1,0},{2,3},{3,2},{4,5},{5,4},{6,7},{7,6},{8,9},{9,8},{10,11... | collective-permute-start | bytes 786440 | tf_op jit(solution)/shard_map/ppermute | solution.py:283
  60.5 7.7 %collective-permute-start.8 = (bf16[16,8192]{1,0:T(8,128)(2,1)S(1)}, bf16[16,8192]{1,0:T(8,128)(2,1)S(1)}, u32[]{:S(2)}, u32[]{:S(2)}) collective-permute-start(bf16[16,8192]{1,0:T(8,128)(2,1)S(1)} %collective-permute-done.7.refs_11_), channel_id=1, source_target_pairs={{0,1},{1,0},{2,3},{3,2},{4,5},{5,4},{6,7},{7,6},{8,9},{9,8},{10,11... | collective-permute-start | bytes 786440 | tf_op jit(solution)/shard_map/ppermute | solution.py:283
  60.6 7.6 %collective-permute-start.15 = (bf16[16,8192]{1,0:T(8,128)(2,1)S(1)}, bf16[16,8192]{1,0:T(8,128)(2,1)S(1)}, u32[]{:S(2)}, u32[]{:S(2)}) collective-permute-start(bf16[16,8192]{1,0:T(8,128)(2,1)S(1)} %collective-permute-done.9.refs_5_), channel_id=1, source_target_pairs={{0,1},{1,0},{2,3},{3,2},{4,5},{5,4},{6,7},{7,6},{8,9},{9,8},{10,11... | collective-permute-start | bytes 786440 | tf_op jit(solution)/shard_map/ppermute | solution.py:283
  61.0 7.2 %collective-permute-start.11 = (bf16[16,8192]{1,0:T(8,128)(2,1)S(1)}, bf16[16,8192]{1,0:T(8,128)(2,1)S(1)}, u32[]{:S(2)}, u32[]{:S(2)}) collective-permute-start(bf16[16,8192]{1,0:T(8,128)(2,1)S(1)} %collective-permute-done.10.refs_13_), channel_id=1, source_target_pairs={{0,1},{1,0},{2,3},{3,2},{4,5},{5,4},{6,7},{7,6},{8,9},{9,8},{10,11... | collective-permute-start | bytes 786440 | tf_op jit(solution)/shard_map/ppermute | solution.py:283
  63.3 5.9 %collective-permute-start.16 = (bf16[16,8192]{1,0:T(8,128)(2,1)S(1)}, bf16[16,8192]{1,0:T(8,128)(2,1)S(1)}, u32[]{:S(2)}, u32[]{:S(2)}) collective-permute-start(bf16[16,8192]{1,0:T(8,128)(2,1)S(1)} %collective-permute-done.12.refs_7_), channel_id=1, source_target_pairs={{0,1},{1,0},{2,3},{3,2},{4,5},{5,4},{6,7},{7,6},{8,9},{9,8},{10,11... | collective-permute-start | bytes 786440 | tf_op jit(solution)/shard_map/ppermute | solution.py:283
  77.2 8.9 %collective-permute-start.17 = (bf16[768,128]{1,0:T(8,128)(2,1)S(1)}, bf16[768,128]{1,0:T(8,128)(2,1)S(1)}, u32[]{:S(2)}, u32[]{:S(2)}) collective-permute-start(bf16[768,128]{1,0:T(8,128)(2,1)S(1)} %get-tuple-element.28), channel_id=1, source_target_pairs={{0,16},{16,0},{1,17},{17,1},{2,18},{18,2},{3,19},{19,3},{4,20},{20... | collective-permute-start | bytes 589832 | tf_op jit(solution)/shard_map/ppermute | solution.py:373

commit v5 on v4

--- a/solution.py
+++ b/solution.py
@@ -72,20 +72,33 @@
     return jnp.exp(jnp.arange(HALF).astype(F32) * (-2.0 * math.log(THETA) / HEAD))
 
 
-def pack_kernel(core_ref, mine_ref, other_ref, out_ref):
+def turn(block_ref, store):
+    turned = block_ref[...].astype(F32).T
+    parts = turned.shape[0] // COLUMNS
+    for part in range(parts):
+        low = part // (parts // 2) * HEAD + part % (parts // 2) * 8
+        rows = jnp.concatenate([turned[low : low + 8], turned[low + HALF : low + HALF + 8]], axis=0)
+        store(part, rows.astype(BF16))
+
+
+def turn_kernel(mine_ref, out_ref):
+    def store(part, rows):
+        out_ref[part] = rows
+
+    turn(mine_ref, store)
+
+
+def pack_kernel(core_ref, turned_ref, other_ref, out_ref):
     core = core_ref[0]
-    tokens = mine_ref.shape[0]
-    heads, parts = 2, out_ref.shape[0] // 2
-    for block_ref, place in ((mine_ref, core), (other_ref, 1 - core)):
-        turned = block_ref[...].astype(F32).T
-        at = pl.multiple_of(place * tokens, 128)
-        for head in range(heads):
-            for part in range(parts):
-                low = head * HEAD + part * 8
-                rows = jnp.concatenate(
-                    [turned[low : low + 8], turned[low + HALF : low + HALF + 8]], axis=0
-                )
-                out_ref[head * parts + part, :, pl.ds(at, tokens)] = rows.astype(BF16)
+    tokens = other_ref.shape[0]
+    here = pl.multiple_of(core * tokens, 128)
+    there = pl.multiple_of((1 - core) * tokens, 128)
+    out_ref[:, :, pl.ds(here, tokens)] = turned_ref[...]
+
+    def store(part, rows):
+        out_ref[part, :, pl.ds(there, tokens)] = rows
+
+    turn(other_ref, store)
 
 
 def halves(block):
@@ -313,6 +326,14 @@
     send = jnp.where(core == 0, values, keys)
     kept_tokens, send = lax.optimization_barrier((kept_tokens, send))
     other = lax.ppermute(send, "core", SWAP)
+    turned_tokens = pl.pallas_call(
+        turn_kernel,
+        in_specs=[vmem],
+        out_specs=vmem,
+        out_shape=jax.ShapeDtypeStruct((sources, COLUMNS, tokens), BF16),
+        compiler_params=pltpu.CompilerParams(vmem_limit_bytes=16 * 1024 * 1024),
+        name="turn",
+    )(kept_tokens)
     packed = pl.pallas_call(
         pack_kernel,
         in_specs=[smem, vmem, vmem],
@@ -320,7 +341,7 @@
         out_shape=jax.ShapeDtypeStruct((sources, COLUMNS, 2 * tokens), BF16),
         compiler_params=pltpu.CompilerParams(vmem_limit_bytes=16 * 1024 * 1024),
         name="pack",
-    )(core_here, kept_tokens, other)
+    )(core_here, turned_tokens, other)
     places_here = positions.astype(F32)
     packed, queries, places_here = lax.optimization_barrier((packed, queries, places_here))
     received = lax.all_to_all(packed, ("yhi", "z"), 0, 0, tiled=True)

time: 87.1 us -> 87.1 us (level)
  no operation moved by 1% of the time
where the time goes in v5:
time: 87.1 us; the launch traced here: 86.8 us
  starting transfers between devices  47.2 us (54%)
  Pallas kernels  20.4 us (23%)
  waiting for transfers between devices  12.9 us (15%)
  other arithmetic  5.63 us (6%)
    ppermute x7, starting transfers between devices, along(): return lax.ppermute(block, ('z', 'core'), onward)  18.1 us
    ppermute x8, starting transfers between devices, across(): return lax.ppermute(block, 'core', SWAP)  12.4 us
    all_to_all x1, starting transfers between devices, on_device(): received = lax.all_to_all(packed, ('yhi', 'z'), 0, 0, tiled=True)  9.33 us
    pallas_call x1, Pallas kernels, gather_attend(): pl.pallas_call(gather_attend_kernel, grid=(rows // ROW_BLOCK,), in_specs=...  7.98 us
    pallas_call x1, Pallas kernels, attend(): pl.pallas_call(attend_kernel, grid=(q.shape[0] // ROW_BLOCK,), in_specs=[...  7.71 us
    ppermute x1, waiting for transfers between devices, on_device(): lax.ppermute(jnp.where(head == 0, turned[1], turned[0]), 'yhi', SWAP)  6.98 us
    pallas_call x1, Pallas kernels, on_device(): pl.pallas_call(transform_kernel, in_specs=[vmem] * 3 + [hbm] * 5, out_spe...  3.64 us
    ppermute x1, starting transfers between devices, on_device(): other = lax.ppermute(send, 'core', SWAP)  3.33 us
  transfers between devices with their start and end apart: 19, of which 7 were waited for; matrix products, arithmetic and copies ran while one was open for 5% of the time, Pallas kernels for 9%

profile of v5, /device:TPU:1, one launch (start us, length us, event | category | flops | bytes accessed | tf_op | source)
XLA Modules:
  0.0 86.8 jit_solution(13470425987393577200)
XLA Ops:
  0.0 1.1 %broadcast_select_fusion = (bf16[512,256]{1,0:T(8,128)(2,1)S(1)}, bf16[512,256]{1,0:T(8,128)(2,1)S(1)}) fusion(bf16[512,256]{1,0:T(8,128)(2,1)} %param.10, bf16[512,256]{1,0:T(8,128)(2,1)} %param.9, pred[]{:T(512)S(6)} %eq.47), kind=kLoop, calls=%fused_computation.13 | loop fusion | flops 262144 | bytes 1048577 | tf_op jit(solution)/shard_map/jit(_where)/select_n | solution.py:326
  1.1 3.3 %collective-permute-start = (bf16[512,256]{1,0:T(8,128)(2,1)S(1)}, bf16[512,256]{1,0:T(8,128)(2,1)S(1)}, u32[]{:S(2)}, u32[]{:S(2)}) collective-permute-start(bf16[512,256]{1,0:T(8,128)(2,1)S(1)} %get-tuple-element.18), channel_id=1, source_target_pairs={{0,1},{1,0},{2,3},{3,2},{4,5},{5,4},{6,7},{7,6},{8,9},{9,8},{10,11... | collective-permute-start | bytes 786440 | tf_op jit(solution)/shard_map/ppermute | solution.py:328
  4.5 0.7 convert_element_type.30
  5.2 0.1 turn.1.turned_ref
  5.3 0.1 dynamic_slice.3
  5.4 0.2 collective-permute-done.other_ref
  5.6 0.9 %pack.1 = bf16[16,16,1024]{2,1,0:T(8,128)(2,1)} custom-call(s32[1]{0:T(128)} %bitcast.core_ref, bf16[16,16,512]{2,1,0:T(8,128)(2,1)S(1)} %turn.1.turned_ref, bf16[512,256]{1,0:T(8,128)(2,1)S(1)} %collective-permute-done.other_ref), custom_call_target="tpu_custom_call" | custom-call | tf_op jit(solution)/shard_map/pack/pallas_call | solution.py:337
  6.6 0.0 copy-start.4
  6.6 9.3 %all-to-all-start = ((bf16[16,16,1024]{2,1,0:T(8,128)(2,1)}), bf16[16,16,1024]{2,1,0:T(8,128)(2,1)S(1)}, u32[]{:S(2)}, u32[]{:S(2)}) async-start(bf16[16,16,1024]{2,1,0:T(8,128)(2,1)} %pack.1), calls=%async_computation | async-start | bytes 1048576 | tf_op jit(solution)/shard_map/all_to_all | solution.py:347
  15.9 1.4 %multiply_cosine_fusion = (f32[768,64]{1,0:T(8,128)S(1)}, f32[768,64]{1,0:T(8,128)S(1)}) fusion(f32[64]{0:T(128)S(1)} %multiply_exponential_fusion, f32[768]{0:T(1024)S(1)} %convert_element_type.30), kind=kLoop, calls=%fused_computation.4 | loop fusion | flops 49152 | bytes 396544 | tf_op jit(solution)/shard_map/cos | solution.py:351
  17.4 0.1 convert_element_type.31
  17.4 0.4 subtract_convert_fusion
  17.8 0.3 convolution_convert_fusion
  18.2 3.0 %collective-permute-start.1 = (bf16[768,128]{1,0:T(8,128)(2,1)S(1)}, bf16[768,128]{1,0:T(8,128)(2,1)S(1)}, u32[]{:S(2)}, u32[]{:S(2)}) collective-permute-start(bf16[768,128]{1,0:T(8,128)(2,1)S(1)} %get-tuple-element.33), channel_id=1, source_target_pairs={{0,16},{16,0},{1,17},{17,1},{2,18},{18,2},{3,19},{19,3},{4,20},{20... | collective-permute-start | bytes 589832 | tf_op jit(solution)/shard_map/ppermute | solution.py:365
  21.2 1.0 %fusion.4 = (f32[8,8192]{1,0:T(8,128)S(1)}, f32[8,8192]{1,0:T(8,128)S(1)}) fusion(f32[8192]{0:T(1024)S(1)} %fusion.15, f32[8]{0:T(128)S(1)} %dynamic_slice.3, pred[]{:T(512)S(6)} %eq.47), kind=kLoop, calls=%fused_computation.12 | loop fusion | flops 196608 | bytes 557089 | tf_op jit(solution)/shard_map/jit(_where)/select_n | solution.py:371
  22.2 7.0 %collective-permute-done.1.q_ref = bf16[768,128]{1,0:T(8,128)(2,1)S(1)} collective-permute-done((bf16[768,128]{1,0:T(8,128)(2,1)S(1)}, bf16[768,128]{1,0:T(8,128)(2,1)S(1)}, u32[]{:S(2)}, u32[]{:S(2)}) %collective-permute-start.1) | collective-permute-done | bytes 196640 | tf_op jit(solution)/shard_map/ppermute | solution.py:365
  29.2 1.9 %all-to-all-done.x_ref = bf16[16,16,1024]{2,1,0:T(8,128)(2,1)S(1)} async-done(((bf16[16,16,1024]{2,1,0:T(8,128)(2,1)}), bf16[16,16,1024]{2,1,0:T(8,128)(2,1)S(1)}, u32[]{:S(2)}, u32[]{:S(2)}) %all-to-all-start) | async-done | bytes 524320 | tf_op jit(solution)/shard_map/all_to_all | solution.py:347
  31.1 3.6 %transform.1.refs_0_ = bf16[16,8192]{1,0:T(8,128)(2,1)S(1)} custom-call(bf16[16,16,1024]{2,1,0:T(8,128)(2,1)S(1)} %all-to-all-done.x_ref, f32[8,8192]{1,0:T(8,128)S(1)} %get-tuple-element.25.cos_ref, f32[8,8192]{1,0:T(8,128)S(1)} %get-tuple-element.26.sin_ref, bf16[272,256]{1,0:T(8,128)(2,1)S(1)} %copy-done.3, f32[2,136,128]{2,1,0:T(8,128)S(1)} %copy-done.2, ...), custom_call_target="tpu_custom_call" | custom-call | tf_op jit(solution)/shard_map/transform/pallas_call | solution.py:376
  34.7 2.9 %collective-permute-start.3 = (bf16[16,8192]{1,0:T(8,128)(2,1)S(1)}, bf16[16,8192]{1,0:T(8,128)(2,1)S(1)}, u32[]{:S(2)}, u32[]{:S(2)}) collective-permute-start(bf16[16,8192]{1,0:T(8,128)(2,1)S(1)} %transform.1.refs_0_), channel_id=1, source_target_pairs={{0,1},{1,0},{2,3},{3,2},{4,5},{5,4},{6,7},{7,6},{8,9},{9,8},{10,11... | collective-permute-start | bytes 786440 | tf_op jit(solution)/shard_map/ppermute | solution.py:296
  37.6 2.2 %collective-permute-start.2 = (bf16[16,8192]{1,0:T(8,128)(2,1)S(1)}, bf16[16,8192]{1,0:T(8,128)(2,1)S(1)}, u32[]{:S(2)}, u32[]{:S(2)}) collective-permute-start(bf16[16,8192]{1,0:T(8,128)(2,1)S(1)} %transform.1.refs_0_), channel_id=1, source_target_pairs={{0,2},{2,4},{4,6},{6,8},{8,10},{10,12},{12,14},{14,0},{1,15},{3,1}... | collective-permute-start | bytes 786440 | tf_op jit(solution)/shard_map/ppermute | solution.py:293
  39.8 1.2 %collective-permute-start.4 = (bf16[16,8192]{1,0:T(8,128)(2,1)S(1)}, bf16[16,8192]{1,0:T(8,128)(2,1)S(1)}, u32[]{:S(2)}, u32[]{:S(2)}) collective-permute-start(bf16[16,8192]{1,0:T(8,128)(2,1)S(1)} %collective-permute-done.3.refs_8_), channel_id=1, source_target_pairs={{0,2},{2,4},{4,6},{6,8},{8,10},{10,12},{12,14},{14,0},{1,15},{3,1}... | collective-permute-start | bytes 786440 | tf_op jit(solution)/shard_map/ppermute | solution.py:293
  40.9 2.2 %collective-permute-done.2.refs_1_ = bf16[16,8192]{1,0:T(8,128)(2,1)S(1)} collective-permute-done((bf16[16,8192]{1,0:T(8,128)(2,1)S(1)}, bf16[16,8192]{1,0:T(8,128)(2,1)S(1)}, u32[]{:S(2)}, u32[]{:S(2)}) %collective-permute-start.2) | collective-permute-done | bytes 262176 | tf_op jit(solution)/shard_map/ppermute | solution.py:293
  43.1 3.1 %collective-permute-start.6 = (bf16[16,8192]{1,0:T(8,128)(2,1)S(1)}, bf16[16,8192]{1,0:T(8,128)(2,1)S(1)}, u32[]{:S(2)}, u32[]{:S(2)}) collective-permute-start(bf16[16,8192]{1,0:T(8,128)(2,1)S(1)} %collective-permute-done.2.refs_1_), channel_id=1, source_target_pairs={{0,2},{2,4},{4,6},{6,8},{8,10},{10,12},{12,14},{14,0},{1,15},{3,1}... | collective-permute-start | bytes 786440 | tf_op jit(solution)/shard_map/ppermute | solution.py:293
  46.2 2.8 %collective-permute-start.7 = (bf16[16,8192]{1,0:T(8,128)(2,1)S(1)}, bf16[16,8192]{1,0:T(8,128)(2,1)S(1)}, u32[]{:S(2)}, u32[]{:S(2)}) collective-permute-start(bf16[16,8192]{1,0:T(8,128)(2,1)S(1)} %collective-permute-done.4.refs_9_), channel_id=1, source_target_pairs={{0,2},{2,4},{4,6},{6,8},{8,10},{10,12},{12,14},{14,0},{1,15},{3,1}... | collective-permute-start | bytes 786440 | tf_op jit(solution)/shard_map/ppermute | solution.py:293
  49.0 0.5 collective-permute-done.6.refs_3_
  49.5 3.1 %collective-permute-start.9 = (bf16[16,8192]{1,0:T(8,128)(2,1)S(1)}, bf16[16,8192]{1,0:T(8,128)(2,1)S(1)}, u32[]{:S(2)}, u32[]{:S(2)}) collective-permute-start(bf16[16,8192]{1,0:T(8,128)(2,1)S(1)} %collective-permute-done.6.refs_3_), channel_id=1, source_target_pairs={{0,2},{2,4},{4,6},{6,8},{8,10},{10,12},{12,14},{14,0},{1,15},{3,1}... | collective-permute-start | bytes 786440 | tf_op jit(solution)/shard_map/ppermute | solution.py:293
  52.6 0.2 collective-permute-start.13
  52.9 0.3 collective-permute-start.5
  53.1 0.0 collective-permute-done.7.refs_11_
  53.1 2.7 %collective-permute-start.10 = (bf16[16,8192]{1,0:T(8,128)(2,1)S(1)}, bf16[16,8192]{1,0:T(8,128)(2,1)S(1)}, u32[]{:S(2)}, u32[]{:S(2)}) collective-permute-start(bf16[16,8192]{1,0:T(8,128)(2,1)S(1)} %collective-permute-done.7.refs_11_), channel_id=1, source_target_pairs={{0,2},{2,4},{4,6},{6,8},{8,10},{10,12},{12,14},{14,0},{1,15},{3,1}... | collective-permute-start | bytes 786440 | tf_op jit(solution)/shard_map/ppermute | solution.py:293
  55.8 0.1 collective-permute-done.9.refs_5_
  55.9 3.1 %collective-permute-start.12 = (bf16[16,8192]{1,0:T(8,128)(2,1)S(1)}, bf16[16,8192]{1,0:T(8,128)(2,1)S(1)}, u32[]{:S(2)}, u32[]{:S(2)}) collective-permute-start(bf16[16,8192]{1,0:T(8,128)(2,1)S(1)} %collective-permute-done.9.refs_5_), channel_id=1, source_target_pairs={{0,2},{2,4},{4,6},{6,8},{8,10},{10,12},{12,14},{14,0},{1,15},{3,1}... | collective-permute-start | bytes 786440 | tf_op jit(solution)/shard_map/ppermute | solution.py:293
  59.1 1.4 %collective-permute-start.14 = (bf16[16,8192]{1,0:T(8,128)(2,1)S(1)}, bf16[16,8192]{1,0:T(8,128)(2,1)S(1)}, u32[]{:S(2)}, u32[]{:S(2)}) collective-permute-start(bf16[16,8192]{1,0:T(8,128)(2,1)S(1)} %collective-permute-done.6.refs_3_), channel_id=1, source_target_pairs={{0,1},{1,0},{2,3},{3,2},{4,5},{5,4},{6,7},{7,6},{8,9},{9,8},{10,11... | collective-permute-start | bytes 786440 | tf_op jit(solution)/shard_map/ppermute | solution.py:296
  60.4 0.0 collective-permute-done.13.refs_10_
  60.4 0.1 collective-permute-start.8
  60.5 0.0 collective-permute-done.5.refs_2_
  60.5 0.4 collective-permute-start.15
  61.0 0.0 collective-permute-done.10.refs_13_
  61.0 2.3 %collective-permute-start.11 = (bf16[16,8192]{1,0:T(8,128)(2,1)S(1)}, bf16[16,8192]{1,0:T(8,128)(2,1)S(1)}, u32[]{:S(2)}, u32[]{:S(2)}) collective-permute-start(bf16[16,8192]{1,0:T(8,128)(2,1)S(1)} %collective-permute-done.10.refs_13_), channel_id=1, source_target_pairs={{0,1},{1,0},{2,3},{3,2},{4,5},{5,4},{6,7},{7,6},{8,9},{9,8},{10,11... | collective-permute-start | bytes 786440 | tf_op jit(solution)/shard_map/ppermute | solution.py:296
  63.2 0.0 collective-permute-done.12.refs_7_
  63.3 4.8 %collective-permute-start.16 = (bf16[16,8192]{1,0:T(8,128)(2,1)S(1)}, bf16[16,8192]{1,0:T(8,128)(2,1)S(1)}, u32[]{:S(2)}, u32[]{:S(2)}) collective-permute-start(bf16[16,8192]{1,0:T(8,128)(2,1)S(1)} %collective-permute-done.12.refs_7_), channel_id=1, source_target_pairs={{0,1},{1,0},{2,3},{3,2},{4,5},{5,4},{6,7},{7,6},{8,9},{9,8},{10,11... | collective-permute-start | bytes 786440 | tf_op jit(solution)/shard_map/ppermute | solution.py:296
  68.0 0.1 fusion.11.order_ref
  68.1 0.0 collective-permute-done.14.refs_12_
  68.2 1.0 %collective-permute-done.16.refs_15_ = bf16[16,8192]{1,0:T(8,128)(2,1)S(1)} collective-permute-done((bf16[16,8192]{1,0:T(8,128)(2,1)S(1)}, bf16[16,8192]{1,0:T(8,128)(2,1)S(1)}, u32[]{:S(2)}, u32[]{:S(2)}) %collective-permute-start.16) | collective-permute-done | bytes 262176 | tf_op jit(solution)/shard_map/ppermute | solution.py:296
  69.2 8.0 %gather_attend.1 = (bf16[768,128]{1,0:T(8,128)(2,1)S(1)}, bf16[2,128,8192]{2,1,0:T(8,128)(2,1)S(1)}) custom-call(s32[1]{0:T(128)} %bitcast.core_ref, bf16[768,128]{1,0:T(8,128)(2,1)S(1)} %collective-permute-done.1.q_ref, bf16[128,128]{1,0:T(8,128)(2,1)S(1)} %fusion.11.order_ref, bf16[16,8192]{1,0:T(8,128)(2,1)S(1)} %transform.1.refs_0_, ...), custom_call_target="tpu_custom_call" | custom-call | tf_op jit(solution)/shard_map/gather_attend/pallas_call | solution.py:249
  77.2 1.1 %collective-permute-start.17 = (bf16[768,128]{1,0:T(8,128)(2,1)S(1)}, bf16[768,128]{1,0:T(8,128)(2,1)S(1)}, u32[]{:S(2)}, u32[]{:S(2)}) collective-permute-start(bf16[768,128]{1,0:T(8,128)(2,1)S(1)} %get-tuple-element.28), channel_id=1, source_target_pairs={{0,16},{16,0},{1,17},{17,1},{2,18},{18,2},{3,19},{19,3},{4,20},{20... | collective-permute-start | bytes 589832 | tf_op jit(solution)/shard_map/ppermute | solution.py:394
  78.3 7.7 %attend.1 = bf16[768,128]{1,0:T(8,128)(2,1)S(1)} custom-call(s32[1]{0:T(128)} %bitcast.core_ref, bf16[768,128]{1,0:T(8,128)(2,1)S(1)} %get-tuple-element.22.q_ref, bf16[128,128]{1,0:T(8,128)(2,1)S(1)} %fusion.11.order_ref, bf16[2,128,8192]{2,1,0:T(8,128)(2,1)S(1)} %get-tuple-element.27.kv_ref), custom_call_target="tpu_custom_call" | custom-call | tf_op jit(solution)/shard_map/attend/pallas_call | solution.py:272
  86.0 0.8 maximum_select_fusion
  (21 shorter events, 0.1 us)
Async XLA Ops:
  0.0 17.4 %copy-start.5 = (bf16[2,768,128]{2,1,0:T(8,128)(2,1)S(1)}, bf16[2,768,128]{2,1,0:T(8,128)(2,1)}, u32[]{:S(2)}) copy-start(bf16[2,768,128]{2,1,0:T(8,128)(2,1)} %param.11) | copy-start | bytes 1179652
  1.1 4.5 %collective-permute-start = (bf16[512,256]{1,0:T(8,128)(2,1)S(1)}, bf16[512,256]{1,0:T(8,128)(2,1)S(1)}, u32[]{:S(2)}, u32[]{:S(2)}) collective-permute-start(bf16[512,256]{1,0:T(8,128)(2,1)S(1)} %get-tuple-element.18), channel_id=1, source_target_pairs={{0,1},{1,0},{2,3},{3,2},{4,5},{5,4},{6,7},{7,6},{8,9},{9,8},{10,11... | collective-permute-start | bytes 786440 | tf_op jit(solution)/shard_map/ppermute | solution.py:328
  6.6 24.5 %copy-start = (bf16[2,512,256]{2,1,0:T(8,128)(2,1)S(1)}, bf16[2,512,256]{2,1,0:T(8,128)(2,1)}, u32[]{:S(2)}) copy-start(bf16[2,512,256]{2,1,0:T(8,128)(2,1)} %constant.141.clone.middle_hbm) | copy-start | bytes 1572868
  6.6 24.5 %copy-start.1 = (f32[2,136,128]{2,1,0:T(8,128)S(1)}, f32[2,136,128]{2,1,0:T(8,128)}, u32[]{:S(2)}) copy-start(f32[2,136,128]{2,1,0:T(8,128)} %constant.142.clone.untwist_hbm) | copy-start | bytes 417796
  6.6 24.5 %copy-start.2 = (f32[2,136,128]{2,1,0:T(8,128)S(1)}, f32[2,136,128]{2,1,0:T(8,128)}, u32[]{:S(2)}) copy-start(f32[2,136,128]{2,1,0:T(8,128)} %constant.140.clone.twist_hbm) | copy-start | bytes 417796
  6.6 24.5 %copy-start.3 = (bf16[272,256]{1,0:T(8,128)(2,1)S(1)}, bf16[272,256]{1,0:T(8,128)(2,1)}, u32[]{:S(2)}) copy-start(bf16[272,256]{1,0:T(8,128)(2,1)} %constant.139.clone.first_hbm) | copy-start | bytes 417796
  6.6 24.5 %copy-start.4 = (bf16[2,128,256]{2,1,0:T(8,128)(2,1)S(1)}, bf16[2,128,256]{2,1,0:T(8,128)(2,1)}, u32[]{:S(2)}) copy-start(bf16[2,128,256]{2,1,0:T(8,128)(2,1)} %constant.143.clone.last_hbm) | copy-start | bytes 393220
  6.6 24.4 %all-to-all-start = ((bf16[16,16,1024]{2,1,0:T(8,128)(2,1)}), bf16[16,16,1024]{2,1,0:T(8,128)(2,1)S(1)}, u32[]{:S(2)}, u32[]{:S(2)}) async-start(bf16[16,16,1024]{2,1,0:T(8,128)(2,1)} %pack.1), calls=%async_computation | async-start | bytes 1048576 | tf_op jit(solution)/shard_map/all_to_all | solution.py:347
  18.2 10.9 %collective-permute-start.1 = (bf16[768,128]{1,0:T(8,128)(2,1)S(1)}, bf16[768,128]{1,0:T(8,128)(2,1)S(1)}, u32[]{:S(2)}, u32[]{:S(2)}) collective-permute-start(bf16[768,128]{1,0:T(8,128)(2,1)S(1)} %get-tuple-element.33), channel_id=1, source_target_pairs={{0,16},{16,0},{1,17},{17,1},{2,18},{18,2},{3,19},{19,3},{4,20},{20... | collective-permute-start | bytes 589832 | tf_op jit(solution)/shard_map/ppermute | solution.py:365
  34.7 5.1 %collective-permute-start.3 = (bf16[16,8192]{1,0:T(8,128)(2,1)S(1)}, bf16[16,8192]{1,0:T(8,128)(2,1)S(1)}, u32[]{:S(2)}, u32[]{:S(2)}) collective-permute-start(bf16[16,8192]{1,0:T(8,128)(2,1)S(1)} %transform.1.refs_0_), channel_id=1, source_target_pairs={{0,1},{1,0},{2,3},{3,2},{4,5},{5,4},{6,7},{7,6},{8,9},{9,8},{10,11... | collective-permute-start | bytes 786440 | tf_op jit(solution)/shard_map/ppermute | solution.py:296
  37.6 5.5 %collective-permute-start.2 = (bf16[16,8192]{1,0:T(8,128)(2,1)S(1)}, bf16[16,8192]{1,0:T(8,128)(2,1)S(1)}, u32[]{:S(2)}, u32[]{:S(2)}) collective-permute-start(bf16[16,8192]{1,0:T(8,128)(2,1)S(1)} %transform.1.refs_0_), channel_id=1, source_target_pairs={{0,2},{2,4},{4,6},{6,8},{8,10},{10,12},{12,14},{14,0},{1,15},{3,1}... | collective-permute-start | bytes 786440 | tf_op jit(solution)/shard_map/ppermute | solution.py:293
  39.8 6.4 %collective-permute-start.4 = (bf16[16,8192]{1,0:T(8,128)(2,1)S(1)}, bf16[16,8192]{1,0:T(8,128)(2,1)S(1)}, u32[]{:S(2)}, u32[]{:S(2)}) collective-permute-start(bf16[16,8192]{1,0:T(8,128)(2,1)S(1)} %collective-permute-done.3.refs_8_), channel_id=1, source_target_pairs={{0,2},{2,4},{4,6},{6,8},{8,10},{10,12},{12,14},{14,0},{1,15},{3,1}... | collective-permute-start | bytes 786440 | tf_op jit(solution)/shard_map/ppermute | solution.py:293
  43.1 6.4 %collective-permute-start.6 = (bf16[16,8192]{1,0:T(8,128)(2,1)S(1)}, bf16[16,8192]{1,0:T(8,128)(2,1)S(1)}, u32[]{:S(2)}, u32[]{:S(2)}) collective-permute-start(bf16[16,8192]{1,0:T(8,128)(2,1)S(1)} %collective-permute-done.2.refs_1_), channel_id=1, source_target_pairs={{0,2},{2,4},{4,6},{6,8},{8,10},{10,12},{12,14},{14,0},{1,15},{3,1}... | collective-permute-start | bytes 786440 | tf_op jit(solution)/shard_map/ppermute | solution.py:293
  46.2 6.9 %collective-permute-start.7 = (bf16[16,8192]{1,0:T(8,128)(2,1)S(1)}, bf16[16,8192]{1,0:T(8,128)(2,1)S(1)}, u32[]{:S(2)}, u32[]{:S(2)}) collective-permute-start(bf16[16,8192]{1,0:T(8,128)(2,1)S(1)} %collective-permute-done.4.refs_9_), channel_id=1, source_target_pairs={{0,2},{2,4},{4,6},{6,8},{8,10},{10,12},{12,14},{14,0},{1,15},{3,1}... | collective-permute-start | bytes 786440 | tf_op jit(solution)/shard_map/ppermute | solution.py:293
  49.5 6.4 %collective-permute-start.9 = (bf16[16,8192]{1,0:T(8,128)(2,1)S(1)}, bf16[16,8192]{1,0:T(8,128)(2,1)S(1)}, u32[]{:S(2)}, u32[]{:S(2)}) collective-permute-start(bf16[16,8192]{1,0:T(8,128)(2,1)S(1)} %collective-permute-done.6.refs_3_), channel_id=1, source_target_pairs={{0,2},{2,4},{4,6},{6,8},{8,10},{10,12},{12,14},{14,0},{1,15},{3,1}... | collective-permute-start | bytes 786440 | tf_op jit(solution)/shard_map/ppermute | solution.py:293
  52.6 7.8 %collective-permute-start.13 = (bf16[16,8192]{1,0:T(8,128)(2,1)S(1)}, bf16[16,8192]{1,0:T(8,128)(2,1)S(1)}, u32[]{:S(2)}, u32[]{:S(2)}) collective-permute-start(bf16[16,8192]{1,0:T(8,128)(2,1)S(1)} %collective-permute-done.2.refs_1_), channel_id=1, source_target_pairs={{0,1},{1,0},{2,3},{3,2},{4,5},{5,4},{6,7},{7,6},{8,9},{9,8},{10,11... | collective-permute-start | bytes 786440 | tf_op jit(solution)/shard_map/ppermute | solution.py:296
  52.9 7.7 %collective-permute-start.5 = (bf16[16,8192]{1,0:T(8,128)(2,1)S(1)}, bf16[16,8192]{1,0:T(8,128)(2,1)S(1)}, u32[]{:S(2)}, u32[]{:S(2)}) collective-permute-start(bf16[16,8192]{1,0:T(8,128)(2,1)S(1)} %collective-permute-done.4.refs_9_), channel_id=1, source_target_pairs={{0,1},{1,0},{2,3},{3,2},{4,5},{5,4},{6,7},{7,6},{8,9},{9,8},{10,11... | collective-permute-start | bytes 786440 | tf_op jit(solution)/shard_map/ppermute | solution.py:296
  53.1 7.8 %collective-permute-start.10 = (bf16[16,8192]{1,0:T(8,128)(2,1)S(1)}, bf16[16,8192]{1,0:T(8,128)(2,1)S(1)}, u32[]{:S(2)}, u32[]{:S(2)}) collective-permute-start(bf16[16,8192]{1,0:T(8,128)(2,1)S(1)} %collective-permute-done.7.refs_11_), channel_id=1, source_target_pairs={{0,2},{2,4},{4,6},{6,8},{8,10},{10,12},{12,14},{14,0},{1,15},{3,1}... | collective-permute-start | bytes 786440 | tf_op jit(solution)/shard_map/ppermute | solution.py:293
  55.9 7.3 %collective-permute-start.12 = (bf16[16,8192]{1,0:T(8,128)(2,1)S(1)}, bf16[16,8192]{1,0:T(8,128)(2,1)S(1)}, u32[]{:S(2)}, u32[]{:S(2)}) collective-permute-start(bf16[16,8192]{1,0:T(8,128)(2,1)S(1)} %collective-permute-done.9.refs_5_), channel_id=1, source_target_pairs={{0,2},{2,4},{4,6},{6,8},{8,10},{10,12},{12,14},{14,0},{1,15},{3,1}... | collective-permute-start | bytes 786440 | tf_op jit(solution)/shard_map/ppermute | solution.py:293
  59.1 9.1 %collective-permute-start.14 = (bf16[16,8192]{1,0:T(8,128)(2,1)S(1)}, bf16[16,8192]{1,0:T(8,128)(2,1)S(1)}, u32[]{:S(2)}, u32[]{:S(2)}) collective-permute-start(bf16[16,8192]{1,0:T(8,128)(2,1)S(1)} %collective-permute-done.6.refs_3_), channel_id=1, source_target_pairs={{0,1},{1,0},{2,3},{3,2},{4,5},{5,4},{6,7},{7,6},{8,9},{9,8},{10,11... | collective-permute-start | bytes 786440 | tf_op jit(solution)/shard_map/ppermute | solution.py:296
  60.4 7.7 %collective-permute-start.8 = (bf16[16,8192]{1,0:T(8,128)(2,1)S(1)}, bf16[16,8192]{1,0:T(8,128)(2,1)S(1)}, u32[]{:S(2)}, u32[]{:S(2)}) collective-permute-start(bf16[16,8192]{1,0:T(8,128)(2,1)S(1)} %collective-permute-done.7.refs_11_), channel_id=1, source_target_pairs={{0,1},{1,0},{2,3},{3,2},{4,5},{5,4},{6,7},{7,6},{8,9},{9,8},{10,11... | collective-permute-start | bytes 786440 | tf_op jit(solution)/shard_map/ppermute | solution.py:296
  60.5 7.6 %collective-permute-start.15 = (bf16[16,8192]{1,0:T(8,128)(2,1)S(1)}, bf16[16,8192]{1,0:T(8,128)(2,1)S(1)}, u32[]{:S(2)}, u32[]{:S(2)}) collective-permute-start(bf16[16,8192]{1,0:T(8,128)(2,1)S(1)} %collective-permute-done.9.refs_5_), channel_id=1, source_target_pairs={{0,1},{1,0},{2,3},{3,2},{4,5},{5,4},{6,7},{7,6},{8,9},{9,8},{10,11... | collective-permute-start | bytes 786440 | tf_op jit(solution)/shard_map/ppermute | solution.py:296
  61.0 7.2 %collective-permute-start.11 = (bf16[16,8192]{1,0:T(8,128)(2,1)S(1)}, bf16[16,8192]{1,0:T(8,128)(2,1)S(1)}, u32[]{:S(2)}, u32[]{:S(2)}) collective-permute-start(bf16[16,8192]{1,0:T(8,128)(2,1)S(1)} %collective-permute-done.10.refs_13_), channel_id=1, source_target_pairs={{0,1},{1,0},{2,3},{3,2},{4,5},{5,4},{6,7},{7,6},{8,9},{9,8},{10,11... | collective-permute-start | bytes 786440 | tf_op jit(solution)/shard_map/ppermute | solution.py:296
  63.3 5.9 %collective-permute-start.16 = (bf16[16,8192]{1,0:T(8,128)(2,1)S(1)}, bf16[16,8192]{1,0:T(8,128)(2,1)S(1)}, u32[]{:S(2)}, u32[]{:S(2)}) collective-permute-start(bf16[16,8192]{1,0:T(8,128)(2,1)S(1)} %collective-permute-done.12.refs_7_), channel_id=1, source_target_pairs={{0,1},{1,0},{2,3},{3,2},{4,5},{5,4},{6,7},{7,6},{8,9},{9,8},{10,11... | collective-permute-start | bytes 786440 | tf_op jit(solution)/shard_map/ppermute | solution.py:296
  77.2 8.9 %collective-permute-start.17 = (bf16[768,128]{1,0:T(8,128)(2,1)S(1)}, bf16[768,128]{1,0:T(8,128)(2,1)S(1)}, u32[]{:S(2)}, u32[]{:S(2)}) collective-permute-start(bf16[768,128]{1,0:T(8,128)(2,1)S(1)} %get-tuple-element.28), channel_id=1, source_target_pairs={{0,16},{16,0},{1,17},{17,1},{2,18},{18,2},{3,19},{19,3},{4,20},{20... | collective-permute-start | bytes 589832 | tf_op jit(solution)/shard_map/ppermute | solution.py:394
